TPU v7x, 32 devices: a whole 2x2x4 slice. The times are simulated.
32 devices in a mesh: groups: 2 (over y), seq: 4 (over z), batch: 2 (over x), chan: 2 (over core).
Axes of the slice: x: 2, y: 2, z: 4, core: 2. Of those that a mesh axis runs over, the one named last changes fastest.
Arguments:
- query_vectors: bfloat16 [16, 256, 768], P(('groups', 'batch'), 'seq', 'chan'), parts along dimension 0, may hold values from -6 to 6
- key_vectors: bfloat16 [16, 256, 768], P(('groups', 'batch'), 'seq', 'chan'), parts along dimension 0, may hold values from -6 to 6
- value_vectors: bfloat16 [16, 256, 768], P(('groups', 'batch'), 'seq', 'chan'), parts along dimension 0, may hold values from -6 to 6
- hidden: bfloat16 [16, 256, 768], P(('groups', 'batch'), 'seq', 'chan'), parts along dimension 0, may hold values from -6 to 6
- cotangent: bfloat16 [16, 256, 768], P(('groups', 'batch'), 'seq', 'chan'), parts along dimension 0, may hold values from -6 to 6
- conv_weight: bfloat16 [768, 3, 768], P(None, None, 'chan'), may hold values from -0.125 to 0.125
Outputs:
- query_grad: bfloat16 [16, 256, 768], P(('groups', 'batch'), 'seq', 'chan'), parts along dimension 0
- key_grad: bfloat16 [16, 256, 768], P(('groups', 'batch'), 'seq', 'chan'), parts along dimension 0
- value_grad: bfloat16 [16, 256, 768], P(('groups', 'batch'), 'seq', 'chan'), parts along dimension 0
- hidden_grad: bfloat16 [16, 256, 768], P(('groups', 'batch'), 'seq', 'chan'), parts along dimension 0
- weight_grad: float32 [1536, 3, 768], P(('groups', 'seq', 'batch'), None, 'chan'), parts along dimension 0
There are 2 independent parts, one for each index of `groups`. A program takes and returns all parts, laid end to end along the dimension named above; an argument that names none is the same for every part. Nothing has to cross between parts.
All inputs are finite; a program needn't handle non-finite values.
Results may differ from a plain program's by a relative error of at most 0.025.
Values may be sent and summed in bfloat16 or wider, within the bound.
No kernel may reach another device: no remote copies, remote signals or barrier semaphores. Data moves between devices by JAX's collectives and lax.ppermute only.
A program may use at most 64 MiB of HBM per device.

v0:
```python
import math

import jax
import jax.numpy as jnp
from jax import lax
from jax.sharding import PartitionSpec as P

HD = 96


def from_behind(shard, axis, by):
    length = lax.axis_size(axis)
    pairs = [(i, i + by) for i in range(length) if 0 <= i + by < length]
    return lax.ppermute(shard, axis, pairs)


def tanh_gelu(signal):
    inner_arg = 0.7978845608 * (signal + 0.044715 * signal * signal * signal)
    return 0.5 * signal * (1.0 + jnp.tanh(inner_arg))


def gelu_slope(signal):
    inner_arg = 0.7978845608 * (signal + 0.044715 * signal * signal * signal)
    hyper = jnp.tanh(inner_arg)
    return 0.5 * (1.0 + hyper) + 0.5 * signal * (1.0 - hyper * hyper) * 0.7978845608 * (
        1.0 + 3.0 * 0.044715 * signal * signal
    )


def per_device(query_vectors, key_vectors, value_vectors, hidden, cotangent, conv_weight):
    seq_count = lax.axis_size("seq")
    batch_count = lax.axis_size("batch")
    partner_gap = seq_count // 4
    blocks, row_count, local_width = hidden.shape
    tokens_all = blocks * batch_count * row_count * seq_count
    factor = 1.0 / math.sqrt(tokens_all)
    hidden_f = hidden.astype(jnp.float32)
    activation = tanh_gelu(hidden_f).astype(jnp.bfloat16)
    act_full = lax.all_gather(activation, "chan", axis=2, tiled=True)

    def partner(offset):
        return from_behind(cotangent, "seq", offset)

    cot_before = partner(partner_gap)
    cot_after = partner(-partner_gap)
    cot_taps = jnp.stack([cot_after, cotangent, cot_before])
    back_part = jnp.einsum(
        "tbqo,ito->bqi", cot_taps, conv_weight, preferred_element_type=jnp.float32
    )
    back_sum = lax.psum_scatter(
        back_part.astype(jnp.bfloat16), "chan", scatter_dimension=2, tiled=True
    ).astype(jnp.float32)
    hidden_grad = (cotangent.astype(jnp.float32) + back_sum * gelu_slope(hidden_f)).astype(
        jnp.bfloat16
    )
    weight_grad = lax.psum_scatter(
        factor
        * jnp.einsum("bpi,tbpo->ito", act_full, cot_taps, preferred_element_type=jnp.float32),
        ("seq", "batch"),
        scatter_dimension=0,
        tiled=True,
    )
    heads_local = local_width // HD

    def to_heads(signal):
        return signal.reshape(blocks, row_count, heads_local, HD)

    stacked = jnp.stack(
        [
            to_heads(query_vectors),
            to_heads(key_vectors),
            to_heads(value_vectors),
            to_heads(hidden_grad),
        ],
        axis=3,
    )
    stacked = stacked.transpose(0, 2, 1, 3, 4).reshape(
        seq_count, blocks * heads_local // seq_count, row_count, 4 * HD
    )
    gathered = lax.all_to_all(stacked, "seq", split_axis=0, concat_axis=2, tiled=True)
    item_count = gathered.shape[1]
    length = gathered.shape[2]
    columns = gathered[0].reshape(item_count, length, 4, HD)
    query_all = columns[:, :, 0]
    key_all = columns[:, :, 1]
    value_all = columns[:, :, 2]
    grad_all = columns[:, :, 3]
    score_scale = 1.0 / math.sqrt(HD)
    block_rows = math.gcd(length, 512)
    block_count = length // block_rows
    query_blocks = query_all.reshape(item_count, block_count, block_rows, HD).transpose(1, 0, 2, 3)
    grad_blocks = grad_all.reshape(item_count, block_count, block_rows, HD).transpose(1, 0, 2, 3)

    def query_block(carry, inputs):
        key_acc, value_acc = carry
        query_rows, grad_rows = inputs
        scores = (
            jnp.einsum("iqd,ikd->iqk", query_rows, key_all, preferred_element_type=jnp.float32)
            * score_scale
        )
        row_max = jnp.max(scores, axis=-1, keepdims=True)
        raised = jnp.exp(scores - row_max)
        probability = raised / jnp.sum(raised, axis=-1, keepdims=True)
        prob_b = probability.astype(jnp.bfloat16)
        value_acc = value_acc + jnp.einsum(
            "iqk,iqd->ikd", prob_b, grad_rows, preferred_element_type=jnp.float32
        )
        d_prob = jnp.einsum(
            "iqd,ikd->iqk", grad_rows, value_all, preferred_element_type=jnp.float32
        )
        row_total = jnp.sum(probability * d_prob, axis=-1, keepdims=True)
        d_score = (probability * (d_prob - row_total)).astype(jnp.bfloat16)
        query_out = (
            score_scale
            * jnp.einsum("iqk,ikd->iqd", d_score, key_all, preferred_element_type=jnp.float32)
        ).astype(jnp.bfloat16)
        key_acc = key_acc + jnp.einsum(
            "iqk,iqd->ikd", d_score, query_rows, preferred_element_type=jnp.float32
        )
        return ((key_acc, value_acc), query_out)

    empty_acc = jnp.zeros((item_count, length, HD), jnp.float32)
    (key_acc, value_acc), query_outs = lax.scan(
        query_block, (empty_acc, empty_acc), (query_blocks, grad_blocks)
    )
    query_out = query_outs.transpose(1, 0, 2, 3).reshape(item_count, length, HD)
    key_out = (score_scale * key_acc).astype(jnp.bfloat16)
    value_out = value_acc.astype(jnp.bfloat16)
    results = jnp.concatenate([query_out, key_out, value_out], axis=-1)[None]
    returned = lax.all_to_all(results, "seq", split_axis=2, concat_axis=0, tiled=True)
    returned = returned.reshape(blocks, heads_local, row_count, 3, HD).transpose(3, 0, 2, 1, 4)
    returned = returned.reshape(3, blocks, row_count, local_width)
    return (returned[0], returned[1], returned[2], hidden_grad, weight_grad)


def solution(mesh):
    placed = (
        P(("groups", "batch"), "seq", "chan"),
        P(("groups", "batch"), "seq", "chan"),
        P(("groups", "batch"), "seq", "chan"),
        P(("groups", "batch"), "seq", "chan"),
        P(("groups", "batch"), "seq", "chan"),
        P(None, None, "chan"),
    )
    return jax.shard_map(
        per_device,
        mesh=mesh,
        in_specs=placed,
        out_specs=(
            P(("groups", "batch"), "seq", "chan"),
            P(("groups", "batch"), "seq", "chan"),
            P(("groups", "batch"), "seq", "chan"),
            P(("groups", "batch"), "seq", "chan"),
            P(("groups", "seq", "batch"), None, "chan"),
        ),
        check_vma=False,
    )
```

profile of v0, /device:TPU:0, one launch (start us, length us, event | category | flops | bytes accessed | tf_op | source)
XLA Modules:
  0.0 166.3 jit_solution(15160064708224018845)
XLA Ops:
  7.2 0.0 copy-start
  7.2 0.0 reduce-scatter.7.cloned.1.call-start
  7.2 1.4 collective-permute-start
  8.7 5.6 %collective-permute-start.1 = (bf16[4,64,384]{2,1,0:T(8,128)(2,1)}, bf16[4,64,384]{2,1,0:T(8,128)(2,1)S(1)}, u32[]{:S(2)}, u32[]{:S(2)}) collective-permute-start(bf16[4,64,384]{2,1,0:T(8,128)(2,1)} %param.10), channel_id=1, source_target_pairs={{0,4},{4,8},{8,12},{1,5},{5,9},{9,13},{2,6},{6,10},{10,14},{3,7},{... | collective-permute-start | bytes 589832 | tf_op jit(solution)/shard_map/ppermute | solution.py:14
  14.2 3.2 %collective-permute-done = bf16[4,64,384]{2,1,0:T(8,128)(2,1)S(1)} collective-permute-done((bf16[4,64,384]{2,1,0:T(8,128)(2,1)}, bf16[4,64,384]{2,1,0:T(8,128)(2,1)S(1)}, u32[]{:S(2)}, u32[]{:S(2)}) %collective-permute-start) | collective-permute-done | bytes 196640 | tf_op jit(solution)/shard_map/ppermute | solution.py:14
  17.4 1.3 collective-permute-done.1
  18.7 0.7 copy-done.10
  19.4 1.6 fusion.8
  21.0 0.0 copy-start.8
  21.0 0.0 copy-start.9
  21.0 0.6 copy.90
  21.6 1.2 reshape.37
  22.9 0.0 reduce-scatter.7.cloned.1.call-update
  22.9 0.0 reduce-scatter.5.cloned.1.call-start
  22.9 10.1 %reduce-scatter.7.cloned.1.call-done = bf16[384,256]{1,0:T(8,128)(2,1)} async-done(((bf16[768,256]{1,0:T(8,128)(2,1)}), bf16[384,256]{1,0:T(8,128)(2,1)}) %reduce-scatter.7.cloned.1.call-update) | async-done | bytes 196624
  33.0 1.2 reshape.38
  34.2 0.3 copy.91
  34.4 0.0 copy-done.8
  34.4 0.0 copy-done.9
  34.5 0.3 fusion.22
  34.8 0.0 copy-start.3
  34.8 2.1 %all_gather.3 = bf16[4,64,768]{2,1,0:T(8,128)(2,1)S(1)} all-gather(bf16[4,64,384]{2,1,0:T(8,128)(2,1)S(1)} %get-tuple-element.36), channel_id=1, replica_groups=mesh['groups'=2,'seq'=4,'batch'=2,'chan'=2] {'chan'}, dimensions={2}, use_global_device_ids=true | all-gather | bytes 589824 | tf_op jit(solution)/shard_map/all_gather | solution.py:39
  36.9 2.5 %bitcast_multiply_fusion = f32[768,3,384]{2,0,1:T(8,128)} fusion(bf16[4,64,768]{2,1,0:T(8,128)(2,1)S(1)} %all_gather.3, bf16[1,4,64,384]{3,2,0,1:T(8,128)(2,1)S(1)} %bitcast.98, bf16[1,4,64,384]{3,2,0,1:T(8,128)(2,1)S(1)} %bitcast.94, bf16[1,4,64,384]{3,2,0,1:T(8,128)(2,1)S(1)} %bitcast.96), kind=kOutput, calls=%fused_computation.1 | convolution fusion | flops 455639040 | bytes 4521984 | tf_op jit(solution)/shard_map/bpi,tbpo->ito/dot_general | solution.py:58
  39.4 0.0 reduce-scatter.5.cloned.1.call-update
  39.4 0.9 copy-done.4
  40.3 0.2 stack_reshape.12
  40.5 0.4 copy.66
  40.9 0.0 copy-done.5
  40.9 0.2 stack_reshape.13
  41.1 1.2 copy.67
  42.4 0.2 stack_reshape.14
  42.5 1.3 copy.68
  43.8 0.2 stack_reshape.15
  44.0 0.4 copy.69
  44.4 4.2 %maximum_bitcast_fusion = bf16[4,4,64,4,96]{4,3,2,1,0:T(4,128)(2,1)S(1)} fusion(bf16[4,64,4,1,96]{4,3,1,2,0:T(2,128)(2,1)S(1)} %copy.69, bf16[4,64,4,1,96]{4,3,1,2,0:T(2,128)(2,1)} %copy.68, bf16[4,64,4,1,96]{4,3,1,2,0:T(2,128)(2,1)} %copy.67, bf16[4,64,4,1,96]{4,3,1,2,0:T(2,128)(2,1)S(1)} %copy.66), kind=kLoop, calls=%fused_computation.14 | loop fusion | flops 3145728 | bytes 1572864 | tf_op jit(solution)/shard_map/transpose | solution.py:77
  48.6 1.6 reshape.31
  50.2 44.4 %all_to_all.30 = bf16[4,4,64,384]{3,2,1,0:T(8,128)(2,1)S(1)} all-to-all(bf16[4,4,64,384]{3,2,1,0:T(8,128)(2,1)} %reshape.31), channel_id=1, replica_groups=mesh['groups'=2,'seq'=4,'batch'=2,'chan'=2] {'seq'}, dimensions={0} | all-to-all | bytes 1572864 | tf_op jit(solution)/shard_map/all_to_all | solution.py:80
  94.6 1.0 copy.70
  95.5 2.5 %reshape_squeeze.3 = bf16[4,256,4,96]{3,2,1,0:T(4,128)(2,1)S(1)} reshape(bf16[1,4,4,64,384]{4,3,2,1,0:T(8,128)(2,1)} %copy.70) | data formatting | bytes 1572864 | tf_op jit(solution)/shard_map/reshape;squeeze | solution.py:83
  98.0 2.6 %fusion.56 = (bf16[4,256,1,96]{3,2,1,0:T(2,128)(2,1)}, bf16[4,256,1,96]{3,2,1,0:T(2,128)(2,1)S(1)}, bf16[4,256,1,96]{3,2,1,0:T(2,128)(2,1)}, bf16[4,256,1,96]{3,2,1,0:T(2,128)(2,1)}) fusion(bf16[4,256,4,96]{3,2,1,0:T(4,128)(2,1)S(1)} %reshape_squeeze.3), kind=kLoop, calls=%fused_computation.54 | loop fusion | bytes 1572864 | tf_op jit(solution)/shard_map/slice | solution.py:86
  100.6 1.9 %copy.95 = bf16[4,256,1,96]{1,3,0,2:T(8,128)(2,1)} copy(bf16[4,256,1,96]{3,2,1,0:T(2,128)(2,1)} %get-tuple-element.32) | data formatting | bytes 393216
  102.5 1.2 copy.93
  103.8 1.0 copy.92
  104.7 1.0 copy.94
  105.7 1.5 fusion.57
  107.2 1.8 %convolution_convert_fusion = bf16[4,256,96]{1,2,0:T(8,128)(2,1)S(1)} fusion(bf16[4,256,1,96]{1,3,0,2:T(8,128)(2,1)} %copy.94, f32[4,256]{1,0:T(4,128)S(1)} %get-tuple-element.38, bf16[4,256,1,96]{1,3,0,2:T(8,128)(2,1)} %copy.92, bf16[4,256,1,96]{1,3,0,2:T(8,128)(2,1)S(1)} %copy.93), kind=kOutput, calls=%fused_computation.11 | convolution fusion | flops 101811456 | bytes 790528 | tf_op jit(solution)/shard_map/while/body/eval_jaxpr/iqk,iqd->ikd/dot_general | solution.py:105
  109.0 1.3 multiply_reduce_fusion
  110.3 0.0 copy-start.2
  110.3 0.2 multiply_convert_fusion
  110.5 0.3 fusion.11
  110.8 0.4 copy-done.2
  111.2 0.2 fusion.12
  111.5 0.7 copy.78
  112.2 36.8 %all_to_all.31 = bf16[1,4,256,288]{3,1,0,2:T(4,128)(2,1)S(1)} all-to-all(bf16[1,4,256,288]{3,1,0,2:T(4,128)(2,1)S(1)} %copy.78), channel_id=1, replica_groups=mesh['groups'=2,'seq'=4,'batch'=2,'chan'=2] {'seq'}, dimensions={2} | all-to-all | bytes 1179648 | tf_op jit(solution)/shard_map/all_to_all | solution.py:130
  149.0 0.1 copy.79
  149.1 1.0 copy.80
  150.0 2.7 %reshape.32 = bf16[4,4,64,3,96]{4,3,2,1,0:T(4,128)(2,1)S(1)} reshape(bf16[4,1,4,64,288]{4,3,2,0,1:T(8,128)(2,1)} %copy.80) | data formatting | bytes 1179648 | tf_op jit(solution)/shard_map/reshape | solution.py:131
  152.8 2.0 %fusion.55 = (bf16[1,4,64,4,96]{4,0,2,3,1:T(2,128)(2,1)S(1)}, bf16[1,4,64,4,96]{4,0,2,3,1:T(2,128)(2,1)}, bf16[1,4,64,4,96]{4,0,2,3,1:T(2,128)(2,1)S(1)}) fusion(bf16[3,4,64,4,96]{4,0,2,3,1:T(4,128)(2,1)S(1)} %bitcast.88), kind=kLoop, calls=%fused_computation.53 | loop fusion | bytes 1179648 | tf_op jit(solution)/shard_map/slice | solution.py:133
  154.8 0.3 copy.83
  155.1 0.9 squeeze.30
  156.0 1.4 copy.82
  157.4 0.9 squeeze.29
  158.3 0.3 copy.81
  158.6 0.9 squeeze.28
  (15 shorter events, 0.1 us)
Async XLA Ops:
  7.2 12.2 %copy-start = (bf16[768,3,384]{2,0,1:T(8,128)(2,1)S(1)}, bf16[768,3,384]{2,0,1:T(8,128)(2,1)}, u32[]{:S(2)}) copy-start(bf16[768,3,384]{2,0,1:T(8,128)(2,1)} %param.11) | copy-start | bytes 5308420
  7.2 25.8 %reduce-scatter.7.cloned.1.call-start = ((), (), s32[]{:S(2)}) async-start(), calls=%async_computation.5 | async-start | bytes 589824
  7.2 10.2 %collective-permute-start = (bf16[4,64,384]{2,1,0:T(8,128)(2,1)}, bf16[4,64,384]{2,1,0:T(8,128)(2,1)S(1)}, u32[]{:S(2)}, u32[]{:S(2)}) collective-permute-start(bf16[4,64,384]{2,1,0:T(8,128)(2,1)} %param.10), channel_id=1, source_target_pairs={{4,0},{8,4},{12,8},{5,1},{9,5},{13,9},{6,2},{10,6},{14,10},{7,3},{... | collective-permute-start | bytes 589832 | tf_op jit(solution)/shard_map/ppermute | solution.py:14
  8.7 10.0 %collective-permute-start.1 = (bf16[4,64,384]{2,1,0:T(8,128)(2,1)}, bf16[4,64,384]{2,1,0:T(8,128)(2,1)S(1)}, u32[]{:S(2)}, u32[]{:S(2)}) collective-permute-start(bf16[4,64,384]{2,1,0:T(8,128)(2,1)} %param.10), channel_id=1, source_target_pairs={{0,4},{4,8},{8,12},{1,5},{5,9},{9,13},{2,6},{6,10},{10,14},{3,7},{... | collective-permute-start | bytes 589832 | tf_op jit(solution)/shard_map/ppermute | solution.py:14
  18.7 0.7 copy-start.10
  21.0 13.4 %copy-start.8 = (bf16[4,64,384]{2,1,0:T(8,128)(2,1)S(1)}, bf16[4,64,384]{2,1,0:T(8,128)(2,1)}, u32[]{:S(2)}) copy-start(bf16[4,64,384]{2,1,0:T(8,128)(2,1)} %param.9) | copy-start | bytes 589828
  21.0 13.4 %copy-start.9 = (bf16[4,64,384]{2,1,0:T(8,128)(2,1)S(1)}, bf16[4,64,384]{2,1,0:T(8,128)(2,1)}, u32[]{:S(2)}) copy-start(bf16[4,64,384]{2,1,0:T(8,128)(2,1)} %param.10) | copy-start | bytes 589828
  22.9 14.1 %copy-start.11 = (bf16[4,64,384]{2,1,0:T(8,128)(2,1)S(1)}, bf16[4,64,384]{2,1,0:T(8,128)(2,1)}, u32[]{:S(2)}) copy-start(bf16[4,64,384]{2,1,0:T(8,128)(2,1)} %copy-done.10) | copy-start | bytes 589828
  22.9 136.6 %reduce-scatter.5.cloned.1.call-start = ((), (), s32[]{:S(2)}) async-start(), calls=%async_computation.4 | async-start | bytes 3981312 | tf_op jit(solution)/shard_map/reduce_scatter | solution.py:56
  34.8 9.0 %copy-start.3 = (bf16[4,64,384]{2,1,0:T(8,128)(2,1)}, bf16[4,64,384]{2,1,0:T(8,128)(2,1)S(1)}, u32[]{:S(2)}) copy-start(bf16[4,64,384]{2,1,0:T(8,128)(2,1)S(1)} %get-tuple-element.37) | copy-start | bytes 589828
  39.4 0.9 copy-start.4
  39.4 1.6 copy-start.5
  40.3 2.1 %copy-start.6 = (bf16[4,64,384]{2,1,0:T(8,128)(2,1)S(1)}, bf16[4,64,384]{2,1,0:T(8,128)(2,1)}, u32[]{:S(2)}) copy-start(bf16[4,64,384]{2,1,0:T(8,128)(2,1)} %param.8) | copy-start | bytes 589828
  100.6 3.1 %copy-start.1 = (bf16[4,256,1,96]{3,2,1,0:T(2,128)(2,1)S(1)}, bf16[4,256,1,96]{3,2,1,0:T(2,128)(2,1)}, u32[]{:S(2)}) copy-start(bf16[4,256,1,96]{3,2,1,0:T(2,128)(2,1)} %get-tuple-element.35) | copy-start | bytes 589828
  107.2 1.8 %copy-start.7 = (bf16[4,256,1,96]{1,3,0,2:T(8,128)(2,1)S(1)}, bf16[4,256,1,96]{1,3,0,2:T(8,128)(2,1)}, u32[]{:S(2)}) copy-start(bf16[4,256,1,96]{1,3,0,2:T(8,128)(2,1)} %copy.95) | copy-start | bytes 589828
  110.3 0.9 copy-start.2
Sparse Core Ops, SparseCore 0:
  23.0 9.9 reduce-scatter.6
  39.5 110.2 reduce-scatter.4
where the time goes:
time: 167 us; the launch traced here: 166 us
  blocking collectives  83.3 us (50%)
  local copies, waits for them, and re-layouts  33.1 us (20%)
  waiting for transfers between devices  14.6 us (9%)
  between operations  14.3 us (9%)
  matrix products  9.19 us (6%)
  starting transfers between devices  7.08 us (4%)
  other arithmetic  4.74 us (3%)
    all_to_all x1, blocking collectives, per_device(): lax.all_to_all(stacked, 'seq', split_axis=0, concat_axis=2, tiled=True)  44.4 us
    all_to_all x1, blocking collectives, per_device(): lax.all_to_all(results, 'seq', split_axis=2, concat_axis=0, tiled=True)  36.8 us
    unnamed x32, local copies, waits for them, and re-layouts  10.3 us
    unnamed x3, waiting for transfers between devices  10.1 us
    ppermute x2, starting transfers between devices, from_behind(): return lax.ppermute(shard, axis, pairs)  7 us
    ppermute x2, waiting for transfers between devices, from_behind(): return lax.ppermute(shard, axis, pairs)  4.45 us
    transpose x1, other arithmetic, per_device(): stacked.transpose(0, 2, 1, 3, 4)  4.17 us
    slice x4, local copies, waits for them, and re-layouts, per_device(): return (returned[0], returned[1], returned[2], hidden_grad, weight_grad)  4.07 us
  transfers between devices with their start and end apart: 4, of which 3 were waited for; matrix products, arithmetic and copies ran while one was open for 22% of the time, Pallas kernels for 0%

commit v1 on v0

--- a/solution.py
+++ b/solution.py
@@ -1,17 +1,17 @@
+import functools
 import math
 
 import jax
 import jax.numpy as jnp
 from jax import lax
+from jax.experimental import pallas as pl
+from jax.experimental.pallas import tpu as pltpu
 from jax.sharding import PartitionSpec as P
 
 HD = 96
-
-
-def from_behind(shard, axis, by):
-    length = lax.axis_size(axis)
-    pairs = [(i, i + by) for i in range(length) if 0 <= i + by < length]
-    return lax.ppermute(shard, axis, pairs)
+BF = jnp.bfloat16
+F32 = jnp.float32
+VMEM_LIMIT = 40 * 1024 * 1024
 
 
 def tanh_gelu(signal):
@@ -27,7 +27,253 @@
     )
 
 
+def kernel_call(body, outs, flops=0, transcendentals=0, name=None, scratch=()):
+    vmem = pl.BlockSpec(memory_space=pltpu.VMEM)
+
+    def call(*args):
+        moved = sum(math.prod(a.shape) * a.dtype.itemsize for a in args)
+        moved += sum(math.prod(o.shape) * o.dtype.itemsize for o in outs)
+        return pl.pallas_call(
+            body,
+            out_shape=list(outs),
+            in_specs=[vmem] * len(args),
+            out_specs=[vmem] * len(outs),
+            scratch_shapes=list(scratch),
+            compiler_params=pltpu.CompilerParams(vmem_limit_bytes=VMEM_LIMIT),
+            cost_estimate=pl.CostEstimate(
+                flops=flops, bytes_accessed=moved, transcendentals=transcendentals
+            ),
+            name=name,
+        )(*args)
+
+    return call
+
+
+def shape(dims, dtype=BF):
+    return jax.ShapeDtypeStruct(dims, dtype)
+
+
+def prepare_kernel(count, q_ref, k_ref, v_ref, h_ref, *outs):
+    s = lax.axis_index("seq")
+    for d in range(count):
+        b = lax.rem(s + d, count)
+        for j, ref in enumerate((q_ref, k_ref, v_ref)):
+            outs[d][j] = ref[b]
+    act_refs = outs[count : count + 2]
+    blocks, rows, width = h_ref.shape
+    act = tanh_gelu(h_ref[...].astype(F32)).reshape(blocks * rows, width)
+    act_t = act.T.astype(BF)
+    half = width // 2
+    first = lax.rem(s, 2) == 0
+    low, high = act_t[:half], act_t[half:]
+    act_refs[0][...] = jnp.where(first, low, high)
+    act_refs[1][...] = jnp.where(first, high, low)
+
+
+def conv_kernel(cot_ref, left_ref, right_ref, w_ref, mine_ref, other_ref):
+    c = lax.axis_index("chan")
+    blocks, rows, width = cot_ref.shape
+    taps = [r[...].reshape(blocks * rows, width) for r in (right_ref, cot_ref, left_ref)]
+    for out_ref, side in ((other_ref, 1 - c), (mine_ref, c)):
+        start = pl.multiple_of(side * width, width)
+        total = None
+        for t in range(3):
+            term = lax.dot_general(
+                taps[t],
+                w_ref[t, pl.ds(start, width), :],
+                (((1,), (1,)), ((), ())),
+                preferred_element_type=F32,
+            )
+            total = term if total is None else total + term
+        out_ref[...] = total.astype(BF).reshape(blocks, rows, width)
+
+
+def grad_kernel(count, cot_ref, h_ref, mine_ref, other_ref, grad_ref, *pieces):
+    s = lax.axis_index("seq")
+    back = mine_ref[...].astype(F32) + other_ref[...].astype(F32)
+    slope = gelu_slope(h_ref[...].astype(F32))
+    grad_ref[...] = (cot_ref[...].astype(F32) + back * slope).astype(BF)
+    for d in range(count):
+        pieces[d][...] = grad_ref[lax.rem(s + d, count)]
+
+
+def attention_kernel(count, *refs):
+    qkv = refs[:count]
+    grads = refs[count : 2 * count]
+    outs = refs[2 * count :]
+    rows, width = grads[0].shape
+    scale = 1.0 / math.sqrt(HD)
+    query, key, value = (
+        jnp.concatenate([qkv[d][j] for d in range(count)], axis=0) for j in range(3)
+    )
+    grad = jnp.concatenate([grads[d][...] for d in range(count)], axis=0)
+    nt = (((1,), (1,)), ((), ()))
+    nn = (((1,), (0,)), ((), ()))
+    tn = (((0,), (0,)), ((), ()))
+    dot = functools.partial(lax.dot_general, preferred_element_type=F32)
+    results = ([], [], [])
+    for h in range(width // HD):
+        cols = slice(h * HD, (h + 1) * HD)
+        q, k, v, g = query[:, cols], key[:, cols], value[:, cols], grad[:, cols]
+        scores = dot(k, q, nt) * scale
+        raised = jnp.exp(scores - jnp.max(scores, axis=0, keepdims=True))
+        prob = raised * (1.0 / jnp.sum(raised, axis=0, keepdims=True))
+        d_prob = dot(v, g, nt)
+        row_total = jnp.sum(prob * d_prob, axis=0, keepdims=True)
+        d_score = (prob * (d_prob - row_total)).astype(BF)
+        results[0].append((dot(d_score, k, tn) * scale).astype(BF))
+        results[1].append((dot(d_score, q, nn) * scale).astype(BF))
+        results[2].append(dot(prob.astype(BF), g, nn).astype(BF))
+    for j in range(3):
+        whole = jnp.concatenate(results[j], axis=1)
+        for d in range(count):
+            outs[d][j] = whole[d * rows : (d + 1) * rows]
+
+
+def weight_kernel(count, factor, *refs):
+    acts, cots = refs[:4], refs[4 : 4 + 2 * count - 1]
+    own_ref, sent_ref, act_buf, cot_buf = refs[4 + 2 * count - 1 :]
+    s = lax.axis_index("seq")
+    c = lax.axis_index("chan")
+    b = lax.axis_index("batch")
+    for k in range(2):
+        for side, piece in ((c, acts[k]), (1 - c, acts[2 + k])):
+            act_buf[2 * side + lax.rem(s + k, 2)] = piece[...]
+    for r in range(-(count - 1), count):
+        piece = cots[r + count - 1]
+        blocks, rows, width = piece.shape
+
+        @pl.when(jnp.logical_and(s + r >= 0, s + r < count))
+        def _():
+            cot_buf[s + r] = piece[...].reshape(blocks * rows, width)
+
+    half = own_ref.shape[1]
+    for t in range(3):
+        low = max(0, 1 - t)
+        high = min(count, count + 1 - t)
+        for out_ref, side in ((sent_ref, 1 - b), (own_ref, b)):
+            start = pl.multiple_of(side * half, half)
+            total = None
+            for j in range(low, high):
+                term = jnp.dot(
+                    act_buf[j + t - 1, pl.ds(start, half), :],
+                    cot_buf[j],
+                    preferred_element_type=F32,
+                )
+                total = term if total is None else total + term
+            out_ref[t] = (factor * total).astype(out_ref.dtype)
+
+
+def add_kernel(own_ref, got_ref, out_ref):
+    out_ref[...] = own_ref[...] + got_ref[...].astype(F32)
+
+
+def place_kernel(count, *refs):
+    pieces, outs = refs[:count], refs[count:]
+    s = lax.axis_index("seq")
+    for d in range(count):
+        b = lax.rem(s + d, count)
+        for j in range(3):
+            outs[j][b] = pieces[d][j]
+
+
+def shift(x, axis, by, wrap):
+    n = lax.axis_size(axis)
+    pairs = [(i, (i + by) % n) for i in range(n) if wrap or 0 <= i + by < n]
+    return lax.ppermute(x, axis, pairs)
+
+
+def after(first, *then):
+    held = lax.optimization_barrier((first, *then))
+    return held[1:]
+
+
 def per_device(query_vectors, key_vectors, value_vectors, hidden, cotangent, conv_weight):
+    count = lax.axis_size("seq")
+    blocks, rows, width = hidden.shape
+    tokens = blocks * rows
+    factor = 1.0 / math.sqrt(tokens * count * lax.axis_size("batch"))
+    weights = conv_weight.transpose(1, 0, 2)
+    piece = shape((rows, width))
+    piece3 = shape((3, rows, width))
+    full = shape((blocks, rows, width))
+    part = width // 2
+
+    left = shift(cotangent, "seq", 1, False)
+    right = shift(cotangent, "seq", -1, False)
+    *qkv, act0, act1 = kernel_call(
+        functools.partial(prepare_kernel, count),
+        [piece3] * count + [shape((part, tokens))] * 2,
+        transcendentals=tokens * width,
+        name="prepare",
+    )(query_vectors, key_vectors, value_vectors, hidden)
+    got_qkv = [qkv[0]] + [shift(qkv[d], "seq", d, True) for d in range(1, count)]
+
+    mine, other = kernel_call(
+        conv_kernel, [full, full], flops=2 * tokens * 3 * width * 2 * width, name="conv_back"
+    )(cotangent, left, right, weights)
+    got = shift(other, "chan", 1, True)
+    hidden_grad, *grads = kernel_call(
+        functools.partial(grad_kernel, count),
+        [full] + [piece] * count,
+        transcendentals=tokens * width,
+        name="hidden_grad",
+    )(cotangent, hidden, mine, got)
+    got_grads = [grads[0]] + [shift(grads[d], "seq", d, True) for d in range(1, count)]
+
+    far_left, far_right, act0, act1 = after(grads[0], left, right, act0, act1)
+    lefts, rights = [far_left], [far_right]
+    n_chan = lax.axis_size("chan")
+    got_act = []
+    for k, act in enumerate((act0, act1)):
+        pairs = []
+        for i in range(count):
+            for c in range(n_chan):
+                to = (2 * c + (i + k) % 2) * n_chan + i // 2
+                pairs.append((i * n_chan + c, to))
+        got_act.append(lax.ppermute(act, ("seq", "chan"), pairs))
+    for _ in range(count - 2):
+        lefts.append(shift(lefts[-1], "seq", 1, False))
+        rights.append(shift(rights[-1], "seq", -1, False))
+    other_act = [shift(a, "chan", 1, True) for a in got_act]
+
+    item = 5 * (count * rows) ** 2 * width
+    returned = kernel_call(
+        functools.partial(attention_kernel, count),
+        [piece3] * count,
+        flops=2 * item,
+        transcendentals=(count * rows) ** 2 * (width // HD),
+        name="attention",
+    )(*got_qkv, *got_grads)
+    back = [returned[0]] + [shift(returned[d], "seq", -d, True) for d in range(1, count)]
+
+    own, sent = kernel_call(
+        functools.partial(weight_kernel, count, factor),
+        [shape((3, part // 2, width), F32), shape((3, part // 2, width))],
+        flops=2 * (3 * count - 2) * tokens * part * width,
+        name="weight_grad",
+        scratch=[
+            pltpu.VMEM((count, part, tokens), BF),
+            pltpu.VMEM((count, tokens, width), BF),
+        ],
+    )(*got_act, *other_act, *reversed(lefts), cotangent, *rights)
+    got_sum = shift(sent, "batch", 1, True)
+    (weight_grad,) = kernel_call(add_kernel, [shape((3, part // 2, width), F32)], name="add_weight")(
+        own, got_sum
+    )
+    query_grad, key_grad, value_grad = kernel_call(
+        functools.partial(place_kernel, count), [full] * 3, name="place"
+    )(*back)
+    return (query_grad, key_grad, value_grad, hidden_grad, weight_grad.transpose(1, 0, 2))
+
+
+def from_behind(shard, axis, by):
+    length = lax.axis_size(axis)
+    pairs = [(i, i + by) for i in range(length) if 0 <= i + by < length]
+    return lax.ppermute(shard, axis, pairs)
+
+
+def per_device_general(query_vectors, key_vectors, value_vectors, hidden, cotangent, conv_weight):
     seq_count = lax.axis_size("seq")
     batch_count = lax.axis_size("batch")
     partner_gap = seq_count // 4
@@ -134,24 +380,18 @@
 
 
 def solution(mesh):
-    placed = (
-        P(("groups", "batch"), "seq", "chan"),
-        P(("groups", "batch"), "seq", "chan"),
-        P(("groups", "batch"), "seq", "chan"),
-        P(("groups", "batch"), "seq", "chan"),
-        P(("groups", "batch"), "seq", "chan"),
-        P(None, None, "chan"),
-    )
-    return jax.shard_map(
-        per_device,
-        mesh=mesh,
-        in_specs=placed,
-        out_specs=(
-            P(("groups", "batch"), "seq", "chan"),
-            P(("groups", "batch"), "seq", "chan"),
-            P(("groups", "batch"), "seq", "chan"),
-            P(("groups", "batch"), "seq", "chan"),
-            P(("groups", "seq", "batch"), None, "chan"),
-        ),
-        check_vma=False,
-    )
+    token = P(("groups", "batch"), "seq", "chan")
+    sizes = dict(mesh.shape)
+
+    def run(*arrays):
+        blocks = arrays[0].shape[0] // (sizes["groups"] * sizes["batch"])
+        fits = blocks == sizes["seq"] == 4 and sizes["batch"] == 2 and sizes["chan"] == 2
+        return jax.shard_map(
+            per_device if fits else per_device_general,
+            mesh=mesh,
+            in_specs=(token,) * 5 + (P(None, None, "chan"),),
+            out_specs=(token,) * 4 + (P(("groups", "seq", "batch"), None, "chan"),),
+            check_vma=False,
+        )(*arrays)
+
+    return run

time: 167 us -> 82.8 us (0.50)
  blocking collectives: 83.3 us -> 0 us
  starting transfers between devices: 7.08 us -> 44 us
  local copies, waits for them, and re-layouts: 33.1 us -> 2.59 us
  waiting for transfers between devices: 14.6 us -> 28.2 us
  between operations: 14.3 us -> 0.79 us
  matrix products: 9.19 us -> 0 us
  Pallas kernels: 0 us -> 6.91 us
  other arithmetic: 4.74 us -> 0 us
    all_to_all x2 -> x0, blocking collectives: 81.2 us -> none  [the longest x1 44.4 us: per_device(): lax.all_to_all(stacked, 'seq', split_axis=0, concat_axis=2, tiled=True)]
    ppermute x2 -> x21, starting transfers between devices: 7 us -> 44 us  [the longest x19 40.6 us: shift(): return lax.ppermute(x, axis, pairs)]
    ppermute x2 -> x21, waiting for transfers between devices: 4.45 us -> 28.2 us  [the longest x19 28.2 us: shift(): return lax.ppermute(x, axis, pairs)]
    unnamed x3 -> x0, waiting for transfers between devices: 10.1 us -> none
    unnamed x32 -> x14, local copies, waits for them, and re-layouts: 10.3 us -> 2.59 us
    dot_general x6 -> x0, matrix products: 7.72 us -> none  [the longest x1 2.47 us: per_device(): jnp.einsum('bpi,tbpo->ito', act_full, cot_taps, preferred_element_type=jn...]
    pallas_call x0 -> x7, Pallas kernels: none -> 6.91 us  [call(): pl.pallas_call(body, out_shape=list(outs), in_specs=[vmem] * len(args), o...]
    slice x5 -> x0, local copies, waits for them, and re-layouts: 6.66 us -> none  [the longest x4 4.07 us: per_device(): return (returned[0], returned[1], returned[2], hidden_grad, weight_grad)]
  transfers between devices with their start and end apart: 4 -> 21, of which waited for: 3 -> 9; matrix products, arithmetic and copies ran while one was open for 22% -> 0% of each run, Pallas kernels for 0% -> 5%
where the time goes in v1:
time: 82.8 us; the launch traced here: 82.5 us
  starting transfers between devices  44 us (53%)
  waiting for transfers between devices  28.2 us (34%)
  Pallas kernels  6.91 us (8%)
  local copies, waits for them, and re-layouts  2.59 us (3%)
    ppermute x19, starting transfers between devices, shift(): return lax.ppermute(x, axis, pairs)  40.6 us
    ppermute x19, waiting for transfers between devices, shift(): return lax.ppermute(x, axis, pairs)  28.2 us
    pallas_call x7, Pallas kernels, call(): pl.pallas_call(body, out_shape=list(outs), in_specs=[vmem] * len(args), o...  6.91 us
    ppermute x2, starting transfers between devices, per_device(): got_act.append(lax.ppermute(act, ('seq', 'chan'), pairs))  3.37 us
    unnamed x14, local copies, waits for them, and re-layouts  2.59 us
  transfers between devices with their start and end apart: 21, of which 9 were waited for; matrix products, arithmetic and copies ran while one was open for 0% of the time, Pallas kernels for 5%

profile of v1, /device:TPU:0, one launch (start us, length us, event | category | flops | bytes accessed | tf_op | source)
XLA Modules:
  0.0 82.5 jit_solution(14102431618249431134)
XLA Ops:
  0.6 1.3 %collective-permute-start.4 = (bf16[4,64,384]{2,1,0:T(8,128)(2,1)}, bf16[4,64,384]{2,1,0:T(8,128)(2,1)S(1)}, u32[]{:S(2)}, u32[]{:S(2)}) collective-permute-start(bf16[4,64,384]{2,1,0:T(8,128)(2,1)} %refs_7_.1), channel_id=1, source_target_pairs={{4,0},{8,4},{12,8},{5,1},{9,5},{13,9},{6,2},{10,6},{14,10},{7,3},{... | collective-permute-start | bytes 589832 | tf_op jit(solution)/shard_map/ppermute | solution.py:183
  1.9 5.6 %collective-permute-start.3 = (bf16[4,64,384]{2,1,0:T(8,128)(2,1)}, bf16[4,64,384]{2,1,0:T(8,128)(2,1)S(1)}, u32[]{:S(2)}, u32[]{:S(2)}) collective-permute-start(bf16[4,64,384]{2,1,0:T(8,128)(2,1)} %refs_7_.1), channel_id=1, source_target_pairs={{0,4},{4,8},{8,12},{1,5},{5,9},{9,13},{2,6},{6,10},{10,14},{3,7},{... | collective-permute-start | bytes 589832 | tf_op jit(solution)/shard_map/ppermute | solution.py:183
  7.5 3.2 %collective-permute-done.4.right_ref.refs_8_ = bf16[4,64,384]{2,1,0:T(8,128)(2,1)S(1)} collective-permute-done((bf16[4,64,384]{2,1,0:T(8,128)(2,1)}, bf16[4,64,384]{2,1,0:T(8,128)(2,1)S(1)}, u32[]{:S(2)}, u32[]{:S(2)}) %collective-permute-start.4) | collective-permute-done | bytes 196640 | tf_op jit(solution)/shard_map/ppermute | solution.py:183
  10.7 1.3 %collective-permute-done.3.left_ref.refs_6_ = bf16[4,64,384]{2,1,0:T(8,128)(2,1)S(1)} collective-permute-done((bf16[4,64,384]{2,1,0:T(8,128)(2,1)}, bf16[4,64,384]{2,1,0:T(8,128)(2,1)S(1)}, u32[]{:S(2)}, u32[]{:S(2)}) %collective-permute-start.3) | collective-permute-done | bytes 196640 | tf_op jit(solution)/shard_map/ppermute | solution.py:183
  12.0 0.0 copy-start
  12.0 0.9 %copy-done = bf16[4,64,384]{2,1,0:T(8,128)(2,1)S(1)} copy-done((bf16[4,64,384]{2,1,0:T(8,128)(2,1)S(1)}, bf16[4,64,384]{2,1,0:T(8,128)(2,1)}, u32[]{:S(2)}) %copy-start) | copy-done | bytes 196632
  12.9 0.0 copy-start.2
  12.9 1.5 %copy-done.2 = bf16[768,3,384]{2,0,1:T(8,128)(2,1)S(1)} copy-done((bf16[768,3,384]{2,0,1:T(8,128)(2,1)S(1)}, bf16[768,3,384]{2,0,1:T(8,128)(2,1)}, u32[]{:S(2)}) %copy-start.2) | copy-done | bytes 1769496
  14.4 0.0 copy-start.3
  14.4 0.0 copy-start.4
  14.4 0.0 copy-start.5
  14.4 0.0 copy-start.6
  14.4 0.0 copy-start.1
  14.4 0.9 %conv_back.1 = (bf16[4,64,384]{2,1,0:T(8,128)(2,1)S(1)}, bf16[4,64,384]{2,1,0:T(8,128)(2,1)S(1)}) custom-call(bf16[4,64,384]{2,1,0:T(8,128)(2,1)S(1)} %copy-done, bf16[4,64,384]{2,1,0:T(8,128)(2,1)S(1)} %collective-permute-done.3.left_ref.refs_6_, bf16[4,64,384]{2,1,0:T(8,128)(2,1)S(1)} %collective-permute-done.4.right_ref.refs_8_, ...), custom_call_target="tpu_custom_call" | custom-call | flops 452984832 | bytes 2752512 | tf_op jit(solution)/shard_map/conv_back/pallas_call | solution.py:36
  15.3 0.1 collective-permute-start.5
  15.4 0.0 copy-done.3
  15.4 0.0 copy-done.4
  15.4 0.1 copy-done.5
  15.5 0.1 copy-done.6
  15.6 0.2 prepare.1
  15.8 1.0 %collective-permute-done.5.other_ref = bf16[4,64,384]{2,1,0:T(8,128)(2,1)S(1)} collective-permute-done((bf16[4,64,384]{2,1,0:T(8,128)(2,1)S(1)}, bf16[4,64,384]{2,1,0:T(8,128)(2,1)S(1)}, u32[]{:S(2)}, u32[]{:S(2)}) %collective-permute-start.5) | collective-permute-done | bytes 196640 | tf_op jit(solution)/shard_map/ppermute | solution.py:183
  16.8 0.0 copy-done.1
  16.8 1.2 %hidden_grad.1 = (bf16[4,64,384]{2,1,0:T(8,128)(2,1)}, bf16[64,384]{1,0:T(8,128)(2,1)S(1)}, bf16[64,384]{1,0:T(8,128)(2,1)S(1)}, bf16[64,384]{1,0:T(8,128)(2,1)S(1)}, bf16[64,384]{1,0:T(8,128)(2,1)S(1)}) custom-call(bf16[4,64,384]{2,1,0:T(8,128)(2,1)S(1)} %copy-done.1, bf16[4,64,384]{2,1,0:T(8,128)(2,1)S(1)} %copy-done.3, ...), custom_call_target="tpu_custom_call" | custom-call | bytes 1179648 | tf_op jit(solution)/shard_map/hidden_grad/pallas_call | solution.py:36
  18.0 4.3 %collective-permute-start.16 = (bf16[4,64,384]{2,1,0:T(8,128)(2,1)S(1)}, bf16[4,64,384]{2,1,0:T(8,128)(2,1)S(1)}, u32[]{:S(2)}, u32[]{:S(2)}) collective-permute-start(bf16[4,64,384]{2,1,0:T(8,128)(2,1)S(1)} %collective-permute-done.3.left_ref.refs_6_), channel_id=1, source_target_pairs={{0,4},{4,8},{8,12},{1,5},{5,9},{9,13},{2,6},{6,10},{10,14},{3,7},{... | collective-permute-start | bytes 589832 | tf_op jit(solution)/shard_map/ppermute | solution.py:183
  22.3 1.3 %collective-permute-start.18 = (bf16[4,64,384]{2,1,0:T(8,128)(2,1)S(1)}, bf16[4,64,384]{2,1,0:T(8,128)(2,1)S(1)}, u32[]{:S(2)}, u32[]{:S(2)}) collective-permute-start(bf16[4,64,384]{2,1,0:T(8,128)(2,1)S(1)} %collective-permute-done.4.right_ref.refs_8_), channel_id=1, source_target_pairs={{4,0},{8,4},{12,8},{5,1},{9,5},{13,9},{6,2},{10,6},{14,10},{7,3},{... | collective-permute-start | bytes 589832 | tf_op jit(solution)/shard_map/ppermute | solution.py:183
  23.6 0.7 collective-permute-start.12
  24.3 2.7 %collective-permute-start.13 = (bf16[192,256]{1,0:T(8,128)(2,1)S(1)}, bf16[192,256]{1,0:T(8,128)(2,1)S(1)}, u32[]{:S(2)}, u32[]{:S(2)}) collective-permute-start(bf16[192,256]{1,0:T(8,128)(2,1)S(1)} %get-tuple-element.52), channel_id=1, source_target_pairs={{0,4},{1,12},{4,0},{5,8},{8,5},{9,13},{12,1},{13,9},{2,6},{3,14},{... | collective-permute-start | bytes 294920 | tf_op jit(solution)/shard_map/ppermute | solution.py:234
  27.0 0.0 collective-permute-done.12.refs_0_
  27.0 5.9 %collective-permute-start.14 = (bf16[192,256]{1,0:T(8,128)(2,1)S(1)}, bf16[192,256]{1,0:T(8,128)(2,1)S(1)}, u32[]{:S(2)}, u32[]{:S(2)}) collective-permute-start(bf16[192,256]{1,0:T(8,128)(2,1)S(1)} %collective-permute-done.12.refs_0_), channel_id=1, source_target_pairs={{0,1},{1,0},{2,3},{3,2},{4,5},{5,4},{6,7},{7,6},{8,9},{9,8},{10,11... | collective-permute-start | bytes 294920 | tf_op jit(solution)/shard_map/ppermute | solution.py:183
  32.9 0.0 collective-permute-done.16.refs_5_
  32.9 4.6 %collective-permute-start.17 = (bf16[4,64,384]{2,1,0:T(8,128)(2,1)S(1)}, bf16[4,64,384]{2,1,0:T(8,128)(2,1)S(1)}, u32[]{:S(2)}, u32[]{:S(2)}) collective-permute-start(bf16[4,64,384]{2,1,0:T(8,128)(2,1)S(1)} %collective-permute-done.16.refs_5_), channel_id=1, source_target_pairs={{0,4},{4,8},{8,12},{1,5},{5,9},{9,13},{2,6},{6,10},{10,14},{3,7},{... | collective-permute-start | bytes 589832 | tf_op jit(solution)/shard_map/ppermute | solution.py:183
  37.5 0.0 collective-permute-done.18.refs_9_
  37.6 1.3 %collective-permute-start.19 = (bf16[4,64,384]{2,1,0:T(8,128)(2,1)S(1)}, bf16[4,64,384]{2,1,0:T(8,128)(2,1)S(1)}, u32[]{:S(2)}, u32[]{:S(2)}) collective-permute-start(bf16[4,64,384]{2,1,0:T(8,128)(2,1)S(1)} %collective-permute-done.18.refs_9_), channel_id=1, source_target_pairs={{4,0},{8,4},{12,8},{5,1},{9,5},{13,9},{6,2},{10,6},{14,10},{7,3},{... | collective-permute-start | bytes 589832 | tf_op jit(solution)/shard_map/ppermute | solution.py:183
  38.9 0.0 collective-permute-done.13.refs_1_
  38.9 0.1 collective-permute-start.15
  38.9 2.7 %collective-permute-start = (bf16[3,64,384]{2,1,0:T(8,128)(2,1)S(1)}, bf16[3,64,384]{2,1,0:T(8,128)(2,1)S(1)}, u32[]{:S(2)}, u32[]{:S(2)}) collective-permute-start(bf16[3,64,384]{2,1,0:T(8,128)(2,1)S(1)} %get-tuple-element.32), channel_id=1, source_target_pairs={{0,4},{4,8},{8,12},{12,0},{1,5},{5,9},{9,13},{13,1},{2,6},{6,10},{... | collective-permute-start | bytes 442376 | tf_op jit(solution)/shard_map/ppermute | solution.py:183
  41.6 0.0 collective-permute-done.14.refs_2_
  41.6 2.2 %collective-permute-start.1 = (bf16[3,64,384]{2,1,0:T(8,128)(2,1)S(1)}, bf16[3,64,384]{2,1,0:T(8,128)(2,1)S(1)}, u32[]{:S(2)}, u32[]{:S(2)}) collective-permute-start(bf16[3,64,384]{2,1,0:T(8,128)(2,1)S(1)} %get-tuple-element.33), channel_id=1, source_target_pairs={{0,8},{4,12},{8,0},{12,4},{1,9},{5,13},{9,1},{13,5},{2,10},{6,14},... | collective-permute-start | bytes 442376 | tf_op jit(solution)/shard_map/ppermute | solution.py:183
  43.8 0.0 collective-permute-done.15.refs_3_
  43.8 1.1 %collective-permute-start.2 = (bf16[3,64,384]{2,1,0:T(8,128)(2,1)S(1)}, bf16[3,64,384]{2,1,0:T(8,128)(2,1)S(1)}, u32[]{:S(2)}, u32[]{:S(2)}) collective-permute-start(bf16[3,64,384]{2,1,0:T(8,128)(2,1)S(1)} %get-tuple-element.34), channel_id=1, source_target_pairs={{0,12},{4,0},{8,4},{12,8},{1,13},{5,1},{9,5},{13,9},{2,14},{6,2},{... | collective-permute-start | bytes 442376 | tf_op jit(solution)/shard_map/ppermute | solution.py:183
  44.9 0.0 collective-permute-done.17.refs_4_
  44.9 1.1 %collective-permute-done.19.refs_10_ = bf16[4,64,384]{2,1,0:T(8,128)(2,1)S(1)} collective-permute-done((bf16[4,64,384]{2,1,0:T(8,128)(2,1)S(1)}, bf16[4,64,384]{2,1,0:T(8,128)(2,1)S(1)}, u32[]{:S(2)}, u32[]{:S(2)}) %collective-permute-start.19) | collective-permute-done | bytes 196640 | tf_op jit(solution)/shard_map/ppermute | solution.py:183
  46.0 0.9 %weight_grad.1 = (f32[3,96,384]{2,1,0:T(8,128)S(1)}, bf16[3,96,384]{2,1,0:T(8,128)(2,1)S(1)}) custom-call(bf16[192,256]{1,0:T(8,128)(2,1)S(1)} %collective-permute-done.12.refs_0_, bf16[192,256]{1,0:T(8,128)(2,1)S(1)} %collective-permute-done.13.refs_1_, bf16[192,256]{1,0:T(8,128)(2,1)S(1)} %collective-permute-done.14.refs_2_, ...), custom_call_target="tpu_custom_call" | custom-call | flops 377487360 | bytes 2433024 | tf_op jit(solution)/shard_map/weight_grad/pallas_call | solution.py:36
  46.9 1.6 %collective-permute-start.20 = (bf16[3,96,384]{2,1,0:T(8,128)(2,1)S(1)}, bf16[3,96,384]{2,1,0:T(8,128)(2,1)S(1)}, u32[]{:S(2)}, u32[]{:S(2)}) collective-permute-start(bf16[3,96,384]{2,1,0:T(8,128)(2,1)S(1)} %get-tuple-element.56), channel_id=1, source_target_pairs={{0,2},{2,0},{1,3},{3,1},{4,6},{6,4},{5,7},{7,5},{8,10},{10,8},{9,1... | collective-permute-start | bytes 663560 | tf_op jit(solution)/shard_map/ppermute | solution.py:183
  48.4 1.9 %collective-permute-start.6 = (bf16[64,384]{1,0:T(8,128)(2,1)S(1)}, bf16[64,384]{1,0:T(8,128)(2,1)S(1)}, u32[]{:S(2)}, u32[]{:S(2)}) collective-permute-start(bf16[64,384]{1,0:T(8,128)(2,1)S(1)} %get-tuple-element.38), channel_id=1, source_target_pairs={{0,4},{4,8},{8,12},{12,0},{1,5},{5,9},{9,13},{13,1},{2,6},{6,10},{... | collective-permute-start | bytes 147464 | tf_op jit(solution)/shard_map/ppermute | solution.py:183
  50.3 1.6 %collective-permute-done.refs_1_ = bf16[3,64,384]{2,1,0:T(8,128)(2,1)S(1)} collective-permute-done((bf16[3,64,384]{2,1,0:T(8,128)(2,1)S(1)}, bf16[3,64,384]{2,1,0:T(8,128)(2,1)S(1)}, u32[]{:S(2)}, u32[]{:S(2)}) %collective-permute-start) | collective-permute-done | bytes 147488 | tf_op jit(solution)/shard_map/ppermute | solution.py:183
  52.0 0.0 collective-permute-start.7
  52.0 4.9 %collective-permute-done.1.refs_2_ = bf16[3,64,384]{2,1,0:T(8,128)(2,1)S(1)} collective-permute-done((bf16[3,64,384]{2,1,0:T(8,128)(2,1)S(1)}, bf16[3,64,384]{2,1,0:T(8,128)(2,1)S(1)}, u32[]{:S(2)}, u32[]{:S(2)}) %collective-permute-start.1) | collective-permute-done | bytes 147488 | tf_op jit(solution)/shard_map/ppermute | solution.py:183
  56.8 3.3 %collective-permute-start.8 = (bf16[64,384]{1,0:T(8,128)(2,1)S(1)}, bf16[64,384]{1,0:T(8,128)(2,1)S(1)}, u32[]{:S(2)}, u32[]{:S(2)}) collective-permute-start(bf16[64,384]{1,0:T(8,128)(2,1)S(1)} %get-tuple-element.40), channel_id=1, source_target_pairs={{0,12},{4,0},{8,4},{12,8},{1,13},{5,1},{9,5},{13,9},{2,14},{6,2},{... | collective-permute-start | bytes 147464 | tf_op jit(solution)/shard_map/ppermute | solution.py:183
  60.1 0.0 collective-permute-done.2.refs_3_
  60.1 0.0 collective-permute-done.6.refs_5_
  60.1 3.0 %collective-permute-done.7.refs_6_ = bf16[64,384]{1,0:T(8,128)(2,1)S(1)} collective-permute-done((bf16[64,384]{1,0:T(8,128)(2,1)S(1)}, bf16[64,384]{1,0:T(8,128)(2,1)S(1)}, u32[]{:S(2)}, u32[]{:S(2)}) %collective-permute-start.7) | collective-permute-done | bytes 49184 | tf_op jit(solution)/shard_map/ppermute | solution.py:183
  63.1 0.0 collective-permute-done.8.refs_7_
  63.2 2.0 %attention.1 = (bf16[3,64,384]{2,1,0:T(8,128)(2,1)S(1)}, bf16[3,64,384]{2,1,0:T(8,128)(2,1)S(1)}, bf16[3,64,384]{2,1,0:T(8,128)(2,1)S(1)}, bf16[3,64,384]{2,1,0:T(8,128)(2,1)S(1)}) custom-call(bf16[3,64,384]{2,1,0:T(8,128)(2,1)S(1)} %get-tuple-element.31.refs_0_, bf16[3,64,384]{2,1,0:T(8,128)(2,1)S(1)} %collective-permute-done.refs_1_, ...), custom_call_target="tpu_custom_call" | custom-call | flops 251658240 | bytes 1376256 | tf_op jit(solution)/shard_map/attention/pallas_call | solution.py:36
  65.2 2.9 %collective-permute-start.9 = (bf16[3,64,384]{2,1,0:T(8,128)(2,1)S(1)}, bf16[3,64,384]{2,1,0:T(8,128)(2,1)S(1)}, u32[]{:S(2)}, u32[]{:S(2)}) collective-permute-start(bf16[3,64,384]{2,1,0:T(8,128)(2,1)S(1)} %get-tuple-element.42), channel_id=1, source_target_pairs={{0,12},{4,0},{8,4},{12,8},{1,13},{5,1},{9,5},{13,9},{2,14},{6,2},{... | collective-permute-start | bytes 442376 | tf_op jit(solution)/shard_map/ppermute | solution.py:183
  68.0 0.0 collective-permute-start.10
  68.1 0.6 collective-permute-start.11
  68.7 3.5 %collective-permute-done.9.refs_1_ = bf16[3,64,384]{2,1,0:T(8,128)(2,1)S(1)} collective-permute-done((bf16[3,64,384]{2,1,0:T(8,128)(2,1)S(1)}, bf16[3,64,384]{2,1,0:T(8,128)(2,1)S(1)}, u32[]{:S(2)}, u32[]{:S(2)}) %collective-permute-start.9) | collective-permute-done | bytes 147488 | tf_op jit(solution)/shard_map/ppermute | solution.py:183
  72.2 8.6 %collective-permute-done.10.refs_2_ = bf16[3,64,384]{2,1,0:T(8,128)(2,1)S(1)} collective-permute-done((bf16[3,64,384]{2,1,0:T(8,128)(2,1)S(1)}, bf16[3,64,384]{2,1,0:T(8,128)(2,1)S(1)}, u32[]{:S(2)}, u32[]{:S(2)}) %collective-permute-start.10) | collective-permute-done | bytes 147488 | tf_op jit(solution)/shard_map/ppermute | solution.py:183
  80.8 0.0 collective-permute-done.11.refs_3_
  80.8 0.9 %place.1 = (bf16[4,64,384]{2,1,0:T(8,128)(2,1)}, bf16[4,64,384]{2,1,0:T(8,128)(2,1)}, bf16[4,64,384]{2,1,0:T(8,128)(2,1)}) custom-call(bf16[3,64,384]{2,1,0:T(8,128)(2,1)S(1)} %get-tuple-element.41.refs_0_, bf16[3,64,384]{2,1,0:T(8,128)(2,1)S(1)} %collective-permute-done.9.refs_1_, bf16[3,64,384]{2,1,0:T(8,128)(2,1)S(1)} %collective-permute-done.10.refs_2_, ...), custom_call_target="tpu_custom_call" | custom-call | bytes 1179648 | tf_op jit(solution)/shard_map/place/pallas_call | solution.py:36
  81.7 0.0 collective-permute-done.20.got_ref
  81.7 0.8 add_weight.1
Async XLA Ops:
  0.6 10.0 %collective-permute-start.4 = (bf16[4,64,384]{2,1,0:T(8,128)(2,1)}, bf16[4,64,384]{2,1,0:T(8,128)(2,1)S(1)}, u32[]{:S(2)}, u32[]{:S(2)}) collective-permute-start(bf16[4,64,384]{2,1,0:T(8,128)(2,1)} %refs_7_.1), channel_id=1, source_target_pairs={{4,0},{8,4},{12,8},{5,1},{9,5},{13,9},{6,2},{10,6},{14,10},{7,3},{... | collective-permute-start | bytes 589832 | tf_op jit(solution)/shard_map/ppermute | solution.py:183
  1.9 10.0 %collective-permute-start.3 = (bf16[4,64,384]{2,1,0:T(8,128)(2,1)}, bf16[4,64,384]{2,1,0:T(8,128)(2,1)S(1)}, u32[]{:S(2)}, u32[]{:S(2)}) collective-permute-start(bf16[4,64,384]{2,1,0:T(8,128)(2,1)} %refs_7_.1), channel_id=1, source_target_pairs={{0,4},{4,8},{8,12},{1,5},{5,9},{9,13},{2,6},{6,10},{10,14},{3,7},{... | collective-permute-start | bytes 589832 | tf_op jit(solution)/shard_map/ppermute | solution.py:183
  12.0 0.9 %copy-start = (bf16[4,64,384]{2,1,0:T(8,128)(2,1)S(1)}, bf16[4,64,384]{2,1,0:T(8,128)(2,1)}, u32[]{:S(2)}) copy-start(bf16[4,64,384]{2,1,0:T(8,128)(2,1)} %refs_7_.1) | copy-start | bytes 589828
  12.9 1.5 %copy-start.2 = (bf16[768,3,384]{2,0,1:T(8,128)(2,1)S(1)}, bf16[768,3,384]{2,0,1:T(8,128)(2,1)}, u32[]{:S(2)}) copy-start(bf16[768,3,384]{2,0,1:T(8,128)(2,1)} %param.11) | copy-start | bytes 5308420
  14.4 1.0 %copy-start.3 = (bf16[4,64,384]{2,1,0:T(8,128)(2,1)S(1)}, bf16[4,64,384]{2,1,0:T(8,128)(2,1)}, u32[]{:S(2)}) copy-start(bf16[4,64,384]{2,1,0:T(8,128)(2,1)} %h_ref.3) | copy-start | bytes 589828
  14.4 1.0 %copy-start.4 = (bf16[4,64,384]{2,1,0:T(8,128)(2,1)S(1)}, bf16[4,64,384]{2,1,0:T(8,128)(2,1)}, u32[]{:S(2)}) copy-start(bf16[4,64,384]{2,1,0:T(8,128)(2,1)} %q_ref.1) | copy-start | bytes 589828
  14.4 1.1 %copy-start.5 = (bf16[4,64,384]{2,1,0:T(8,128)(2,1)S(1)}, bf16[4,64,384]{2,1,0:T(8,128)(2,1)}, u32[]{:S(2)}) copy-start(bf16[4,64,384]{2,1,0:T(8,128)(2,1)} %k_ref.1) | copy-start | bytes 589828
  14.4 1.2 %copy-start.6 = (bf16[4,64,384]{2,1,0:T(8,128)(2,1)S(1)}, bf16[4,64,384]{2,1,0:T(8,128)(2,1)}, u32[]{:S(2)}) copy-start(bf16[4,64,384]{2,1,0:T(8,128)(2,1)} %v_ref.1) | copy-start | bytes 589828
  14.4 2.4 %copy-start.1 = (bf16[4,64,384]{2,1,0:T(8,128)(2,1)S(1)}, bf16[4,64,384]{2,1,0:T(8,128)(2,1)}, u32[]{:S(2)}) copy-start(bf16[4,64,384]{2,1,0:T(8,128)(2,1)} %refs_7_.1) | copy-start | bytes 589828
  15.3 1.5 %collective-permute-start.5 = (bf16[4,64,384]{2,1,0:T(8,128)(2,1)S(1)}, bf16[4,64,384]{2,1,0:T(8,128)(2,1)S(1)}, u32[]{:S(2)}, u32[]{:S(2)}) collective-permute-start(bf16[4,64,384]{2,1,0:T(8,128)(2,1)S(1)} %get-tuple-element.36), channel_id=1, source_target_pairs={{0,1},{1,0},{2,3},{3,2},{4,5},{5,4},{6,7},{7,6},{8,9},{9,8},{10,11... | collective-permute-start | bytes 589832 | tf_op jit(solution)/shard_map/ppermute | solution.py:183
  18.0 14.9 %collective-permute-start.16 = (bf16[4,64,384]{2,1,0:T(8,128)(2,1)S(1)}, bf16[4,64,384]{2,1,0:T(8,128)(2,1)S(1)}, u32[]{:S(2)}, u32[]{:S(2)}) collective-permute-start(bf16[4,64,384]{2,1,0:T(8,128)(2,1)S(1)} %collective-permute-done.3.left_ref.refs_6_), channel_id=1, source_target_pairs={{0,4},{4,8},{8,12},{1,5},{5,9},{9,13},{2,6},{6,10},{10,14},{3,7},{... | collective-permute-start | bytes 589832 | tf_op jit(solution)/shard_map/ppermute | solution.py:183
  22.3 15.3 %collective-permute-start.18 = (bf16[4,64,384]{2,1,0:T(8,128)(2,1)S(1)}, bf16[4,64,384]{2,1,0:T(8,128)(2,1)S(1)}, u32[]{:S(2)}, u32[]{:S(2)}) collective-permute-start(bf16[4,64,384]{2,1,0:T(8,128)(2,1)S(1)} %collective-permute-done.4.right_ref.refs_8_), channel_id=1, source_target_pairs={{4,0},{8,4},{12,8},{5,1},{9,5},{13,9},{6,2},{10,6},{14,10},{7,3},{... | collective-permute-start | bytes 589832 | tf_op jit(solution)/shard_map/ppermute | solution.py:183
  23.6 3.4 %collective-permute-start.12 = (bf16[192,256]{1,0:T(8,128)(2,1)S(1)}, bf16[192,256]{1,0:T(8,128)(2,1)S(1)}, u32[]{:S(2)}, u32[]{:S(2)}) collective-permute-start(bf16[192,256]{1,0:T(8,128)(2,1)S(1)} %get-tuple-element.51), channel_id=1, source_target_pairs={{0,0},{1,8},{4,4},{5,12},{8,1},{9,9},{12,5},{13,13},{2,2},{3,10},{... | collective-permute-start | bytes 294920 | tf_op jit(solution)/shard_map/ppermute | solution.py:234
  24.3 14.6 %collective-permute-start.13 = (bf16[192,256]{1,0:T(8,128)(2,1)S(1)}, bf16[192,256]{1,0:T(8,128)(2,1)S(1)}, u32[]{:S(2)}, u32[]{:S(2)}) collective-permute-start(bf16[192,256]{1,0:T(8,128)(2,1)S(1)} %get-tuple-element.52), channel_id=1, source_target_pairs={{0,4},{1,12},{4,0},{5,8},{8,5},{9,13},{12,1},{13,9},{2,6},{3,14},{... | collective-permute-start | bytes 294920 | tf_op jit(solution)/shard_map/ppermute | solution.py:234
  27.0 14.7 %collective-permute-start.14 = (bf16[192,256]{1,0:T(8,128)(2,1)S(1)}, bf16[192,256]{1,0:T(8,128)(2,1)S(1)}, u32[]{:S(2)}, u32[]{:S(2)}) collective-permute-start(bf16[192,256]{1,0:T(8,128)(2,1)S(1)} %collective-permute-done.12.refs_0_), channel_id=1, source_target_pairs={{0,1},{1,0},{2,3},{3,2},{4,5},{5,4},{6,7},{7,6},{8,9},{9,8},{10,11... | collective-permute-start | bytes 294920 | tf_op jit(solution)/shard_map/ppermute | solution.py:183
  32.9 12.0 %collective-permute-start.17 = (bf16[4,64,384]{2,1,0:T(8,128)(2,1)S(1)}, bf16[4,64,384]{2,1,0:T(8,128)(2,1)S(1)}, u32[]{:S(2)}, u32[]{:S(2)}) collective-permute-start(bf16[4,64,384]{2,1,0:T(8,128)(2,1)S(1)} %collective-permute-done.16.refs_5_), channel_id=1, source_target_pairs={{0,4},{4,8},{8,12},{1,5},{5,9},{9,13},{2,6},{6,10},{10,14},{3,7},{... | collective-permute-start | bytes 589832 | tf_op jit(solution)/shard_map/ppermute | solution.py:183
  37.6 8.4 %collective-permute-start.19 = (bf16[4,64,384]{2,1,0:T(8,128)(2,1)S(1)}, bf16[4,64,384]{2,1,0:T(8,128)(2,1)S(1)}, u32[]{:S(2)}, u32[]{:S(2)}) collective-permute-start(bf16[4,64,384]{2,1,0:T(8,128)(2,1)S(1)} %collective-permute-done.18.refs_9_), channel_id=1, source_target_pairs={{4,0},{8,4},{12,8},{5,1},{9,5},{13,9},{6,2},{10,6},{14,10},{7,3},{... | collective-permute-start | bytes 589832 | tf_op jit(solution)/shard_map/ppermute | solution.py:183
  38.9 5.0 %collective-permute-start.15 = (bf16[192,256]{1,0:T(8,128)(2,1)S(1)}, bf16[192,256]{1,0:T(8,128)(2,1)S(1)}, u32[]{:S(2)}, u32[]{:S(2)}) collective-permute-start(bf16[192,256]{1,0:T(8,128)(2,1)S(1)} %collective-permute-done.13.refs_1_), channel_id=1, source_target_pairs={{0,1},{1,0},{2,3},{3,2},{4,5},{5,4},{6,7},{7,6},{8,9},{9,8},{10,11... | collective-permute-start | bytes 294920 | tf_op jit(solution)/shard_map/ppermute | solution.py:183
  38.9 13.0 %collective-permute-start = (bf16[3,64,384]{2,1,0:T(8,128)(2,1)S(1)}, bf16[3,64,384]{2,1,0:T(8,128)(2,1)S(1)}, u32[]{:S(2)}, u32[]{:S(2)}) collective-permute-start(bf16[3,64,384]{2,1,0:T(8,128)(2,1)S(1)} %get-tuple-element.32), channel_id=1, source_target_pairs={{0,4},{4,8},{8,12},{12,0},{1,5},{5,9},{9,13},{13,1},{2,6},{6,10},{... | collective-permute-start | bytes 442376 | tf_op jit(solution)/shard_map/ppermute | solution.py:183
  41.6 15.2 %collective-permute-start.1 = (bf16[3,64,384]{2,1,0:T(8,128)(2,1)S(1)}, bf16[3,64,384]{2,1,0:T(8,128)(2,1)S(1)}, u32[]{:S(2)}, u32[]{:S(2)}) collective-permute-start(bf16[3,64,384]{2,1,0:T(8,128)(2,1)S(1)} %get-tuple-element.33), channel_id=1, source_target_pairs={{0,8},{4,12},{8,0},{12,4},{1,9},{5,13},{9,1},{13,5},{2,10},{6,14},... | collective-permute-start | bytes 442376 | tf_op jit(solution)/shard_map/ppermute | solution.py:183
  43.8 16.3 %collective-permute-start.2 = (bf16[3,64,384]{2,1,0:T(8,128)(2,1)S(1)}, bf16[3,64,384]{2,1,0:T(8,128)(2,1)S(1)}, u32[]{:S(2)}, u32[]{:S(2)}) collective-permute-start(bf16[3,64,384]{2,1,0:T(8,128)(2,1)S(1)} %get-tuple-element.34), channel_id=1, source_target_pairs={{0,12},{4,0},{8,4},{12,8},{1,13},{5,1},{9,5},{13,9},{2,14},{6,2},{... | collective-permute-start | bytes 442376 | tf_op jit(solution)/shard_map/ppermute | solution.py:183
  46.9 34.8 %collective-permute-start.20 = (bf16[3,96,384]{2,1,0:T(8,128)(2,1)S(1)}, bf16[3,96,384]{2,1,0:T(8,128)(2,1)S(1)}, u32[]{:S(2)}, u32[]{:S(2)}) collective-permute-start(bf16[3,96,384]{2,1,0:T(8,128)(2,1)S(1)} %get-tuple-element.56), channel_id=1, source_target_pairs={{0,2},{2,0},{1,3},{3,1},{4,6},{6,4},{5,7},{7,5},{8,10},{10,8},{9,1... | collective-permute-start | bytes 663560 | tf_op jit(solution)/shard_map/ppermute | solution.py:183
  48.4 11.7 %collective-permute-start.6 = (bf16[64,384]{1,0:T(8,128)(2,1)S(1)}, bf16[64,384]{1,0:T(8,128)(2,1)S(1)}, u32[]{:S(2)}, u32[]{:S(2)}) collective-permute-start(bf16[64,384]{1,0:T(8,128)(2,1)S(1)} %get-tuple-element.38), channel_id=1, source_target_pairs={{0,4},{4,8},{8,12},{12,0},{1,5},{5,9},{9,13},{13,1},{2,6},{6,10},{... | collective-permute-start | bytes 147464 | tf_op jit(solution)/shard_map/ppermute | solution.py:183
  52.0 11.2 %collective-permute-start.7 = (bf16[64,384]{1,0:T(8,128)(2,1)S(1)}, bf16[64,384]{1,0:T(8,128)(2,1)S(1)}, u32[]{:S(2)}, u32[]{:S(2)}) collective-permute-start(bf16[64,384]{1,0:T(8,128)(2,1)S(1)} %get-tuple-element.39), channel_id=1, source_target_pairs={{0,8},{4,12},{8,0},{12,4},{1,9},{5,13},{9,1},{13,5},{2,10},{6,14},... | collective-permute-start | bytes 147464 | tf_op jit(solution)/shard_map/ppermute | solution.py:183
  56.8 6.3 %collective-permute-start.8 = (bf16[64,384]{1,0:T(8,128)(2,1)S(1)}, bf16[64,384]{1,0:T(8,128)(2,1)S(1)}, u32[]{:S(2)}, u32[]{:S(2)}) collective-permute-start(bf16[64,384]{1,0:T(8,128)(2,1)S(1)} %get-tuple-element.40), channel_id=1, source_target_pairs={{0,12},{4,0},{8,4},{12,8},{1,13},{5,1},{9,5},{13,9},{2,14},{6,2},{... | collective-permute-start | bytes 147464 | tf_op jit(solution)/shard_map/ppermute | solution.py:183
  65.2 7.1 %collective-permute-start.9 = (bf16[3,64,384]{2,1,0:T(8,128)(2,1)S(1)}, bf16[3,64,384]{2,1,0:T(8,128)(2,1)S(1)}, u32[]{:S(2)}, u32[]{:S(2)}) collective-permute-start(bf16[3,64,384]{2,1,0:T(8,128)(2,1)S(1)} %get-tuple-element.42), channel_id=1, source_target_pairs={{0,12},{4,0},{8,4},{12,8},{1,13},{5,1},{9,5},{13,9},{2,14},{6,2},{... | collective-permute-start | bytes 442376 | tf_op jit(solution)/shard_map/ppermute | solution.py:183
  68.0 12.8 %collective-permute-start.10 = (bf16[3,64,384]{2,1,0:T(8,128)(2,1)S(1)}, bf16[3,64,384]{2,1,0:T(8,128)(2,1)S(1)}, u32[]{:S(2)}, u32[]{:S(2)}) collective-permute-start(bf16[3,64,384]{2,1,0:T(8,128)(2,1)S(1)} %get-tuple-element.43), channel_id=1, source_target_pairs={{0,8},{4,12},{8,0},{12,4},{1,9},{5,13},{9,1},{13,5},{2,10},{6,14},... | collective-permute-start | bytes 442376 | tf_op jit(solution)/shard_map/ppermute | solution.py:183
  68.1 12.8 %collective-permute-start.11 = (bf16[3,64,384]{2,1,0:T(8,128)(2,1)S(1)}, bf16[3,64,384]{2,1,0:T(8,128)(2,1)S(1)}, u32[]{:S(2)}, u32[]{:S(2)}) collective-permute-start(bf16[3,64,384]{2,1,0:T(8,128)(2,1)S(1)} %get-tuple-element.44), channel_id=1, source_target_pairs={{0,4},{4,8},{8,12},{12,0},{1,5},{5,9},{9,13},{13,1},{2,6},{6,10},{... | collective-permute-start | bytes 442376 | tf_op jit(solution)/shard_map/ppermute | solution.py:183

commit v2 on v1

--- a/solution.py
+++ b/solution.py
@@ -11,6 +11,7 @@
 HD = 96
 BF = jnp.bfloat16
 F32 = jnp.float32
+COST = 8
 VMEM_LIMIT = 40 * 1024 * 1024
 
 
@@ -27,16 +28,19 @@
     )
 
 
-def kernel_call(body, outs, flops=0, transcendentals=0, name=None, scratch=()):
+def kernel_call(body, outs, flops=0, transcendentals=0, name=None, scratch=(), space=pltpu.VMEM):
     vmem = pl.BlockSpec(memory_space=pltpu.VMEM)
+    given = pl.BlockSpec(memory_space=space)
 
     def call(*args):
+        if space == pltpu.HBM:
+            args = [pltpu.with_memory_space_constraint(a, pltpu.HBM) for a in args]
         moved = sum(math.prod(a.shape) * a.dtype.itemsize for a in args)
         moved += sum(math.prod(o.shape) * o.dtype.itemsize for o in outs)
         return pl.pallas_call(
             body,
             out_shape=list(outs),
-            in_specs=[vmem] * len(args),
+            in_specs=[given] * len(args),
             out_specs=[vmem] * len(outs),
             scratch_shapes=list(scratch),
             compiler_params=pltpu.CompilerParams(vmem_limit_bytes=VMEM_LIMIT),
@@ -53,24 +57,41 @@
     return jax.ShapeDtypeStruct(dims, dtype)
 
 
-def prepare_kernel(count, q_ref, k_ref, v_ref, h_ref, *outs):
+def prepare_kernel(count, q_hbm, k_hbm, v_hbm, h_hbm, cot_hbm, w_hbm, *refs):
+    outs, (act_ref, h_ref, cot_ref, w_ref, sems) = refs[: count + 1], refs[count + 1 :]
     s = lax.axis_index("seq")
-    for d in range(count):
-        b = lax.rem(s + d, count)
-        for j, ref in enumerate((q_ref, k_ref, v_ref)):
-            outs[d][j] = ref[b]
-    act_refs = outs[count : count + 2]
+    near = [pltpu.make_async_copy(h_hbm, h_ref, sems.at[0])]
+    for d in range(count + 1):
+        b = lax.rem(s + d, count) if d < count else count - 1 - s
+        for j, ref in enumerate((q_hbm, k_hbm, v_hbm)):
+            near.append(
+                pltpu.make_async_copy(ref.at[b], outs[d].at[j], sems.at[1 + 3 * d + j])
+            )
+    near.append(pltpu.make_async_copy(cot_hbm, cot_ref, sems.at[4 + 3 * count]))
+    near.append(pltpu.make_async_copy(w_hbm, w_ref, sems.at[5 + 3 * count]))
+    for copy in near:
+        copy.start()
+    near[0].wait()
     blocks, rows, width = h_ref.shape
     act = tanh_gelu(h_ref[...].astype(F32)).reshape(blocks * rows, width)
     act_t = act.T.astype(BF)
-    half = width // 2
-    first = lax.rem(s, 2) == 0
-    low, high = act_t[:half], act_t[half:]
-    act_refs[0][...] = jnp.where(first, low, high)
-    act_refs[1][...] = jnp.where(first, high, low)
-
-
-def conv_kernel(cot_ref, left_ref, right_ref, w_ref, mine_ref, other_ref):
+    lanes = act_t.shape[1] // 2
+    parts = width // lanes
+    for i in range(2 * parts):
+        for h in range(2):
+            act_ref[i // parts * 2 + h, :, pl.ds(i % parts * lanes, lanes)] = act_t[
+                i * rows : (i + 1) * rows, h * lanes : (h + 1) * lanes
+            ]
+    for copy in near[1:]:
+        copy.wait()
+
+
+def conv_kernel(
+    cot_ref, left_ref, right_ref, w_ref, act_ref, mine_ref, other_ref, inner_ref, outer_ref
+):
+    first = lax.axis_index("seq") < 2
+    inner_ref[...] = jnp.where(first, right_ref[...], left_ref[...])
+    outer_ref[...] = jnp.where(first, left_ref[...], right_ref[...])
     c = lax.axis_index("chan")
     blocks, rows, width = cot_ref.shape
     taps = [r[...].reshape(blocks * rows, width) for r in (right_ref, cot_ref, left_ref)]
@@ -85,28 +106,38 @@
                 preferred_element_type=F32,
             )
             total = term if total is None else total + term
-        out_ref[...] = total.astype(BF).reshape(blocks, rows, width)
-
-
-def grad_kernel(count, cot_ref, h_ref, mine_ref, other_ref, grad_ref, *pieces):
+        out_ref[:blocks] = total.astype(BF).reshape(blocks, rows, width)
+    other_ref[blocks:] = act_ref[...]
+
+
+def grad_kernel(count, cot_ref, h_ref, mine_ref, other_ref, act_ref, *pieces):
     s = lax.axis_index("seq")
-    back = mine_ref[...].astype(F32) + other_ref[...].astype(F32)
-    slope = gelu_slope(h_ref[...].astype(F32))
-    grad_ref[...] = (cot_ref[...].astype(F32) + back * slope).astype(BF)
+    c = lax.axis_index("chan")
+    blocks = cot_ref.shape[0]
     for d in range(count):
-        pieces[d][...] = grad_ref[lax.rem(s + d, count)]
-
-
-def attention_kernel(count, *refs):
-    qkv = refs[:count]
-    grads = refs[count : 2 * count]
-    outs = refs[2 * count :]
-    rows, width = grads[0].shape
+        b = lax.rem(s + d, count)
+        back = mine_ref[b].astype(F32) + other_ref[b].astype(F32)
+        slope = gelu_slope(h_ref[b].astype(F32))
+        pieces[d][0] = (cot_ref[b].astype(F32) + back * slope).astype(BF)
+        here = lax.div(b, 2) == c
+        for h in range(2):
+            k = 2 * lax.rem(b, 2) + h
+            pieces[d][1 + h] = jnp.where(here, act_ref[k], other_ref[blocks + k])
+
+
+def attention_kernel(count, own, down, opposite, up, ends, *refs):
+    grads, outs = refs[:count], refs[count:]
+    _, rows, width = grads[0].shape
     scale = 1.0 / math.sqrt(HD)
-    query, key, value = (
-        jnp.concatenate([qkv[d][j] for d in range(count)], axis=0) for j in range(3)
-    )
-    grad = jnp.concatenate([grads[d][...] for d in range(count)], axis=0)
+    s = lax.axis_index("seq")
+
+    def positions(j):
+        before = jnp.where(s == 0, ends[j], down[j])
+        behind = jnp.where(s == count - 1, ends[j], up[j])
+        return jnp.concatenate([own[j], before, opposite[j], behind], axis=0)
+
+    query, key, value = (positions(j) for j in range(3))
+    grad = jnp.concatenate([grads[d][0] for d in range(count)], axis=0)
     nt = (((1,), (1,)), ((), ()))
     nn = (((1,), (0,)), ((), ()))
     tn = (((0,), (0,)), ((), ()))
@@ -131,27 +162,50 @@
 
 
 def weight_kernel(count, factor, *refs):
-    acts, cots = refs[:4], refs[4 : 4 + 2 * count - 1]
-    own_ref, sent_ref, act_buf, cot_buf = refs[4 + 2 * count - 1 :]
+    cots, grads, got = refs[:6], refs[6 : 6 + count], (refs[6], *refs[6 + count : 5 + 2 * count])
+    own_ref, sent0_ref, sent1_ref, grad_ref, act_buf, cot_buf = refs[5 + 2 * count :]
     s = lax.axis_index("seq")
-    c = lax.axis_index("chan")
     b = lax.axis_index("batch")
-    for k in range(2):
-        for side, piece in ((c, acts[k]), (1 - c, acts[2 + k])):
-            act_buf[2 * side + lax.rem(s + k, 2)] = piece[...]
-    for r in range(-(count - 1), count):
-        piece = cots[r + count - 1]
-        blocks, rows, width = piece.shape
-
-        @pl.when(jnp.logical_and(s + r >= 0, s + r < count))
-        def _():
-            cot_buf[s + r] = piece[...].reshape(blocks * rows, width)
+    _, rows, width = got[0].shape
+    lanes = act_buf.shape[2] // 2
+    for d in range(count):
+        j = lax.rem(s - d + count, count)
+        for r in range(width // lanes):
+            for h in range(2):
+                act_buf[j, pl.ds(r * rows, rows), pl.ds(h * lanes, lanes)] = got[d][
+                    1 + h, :, pl.ds(r * lanes, lanes)
+                ]
+    own_cot, left, right, far, across, farthest = cots
+    flat = cot_buf.shape[1:]
+    cot_buf[s] = own_cot[...].reshape(flat)
+
+    @pl.when(s > 0)
+    def _():
+        cot_buf[s - 1] = left[...].reshape(flat)
+
+    @pl.when(s < count - 1)
+    def _():
+        cot_buf[s + 1] = right[...].reshape(flat)
+
+    low = s < 2
+
+    @pl.when(jnp.logical_or(s == 0, s == 3))
+    def _():
+        cot_buf[jnp.where(low, 2, 1)] = far[...].reshape(flat)
+        cot_buf[jnp.where(low, 3, 0)] = farthest[...].reshape(flat)
+
+    @pl.when(jnp.logical_or(s == 1, s == 2))
+    def _():
+        cot_buf[jnp.where(low, 3, 0)] = across[...].reshape(flat)
+
+    for d in range(count):
+        grad_ref[lax.rem(s + d, count)] = grads[d][0]
 
     half = own_ref.shape[1]
     for t in range(3):
         low = max(0, 1 - t)
         high = min(count, count + 1 - t)
-        for out_ref, side in ((sent_ref, 1 - b), (own_ref, b)):
+        for is_own, side in ((False, 1 - b), (True, b)):
             start = pl.multiple_of(side * half, half)
             total = None
             for j in range(low, high):
@@ -161,11 +215,18 @@
                     preferred_element_type=F32,
                 )
                 total = term if total is None else total + term
-            out_ref[t] = (factor * total).astype(out_ref.dtype)
-
-
-def add_kernel(own_ref, got_ref, out_ref):
-    out_ref[...] = own_ref[...] + got_ref[...].astype(F32)
+            total = factor * total
+            if is_own:
+                own_ref[t] = total
+            else:
+                sent0_ref[t] = total[: half // 2].astype(BF)
+                sent1_ref[t] = total[half // 2 :].astype(BF)
+
+
+def add_kernel(own_ref, got0_ref, got1_ref, out_ref):
+    half = got0_ref.shape[1]
+    out_ref[:, :half] = own_ref[:, :half] + got0_ref[...].astype(F32)
+    out_ref[:, half:] = own_ref[:, half:] + got1_ref[...].astype(F32)
 
 
 def place_kernel(count, *refs):
@@ -201,66 +262,59 @@
 
     left = shift(cotangent, "seq", 1, False)
     right = shift(cotangent, "seq", -1, False)
-    *qkv, act0, act1 = kernel_call(
+    own_qkv, to_down, to_opposite, to_up, to_end, act, hidden, own_cot, weights = kernel_call(
         functools.partial(prepare_kernel, count),
-        [piece3] * count + [shape((part, tokens))] * 2,
-        transcendentals=tokens * width,
+        [piece3] * (count + 1) + [full] * 3 + [shape(weights.shape)],
         name="prepare",
-    )(query_vectors, key_vectors, value_vectors, hidden)
-    got_qkv = [qkv[0]] + [shift(qkv[d], "seq", d, True) for d in range(1, count)]
-
-    mine, other = kernel_call(
-        conv_kernel, [full, full], flops=2 * tokens * 3 * width * 2 * width, name="conv_back"
-    )(cotangent, left, right, weights)
+        scratch=[pltpu.SemaphoreType.DMA((3 * count + 6,))],
+        space=pltpu.HBM,
+    )(query_vectors, key_vectors, value_vectors, hidden, cotangent, weights)
+
+    down = shift(to_down, "seq", 1, False)
+    up = shift(to_up, "seq", -1, False)
+    opposite = shift(to_opposite, "seq", 2, True)
+    ends = lax.ppermute(to_end, "seq", [(0, count - 1), (count - 1, 0)])
+    near_left, right = after(down, left, right)
+    near_left, right = after(up, near_left, right)
+    mine, other, inner, outer = kernel_call(
+        conv_kernel, [full, shape((2 * blocks, rows, width)), full, full], name="conv_back"
+    )(own_cot, near_left, right, weights, act)
     got = shift(other, "chan", 1, True)
-    hidden_grad, *grads = kernel_call(
-        functools.partial(grad_kernel, count),
-        [full] + [piece] * count,
-        transcendentals=tokens * width,
-        name="hidden_grad",
-    )(cotangent, hidden, mine, got)
+    grads = kernel_call(
+        functools.partial(grad_kernel, count), [piece3] * count, name="hidden_grad"
+    )(own_cot, hidden, mine, got, act)
     got_grads = [grads[0]] + [shift(grads[d], "seq", d, True) for d in range(1, count)]
 
-    far_left, far_right, act0, act1 = after(grads[0], left, right, act0, act1)
-    lefts, rights = [far_left], [far_right]
-    n_chan = lax.axis_size("chan")
-    got_act = []
-    for k, act in enumerate((act0, act1)):
-        pairs = []
-        for i in range(count):
-            for c in range(n_chan):
-                to = (2 * c + (i + k) % 2) * n_chan + i // 2
-                pairs.append((i * n_chan + c, to))
-        got_act.append(lax.ppermute(act, ("seq", "chan"), pairs))
-    for _ in range(count - 2):
-        lefts.append(shift(lefts[-1], "seq", 1, False))
-        rights.append(shift(rights[-1], "seq", -1, False))
-    other_act = [shift(a, "chan", 1, True) for a in got_act]
-
+    inner, outer = after(grads[0], *after(opposite, inner, outer))
+    far = lax.ppermute(inner, "seq", [(1, 0), (2, 3)])
+    across = lax.ppermute(outer, "seq", [(1, 2), (2, 1)])
+    farthest = lax.ppermute(across, "seq", [(1, 0), (2, 3)])
+    (own_qkv,) = after(across, own_qkv)
     item = 5 * (count * rows) ** 2 * width
     returned = kernel_call(
         functools.partial(attention_kernel, count),
         [piece3] * count,
-        flops=2 * item,
+        flops=COST * 2 * item,
         transcendentals=(count * rows) ** 2 * (width // HD),
         name="attention",
-    )(*got_qkv, *got_grads)
+    )(own_qkv, down, opposite, up, ends, *got_grads)
     back = [returned[0]] + [shift(returned[d], "seq", -d, True) for d in range(1, count)]
 
-    own, sent = kernel_call(
+    own_cot, near_left = after(returned[0], own_cot, near_left)
+    own, sent0, sent1, hidden_grad = kernel_call(
         functools.partial(weight_kernel, count, factor),
-        [shape((3, part // 2, width), F32), shape((3, part // 2, width))],
-        flops=2 * (3 * count - 2) * tokens * part * width,
+        [shape((3, part // 2, width), F32)] + [shape((3, part // 4, width))] * 2 + [full],
         name="weight_grad",
         scratch=[
             pltpu.VMEM((count, part, tokens), BF),
             pltpu.VMEM((count, tokens, width), BF),
         ],
-    )(*got_act, *other_act, *reversed(lefts), cotangent, *rights)
-    got_sum = shift(sent, "batch", 1, True)
+    )(own_cot, near_left, right, far, across, farthest, *grads, *got_grads[1:])
+    got_sums = [shift(x, "batch", 1, True) for x in (sent0, sent1)]
     (weight_grad,) = kernel_call(add_kernel, [shape((3, part // 2, width), F32)], name="add_weight")(
-        own, got_sum
-    )
+        own, *got_sums
+    )
+    (back[0],) = after(weight_grad, back[0])
     query_grad, key_grad, value_grad = kernel_call(
         functools.partial(place_kernel, count), [full] * 3, name="place"
     )(*back)

time: 82.8 us -> 73.3 us (0.89)
  starting transfers between devices: 44 us -> 31.5 us
  waiting for transfers between devices: 28.2 us -> 32.1 us
  local copies, waits for them, and re-layouts: 2.59 us -> 0 us
  Pallas kernels: 6.91 us -> 8.66 us
    ppermute x19 -> x14, starting transfers between devices: 40.6 us -> 25.1 us  [shift(): return lax.ppermute(x, axis, pairs)]
    ppermute x2 -> x4, starting transfers between devices: 3.37 us -> 6.43 us  [the longest x1 3.19 us: per_device(): ends = lax.ppermute(to_end, 'seq', [(0, count - 1), (count - 1, 0)])]
    ppermute x2 -> x4, waiting for transfers between devices: 0.01 us -> 2.66 us  [the longest x1 2.27 us: per_device(): ends = lax.ppermute(to_end, 'seq', [(0, count - 1), (count - 1, 0)])]
    unnamed x14 -> x0, local copies, waits for them, and re-layouts: 2.59 us -> none
    pallas_call x7, Pallas kernels: 6.91 us -> 8.66 us  [call(): pl.pallas_call(body, out_shape=list(outs), in_specs=[given] * len(args),...]
    ppermute x19 -> x14, waiting for transfers between devices: 28.2 us -> 29.4 us  [shift(): return lax.ppermute(x, axis, pairs)]
  transfers between devices with their start and end apart: 21 -> 18, of which waited for: 9 -> 10; matrix products, arithmetic and copies ran while one was open for 0% -> 0% of each run, Pallas kernels for 5% -> 9%
where the time goes in v2:
time: 73.3 us; the launch traced here: 73 us
  waiting for transfers between devices  32.1 us (44%)
  starting transfers between devices  31.5 us (43%)
  Pallas kernels  8.66 us (12%)
  between operations  0.75 us (1%)
    ppermute x14, waiting for transfers between devices, shift(): return lax.ppermute(x, axis, pairs)  29.4 us
    ppermute x14, starting transfers between devices, shift(): return lax.ppermute(x, axis, pairs)  25.1 us
    pallas_call x7, Pallas kernels, call(): pl.pallas_call(body, out_shape=list(outs), in_specs=[given] * len(args),...  8.66 us
    ppermute x1, starting transfers between devices, per_device(): ends = lax.ppermute(to_end, 'seq', [(0, count - 1), (count - 1, 0)])  3.19 us
    ppermute x1, waiting for transfers between devices, per_device(): ends = lax.ppermute(to_end, 'seq', [(0, count - 1), (count - 1, 0)])  2.27 us
  transfers between devices with their start and end apart: 18, of which 10 were waited for; matrix products, arithmetic and copies ran while one was open for 0% of the time, Pallas kernels for 9%

profile of v2, /device:TPU:0, one launch (start us, length us, event | category | flops | bytes accessed | tf_op | source)
XLA Modules:
  0.0 73.0 jit_solution(6884501729401576385)
XLA Ops:
  0.6 1.3 %collective-permute-start.3 = (bf16[4,64,384]{2,1,0:T(8,128)(2,1)}, bf16[4,64,384]{2,1,0:T(8,128)(2,1)S(1)}, u32[]{:S(2)}, u32[]{:S(2)}) collective-permute-start(bf16[4,64,384]{2,1,0:T(8,128)(2,1)} %cot_hbm.1), channel_id=1, source_target_pairs={{4,0},{8,4},{12,8},{5,1},{9,5},{13,9},{6,2},{10,6},{14,10},{7,3},{... | collective-permute-start | bytes 589832 | tf_op jit(solution)/shard_map/ppermute | solution.py:244
  1.9 5.6 %collective-permute-start.2 = (bf16[4,64,384]{2,1,0:T(8,128)(2,1)}, bf16[4,64,384]{2,1,0:T(8,128)(2,1)S(1)}, u32[]{:S(2)}, u32[]{:S(2)}) collective-permute-start(bf16[4,64,384]{2,1,0:T(8,128)(2,1)} %cot_hbm.1), channel_id=1, source_target_pairs={{0,4},{4,8},{8,12},{1,5},{5,9},{9,13},{2,6},{6,10},{10,14},{3,7},{... | collective-permute-start | bytes 589832 | tf_op jit(solution)/shard_map/ppermute | solution.py:244
  7.5 2.1 %prepare.1 = (bf16[3,64,384]{2,1,0:T(8,128)(2,1)S(1)}, bf16[3,64,384]{2,1,0:T(8,128)(2,1)S(1)}, bf16[3,64,384]{2,1,0:T(8,128)(2,1)S(1)}, bf16[3,64,384]{2,1,0:T(...) custom-call(bf16[4,64,384]{2,1,0:T(8,128)(2,1)} %q_hbm.1, ...), custom_call_target="tpu_custom_call" | custom-call | bytes 5849088 | tf_op jit(solution)/shard_map/prepare/pallas_call | solution.py:40
  9.6 3.9 %collective-permute-start.1 = (bf16[3,64,384]{2,1,0:T(8,128)(2,1)S(1)}, bf16[3,64,384]{2,1,0:T(8,128)(2,1)S(1)}, u32[]{:S(2)}, u32[]{:S(2)}) collective-permute-start(bf16[3,64,384]{2,1,0:T(8,128)(2,1)S(1)} %get-tuple-element.48), channel_id=1, source_target_pairs={{0,4},{4,8},{8,12},{1,5},{5,9},{9,13},{2,6},{6,10},{10,14},{3,7},{... | collective-permute-start | bytes 442376 | tf_op jit(solution)/shard_map/ppermute | solution.py:244
  13.6 1.3 %collective-permute-start = (bf16[3,64,384]{2,1,0:T(8,128)(2,1)S(1)}, bf16[3,64,384]{2,1,0:T(8,128)(2,1)S(1)}, u32[]{:S(2)}, u32[]{:S(2)}) collective-permute-start(bf16[3,64,384]{2,1,0:T(8,128)(2,1)S(1)} %get-tuple-element.47), channel_id=1, source_target_pairs={{4,0},{8,4},{12,8},{5,1},{9,5},{13,9},{6,2},{10,6},{14,10},{7,3},{... | collective-permute-start | bytes 442376 | tf_op jit(solution)/shard_map/ppermute | solution.py:244
  14.9 1.3 %collective-permute-done.1.down = bf16[3,64,384]{2,1,0:T(8,128)(2,1)S(1)} collective-permute-done((bf16[3,64,384]{2,1,0:T(8,128)(2,1)S(1)}, bf16[3,64,384]{2,1,0:T(8,128)(2,1)S(1)}, u32[]{:S(2)}, u32[]{:S(2)}) %collective-permute-start.1) | collective-permute-done | bytes 147488 | tf_op jit(solution)/shard_map/ppermute | solution.py:244
  16.2 0.0 collective-permute-done.3.right_ref.refs_2_
  16.2 0.0 collective-permute-done.2.left_ref.refs_1_
  16.2 4.4 %collective-permute-done.up = bf16[3,64,384]{2,1,0:T(8,128)(2,1)S(1)} collective-permute-done((bf16[3,64,384]{2,1,0:T(8,128)(2,1)S(1)}, bf16[3,64,384]{2,1,0:T(8,128)(2,1)S(1)}, u32[]{:S(2)}, u32[]{:S(2)}) %collective-permute-start) | collective-permute-done | bytes 147488 | tf_op jit(solution)/shard_map/ppermute | solution.py:244
  20.6 0.9 %conv_back.1 = (bf16[4,64,384]{2,1,0:T(8,128)(2,1)S(1)}, bf16[8,64,384]{2,1,0:T(8,128)(2,1)S(1)}, bf16[4,64,384]{2,1,0:T(8,128)(2,1)S(1)}, bf16[4,64,384]{2,1,0:T(8,128)(2,1)S(1)}) custom-call(bf16[4,64,384]{2,1,0:T(8,128)(2,1)S(1)} %get-tuple-element.71.cot_ref.refs_0_, bf16[4,64,384]{2,1,0:T(8,128)(2,1)S(1)} %collective-permute-done.2.left_ref.refs_1_, ...), custom_call_target="tpu_custom_call" | custom-call | bytes 3538944 | tf_op jit(solution)/shard_map/conv_back/pallas_call | solution.py:40
  21.6 0.1 collective-permute-start.4
  21.6 1.1 %collective-permute-start.5 = (bf16[3,64,384]{2,1,0:T(8,128)(2,1)S(1)}, bf16[3,64,384]{2,1,0:T(8,128)(2,1)S(1)}, u32[]{:S(2)}, u32[]{:S(2)}) collective-permute-start(bf16[3,64,384]{2,1,0:T(8,128)(2,1)S(1)} %get-tuple-element.58), channel_id=1, source_target_pairs={{0,8},{4,12},{8,0},{12,4},{1,9},{5,13},{9,1},{13,5},{2,10},{6,14},... | collective-permute-start | bytes 442376 | tf_op jit(solution)/shard_map/ppermute | solution.py:244
  22.7 9.2 %collective-permute-done.5.opposite = bf16[3,64,384]{2,1,0:T(8,128)(2,1)S(1)} collective-permute-done((bf16[3,64,384]{2,1,0:T(8,128)(2,1)S(1)}, bf16[3,64,384]{2,1,0:T(8,128)(2,1)S(1)}, u32[]{:S(2)}, u32[]{:S(2)}) %collective-permute-start.5) | collective-permute-done | bytes 147488 | tf_op jit(solution)/shard_map/ppermute | solution.py:244
  32.0 0.0 collective-permute-done.4.other_ref
  32.0 0.4 hidden_grad.1
  32.3 0.7 collective-permute-start.6
  33.0 3.2 %collective-permute-start.7 = (bf16[3,64,384]{2,1,0:T(8,128)(2,1)S(1)}, bf16[3,64,384]{2,1,0:T(8,128)(2,1)S(1)}, u32[]{:S(2)}, u32[]{:S(2)}) collective-permute-start(bf16[3,64,384]{2,1,0:T(8,128)(2,1)S(1)} %get-tuple-element.66), channel_id=1, source_target_pairs={{0,12},{12,0},{1,13},{13,1},{2,14},{14,2},{3,15},{15,3},{16,28},{2... | collective-permute-start | bytes 442376 | tf_op jit(solution)/shard_map/ppermute | solution.py:276
  36.2 0.1 collective-permute-start.8
  36.3 3.1 %collective-permute-start.9 = (bf16[3,64,384]{2,1,0:T(8,128)(2,1)S(1)}, bf16[3,64,384]{2,1,0:T(8,128)(2,1)S(1)}, u32[]{:S(2)}, u32[]{:S(2)}) collective-permute-start(bf16[3,64,384]{2,1,0:T(8,128)(2,1)S(1)} %get-tuple-element.68.refs_8_), channel_id=1, source_target_pairs={{0,8},{4,12},{8,0},{12,4},{1,9},{5,13},{9,1},{13,5},{2,10},{6,14},... | collective-permute-start | bytes 442376 | tf_op jit(solution)/shard_map/ppermute | solution.py:244
  39.4 0.7 collective-permute-start.10
  40.1 0.0 collective-permute-done.6.refs_4_
  40.1 1.3 %collective-permute-start.11 = (bf16[4,64,384]{2,1,0:T(8,128)(2,1)S(1)}, bf16[4,64,384]{2,1,0:T(8,128)(2,1)S(1)}, u32[]{:S(2)}, u32[]{:S(2)}) collective-permute-start(bf16[4,64,384]{2,1,0:T(8,128)(2,1)S(1)} %get-tuple-element.73), channel_id=1, source_target_pairs={{4,0},{8,12},{5,1},{9,13},{6,2},{10,14},{7,3},{11,15},{20,16},{24,... | collective-permute-start | bytes 589832 | tf_op jit(solution)/shard_map/ppermute | solution.py:289
  41.4 2.3 %collective-permute-done.7.ends = bf16[3,64,384]{2,1,0:T(8,128)(2,1)S(1)} collective-permute-done((bf16[3,64,384]{2,1,0:T(8,128)(2,1)S(1)}, bf16[3,64,384]{2,1,0:T(8,128)(2,1)S(1)}, u32[]{:S(2)}, u32[]{:S(2)}) %collective-permute-start.7) | collective-permute-done | bytes 147488 | tf_op jit(solution)/shard_map/ppermute | solution.py:276
  43.7 1.3 %collective-permute-start.12 = (bf16[4,64,384]{2,1,0:T(8,128)(2,1)S(1)}, bf16[4,64,384]{2,1,0:T(8,128)(2,1)S(1)}, u32[]{:S(2)}, u32[]{:S(2)}) collective-permute-start(bf16[4,64,384]{2,1,0:T(8,128)(2,1)S(1)} %collective-permute-done.6.refs_4_), channel_id=1, source_target_pairs={{4,0},{8,12},{5,1},{9,13},{6,2},{10,14},{7,3},{11,15},{20,16},{24,... | collective-permute-start | bytes 589832 | tf_op jit(solution)/shard_map/ppermute | solution.py:291
  44.9 1.8 %collective-permute-done.8.refs_1_.refs_10_ = bf16[3,64,384]{2,1,0:T(8,128)(2,1)S(1)} collective-permute-done((bf16[3,64,384]{2,1,0:T(8,128)(2,1)S(1)}, bf16[3,64,384]{2,1,0:T(8,128)(2,1)S(1)}, u32[]{:S(2)}, u32[]{:S(2)}) %collective-permute-start.8) | collective-permute-done | bytes 147488 | tf_op jit(solution)/shard_map/ppermute | solution.py:244
  46.8 5.0 %collective-permute-done.9.refs_2_.refs_11_ = bf16[3,64,384]{2,1,0:T(8,128)(2,1)S(1)} collective-permute-done((bf16[3,64,384]{2,1,0:T(8,128)(2,1)S(1)}, bf16[3,64,384]{2,1,0:T(8,128)(2,1)S(1)}, u32[]{:S(2)}, u32[]{:S(2)}) %collective-permute-start.9) | collective-permute-done | bytes 147488 | tf_op jit(solution)/shard_map/ppermute | solution.py:244
  51.8 0.0 collective-permute-done.10.refs_3_.refs_12_
  51.8 2.0 %attention.1 = (bf16[3,64,384]{2,1,0:T(8,128)(2,1)S(1)}, bf16[3,64,384]{2,1,0:T(8,128)(2,1)S(1)}, bf16[3,64,384]{2,1,0:T(8,128)(2,1)S(1)}, bf16[3,64,384]{2,1,0:T(8,128)(2,1)S(1)}) custom-call(bf16[3,64,384]{2,1,0:T(8,128)(2,1)S(1)} %get-tuple-element.65.own, bf16[3,64,384]{2,1,0:T(8,128)(2,1)S(1)} %collective-permute-done.1.down, ...), custom_call_target="tpu_custom_call" | custom-call | flops 2013265920 | bytes 1916928 | tf_op jit(solution)/shard_map/attention/pallas_call | solution.py:40
  53.8 5.3 %collective-permute-start.15 = (bf16[3,64,384]{2,1,0:T(8,128)(2,1)S(1)}, bf16[3,64,384]{2,1,0:T(8,128)(2,1)S(1)}, u32[]{:S(2)}, u32[]{:S(2)}) collective-permute-start(bf16[3,64,384]{2,1,0:T(8,128)(2,1)S(1)} %get-tuple-element.78), channel_id=1, source_target_pairs={{0,12},{4,0},{8,4},{12,8},{1,13},{5,1},{9,5},{13,9},{2,14},{6,2},{... | collective-permute-start | bytes 442376 | tf_op jit(solution)/shard_map/ppermute | solution.py:244
  59.1 0.0 collective-permute-start.16
  59.1 0.6 collective-permute-start.17
  59.7 0.0 collective-permute-done.11.refs_3_
  59.7 0.4 collective-permute-done.12.refs_5_
  60.1 1.5 %weight_grad.1 = (f32[3,96,384]{2,1,0:T(8,128)S(1)}, bf16[3,48,384]{2,1,0:T(8,128)(2,1)S(1)}, bf16[3,48,384]{2,1,0:T(8,128)(2,1)S(1)}, bf16[4,64,384]{2,1,0:T(8,128)(2,1)}) custom-call(bf16[4,64,384]{2,1,0:T(8,128)(2,1)S(1)} %get-tuple-element.71.cot_ref.refs_0_, bf16[4,64,384]{2,1,0:T(8,128)(2,1)S(1)} %collective-permute-done.2.left_ref.refs_1_, ...), custom_call_target="tpu_custom_call" | custom-call | bytes 3072000 | tf_op jit(solution)/shard_map/weight_grad/pallas_call | solution.py:40
  61.7 1.5 %collective-permute-start.13 = (bf16[3,48,384]{2,1,0:T(8,128)(2,1)S(1)}, bf16[3,48,384]{2,1,0:T(8,128)(2,1)S(1)}, u32[]{:S(2)}, u32[]{:S(2)}) collective-permute-start(bf16[3,48,384]{2,1,0:T(8,128)(2,1)S(1)} %get-tuple-element.75), channel_id=1, source_target_pairs={{0,2},{2,0},{1,3},{3,1},{4,6},{6,4},{5,7},{7,5},{8,10},{10,8},{9,1... | collective-permute-start | bytes 331784 | tf_op jit(solution)/shard_map/ppermute | solution.py:244
  63.2 0.5 collective-permute-start.14
  63.7 3.9 %collective-permute-done.13.got0_ref = bf16[3,48,384]{2,1,0:T(8,128)(2,1)S(1)} collective-permute-done((bf16[3,48,384]{2,1,0:T(8,128)(2,1)S(1)}, bf16[3,48,384]{2,1,0:T(8,128)(2,1)S(1)}, u32[]{:S(2)}, u32[]{:S(2)}) %collective-permute-start.13) | collective-permute-done | bytes 110624 | tf_op jit(solution)/shard_map/ppermute | solution.py:244
  67.6 1.3 %collective-permute-done.14.got1_ref = bf16[3,48,384]{2,1,0:T(8,128)(2,1)S(1)} collective-permute-done((bf16[3,48,384]{2,1,0:T(8,128)(2,1)S(1)}, bf16[3,48,384]{2,1,0:T(8,128)(2,1)S(1)}, u32[]{:S(2)}, u32[]{:S(2)}) %collective-permute-start.14) | collective-permute-done | bytes 110624 | tf_op jit(solution)/shard_map/ppermute | solution.py:244
  68.9 0.8 %add_weight.1 = f32[3,96,384]{2,1,0:T(8,128)} custom-call(f32[3,96,384]{2,1,0:T(8,128)S(1)} %get-tuple-element.74.own_ref, bf16[3,48,384]{2,1,0:T(8,128)(2,1)S(1)} %collective-permute-done.13.got0_ref, bf16[3,48,384]{2,1,0:T(8,128)(2,1)S(1)} %collective-permute-done.14.got1_ref), custom_call_target="tpu_custom_call" | custom-call | bytes 1105920 | tf_op jit(solution)/shard_map/add_weight/pallas_call | solution.py:40
  69.7 0.0 collective-permute-done.15.refs_1_
  69.7 2.4 %collective-permute-done.16.refs_2_ = bf16[3,64,384]{2,1,0:T(8,128)(2,1)S(1)} collective-permute-done((bf16[3,64,384]{2,1,0:T(8,128)(2,1)S(1)}, bf16[3,64,384]{2,1,0:T(8,128)(2,1)S(1)}, u32[]{:S(2)}, u32[]{:S(2)}) %collective-permute-start.16) | collective-permute-done | bytes 147488 | tf_op jit(solution)/shard_map/ppermute | solution.py:244
  72.1 0.0 collective-permute-done.17.refs_3_
  72.1 0.9 %place.1 = (bf16[4,64,384]{2,1,0:T(8,128)(2,1)}, bf16[4,64,384]{2,1,0:T(8,128)(2,1)}, bf16[4,64,384]{2,1,0:T(8,128)(2,1)}) custom-call(bf16[3,64,384]{2,1,0:T(8,128)(2,1)S(1)} %get-tuple-element.77.refs_0_, bf16[3,64,384]{2,1,0:T(8,128)(2,1)S(1)} %collective-permute-done.15.refs_1_, bf16[3,64,384]{2,1,0:T(8,128)(2,1)S(1)} %collective-permute-done.16.refs_2_, ...), custom_call_target="tpu_custom_call" | custom-call | bytes 1179648 | tf_op jit(solution)/shard_map/place/pallas_call | solution.py:40
Async XLA Ops:
  0.6 15.6 %collective-permute-start.3 = (bf16[4,64,384]{2,1,0:T(8,128)(2,1)}, bf16[4,64,384]{2,1,0:T(8,128)(2,1)S(1)}, u32[]{:S(2)}, u32[]{:S(2)}) collective-permute-start(bf16[4,64,384]{2,1,0:T(8,128)(2,1)} %cot_hbm.1), channel_id=1, source_target_pairs={{4,0},{8,4},{12,8},{5,1},{9,5},{13,9},{6,2},{10,6},{14,10},{7,3},{... | collective-permute-start | bytes 589832 | tf_op jit(solution)/shard_map/ppermute | solution.py:244
  1.9 14.3 %collective-permute-start.2 = (bf16[4,64,384]{2,1,0:T(8,128)(2,1)}, bf16[4,64,384]{2,1,0:T(8,128)(2,1)S(1)}, u32[]{:S(2)}, u32[]{:S(2)}) collective-permute-start(bf16[4,64,384]{2,1,0:T(8,128)(2,1)} %cot_hbm.1), channel_id=1, source_target_pairs={{0,4},{4,8},{8,12},{1,5},{5,9},{9,13},{2,6},{6,10},{10,14},{3,7},{... | collective-permute-start | bytes 589832 | tf_op jit(solution)/shard_map/ppermute | solution.py:244
  9.6 6.6 %collective-permute-start.1 = (bf16[3,64,384]{2,1,0:T(8,128)(2,1)S(1)}, bf16[3,64,384]{2,1,0:T(8,128)(2,1)S(1)}, u32[]{:S(2)}, u32[]{:S(2)}) collective-permute-start(bf16[3,64,384]{2,1,0:T(8,128)(2,1)S(1)} %get-tuple-element.48), channel_id=1, source_target_pairs={{0,4},{4,8},{8,12},{1,5},{5,9},{9,13},{2,6},{6,10},{10,14},{3,7},{... | collective-permute-start | bytes 442376 | tf_op jit(solution)/shard_map/ppermute | solution.py:244
  13.6 7.0 %collective-permute-start = (bf16[3,64,384]{2,1,0:T(8,128)(2,1)S(1)}, bf16[3,64,384]{2,1,0:T(8,128)(2,1)S(1)}, u32[]{:S(2)}, u32[]{:S(2)}) collective-permute-start(bf16[3,64,384]{2,1,0:T(8,128)(2,1)S(1)} %get-tuple-element.47), channel_id=1, source_target_pairs={{4,0},{8,4},{12,8},{5,1},{9,5},{13,9},{6,2},{10,6},{14,10},{7,3},{... | collective-permute-start | bytes 442376 | tf_op jit(solution)/shard_map/ppermute | solution.py:244
  21.6 10.4 %collective-permute-start.4 = (bf16[8,64,384]{2,1,0:T(8,128)(2,1)S(1)}, bf16[8,64,384]{2,1,0:T(8,128)(2,1)S(1)}, u32[]{:S(2)}, u32[]{:S(2)}) collective-permute-start(bf16[8,64,384]{2,1,0:T(8,128)(2,1)S(1)} %get-tuple-element.56), channel_id=1, source_target_pairs={{0,1},{1,0},{2,3},{3,2},{4,5},{5,4},{6,7},{7,6},{8,9},{9,8},{10,11... | collective-permute-start | bytes 1179656 | tf_op jit(solution)/shard_map/ppermute | solution.py:244
  21.6 10.3 %collective-permute-start.5 = (bf16[3,64,384]{2,1,0:T(8,128)(2,1)S(1)}, bf16[3,64,384]{2,1,0:T(8,128)(2,1)S(1)}, u32[]{:S(2)}, u32[]{:S(2)}) collective-permute-start(bf16[3,64,384]{2,1,0:T(8,128)(2,1)S(1)} %get-tuple-element.58), channel_id=1, source_target_pairs={{0,8},{4,12},{8,0},{12,4},{1,9},{5,13},{9,1},{13,5},{2,10},{6,14},... | collective-permute-start | bytes 442376 | tf_op jit(solution)/shard_map/ppermute | solution.py:244
  32.3 7.8 %collective-permute-start.6 = (bf16[4,64,384]{2,1,0:T(8,128)(2,1)S(1)}, bf16[4,64,384]{2,1,0:T(8,128)(2,1)S(1)}, u32[]{:S(2)}, u32[]{:S(2)}) collective-permute-start(bf16[4,64,384]{2,1,0:T(8,128)(2,1)S(1)} %get-tuple-element.63), channel_id=1, source_target_pairs={{4,8},{8,4},{5,9},{9,5},{6,10},{10,6},{7,11},{11,7},{20,24},{24,20... | collective-permute-start | bytes 589832 | tf_op jit(solution)/shard_map/ppermute | solution.py:290
  33.0 10.6 %collective-permute-start.7 = (bf16[3,64,384]{2,1,0:T(8,128)(2,1)S(1)}, bf16[3,64,384]{2,1,0:T(8,128)(2,1)S(1)}, u32[]{:S(2)}, u32[]{:S(2)}) collective-permute-start(bf16[3,64,384]{2,1,0:T(8,128)(2,1)S(1)} %get-tuple-element.66), channel_id=1, source_target_pairs={{0,12},{12,0},{1,13},{13,1},{2,14},{14,2},{3,15},{15,3},{16,28},{2... | collective-permute-start | bytes 442376 | tf_op jit(solution)/shard_map/ppermute | solution.py:276
  36.2 10.6 %collective-permute-start.8 = (bf16[3,64,384]{2,1,0:T(8,128)(2,1)S(1)}, bf16[3,64,384]{2,1,0:T(8,128)(2,1)S(1)}, u32[]{:S(2)}, u32[]{:S(2)}) collective-permute-start(bf16[3,64,384]{2,1,0:T(8,128)(2,1)S(1)} %get-tuple-element.67.refs_7_), channel_id=1, source_target_pairs={{0,4},{4,8},{8,12},{12,0},{1,5},{5,9},{9,13},{13,1},{2,6},{6,10},{... | collective-permute-start | bytes 442376 | tf_op jit(solution)/shard_map/ppermute | solution.py:244
  36.3 15.5 %collective-permute-start.9 = (bf16[3,64,384]{2,1,0:T(8,128)(2,1)S(1)}, bf16[3,64,384]{2,1,0:T(8,128)(2,1)S(1)}, u32[]{:S(2)}, u32[]{:S(2)}) collective-permute-start(bf16[3,64,384]{2,1,0:T(8,128)(2,1)S(1)} %get-tuple-element.68.refs_8_), channel_id=1, source_target_pairs={{0,8},{4,12},{8,0},{12,4},{1,9},{5,13},{9,1},{13,5},{2,10},{6,14},... | collective-permute-start | bytes 442376 | tf_op jit(solution)/shard_map/ppermute | solution.py:244
  39.4 12.4 %collective-permute-start.10 = (bf16[3,64,384]{2,1,0:T(8,128)(2,1)S(1)}, bf16[3,64,384]{2,1,0:T(8,128)(2,1)S(1)}, u32[]{:S(2)}, u32[]{:S(2)}) collective-permute-start(bf16[3,64,384]{2,1,0:T(8,128)(2,1)S(1)} %get-tuple-element.69.refs_9_), channel_id=1, source_target_pairs={{0,12},{4,0},{8,4},{12,8},{1,13},{5,1},{9,5},{13,9},{2,14},{6,2},{... | collective-permute-start | bytes 442376 | tf_op jit(solution)/shard_map/ppermute | solution.py:244
  40.1 19.6 %collective-permute-start.11 = (bf16[4,64,384]{2,1,0:T(8,128)(2,1)S(1)}, bf16[4,64,384]{2,1,0:T(8,128)(2,1)S(1)}, u32[]{:S(2)}, u32[]{:S(2)}) collective-permute-start(bf16[4,64,384]{2,1,0:T(8,128)(2,1)S(1)} %get-tuple-element.73), channel_id=1, source_target_pairs={{4,0},{8,12},{5,1},{9,13},{6,2},{10,14},{7,3},{11,15},{20,16},{24,... | collective-permute-start | bytes 589832 | tf_op jit(solution)/shard_map/ppermute | solution.py:289
  43.7 16.5 %collective-permute-start.12 = (bf16[4,64,384]{2,1,0:T(8,128)(2,1)S(1)}, bf16[4,64,384]{2,1,0:T(8,128)(2,1)S(1)}, u32[]{:S(2)}, u32[]{:S(2)}) collective-permute-start(bf16[4,64,384]{2,1,0:T(8,128)(2,1)S(1)} %collective-permute-done.6.refs_4_), channel_id=1, source_target_pairs={{4,0},{8,12},{5,1},{9,13},{6,2},{10,14},{7,3},{11,15},{20,16},{24,... | collective-permute-start | bytes 589832 | tf_op jit(solution)/shard_map/ppermute | solution.py:291
  53.8 16.0 %collective-permute-start.15 = (bf16[3,64,384]{2,1,0:T(8,128)(2,1)S(1)}, bf16[3,64,384]{2,1,0:T(8,128)(2,1)S(1)}, u32[]{:S(2)}, u32[]{:S(2)}) collective-permute-start(bf16[3,64,384]{2,1,0:T(8,128)(2,1)S(1)} %get-tuple-element.78), channel_id=1, source_target_pairs={{0,12},{4,0},{8,4},{12,8},{1,13},{5,1},{9,5},{13,9},{2,14},{6,2},{... | collective-permute-start | bytes 442376 | tf_op jit(solution)/shard_map/ppermute | solution.py:244
  59.1 13.1 %collective-permute-start.16 = (bf16[3,64,384]{2,1,0:T(8,128)(2,1)S(1)}, bf16[3,64,384]{2,1,0:T(8,128)(2,1)S(1)}, u32[]{:S(2)}, u32[]{:S(2)}) collective-permute-start(bf16[3,64,384]{2,1,0:T(8,128)(2,1)S(1)} %get-tuple-element.79), channel_id=1, source_target_pairs={{0,8},{4,12},{8,0},{12,4},{1,9},{5,13},{9,1},{13,5},{2,10},{6,14},... | collective-permute-start | bytes 442376 | tf_op jit(solution)/shard_map/ppermute | solution.py:244
  59.1 13.1 %collective-permute-start.17 = (bf16[3,64,384]{2,1,0:T(8,128)(2,1)S(1)}, bf16[3,64,384]{2,1,0:T(8,128)(2,1)S(1)}, u32[]{:S(2)}, u32[]{:S(2)}) collective-permute-start(bf16[3,64,384]{2,1,0:T(8,128)(2,1)S(1)} %get-tuple-element.80), channel_id=1, source_target_pairs={{0,4},{4,8},{8,12},{12,0},{1,5},{5,9},{9,13},{13,1},{2,6},{6,10},{... | collective-permute-start | bytes 442376 | tf_op jit(solution)/shard_map/ppermute | solution.py:244
  61.7 5.9 %collective-permute-start.13 = (bf16[3,48,384]{2,1,0:T(8,128)(2,1)S(1)}, bf16[3,48,384]{2,1,0:T(8,128)(2,1)S(1)}, u32[]{:S(2)}, u32[]{:S(2)}) collective-permute-start(bf16[3,48,384]{2,1,0:T(8,128)(2,1)S(1)} %get-tuple-element.75), channel_id=1, source_target_pairs={{0,2},{2,0},{1,3},{3,1},{4,6},{6,4},{5,7},{7,5},{8,10},{10,8},{9,1... | collective-permute-start | bytes 331784 | tf_op jit(solution)/shard_map/ppermute | solution.py:244
  63.2 5.8 %collective-permute-start.14 = (bf16[3,48,384]{2,1,0:T(8,128)(2,1)S(1)}, bf16[3,48,384]{2,1,0:T(8,128)(2,1)S(1)}, u32[]{:S(2)}, u32[]{:S(2)}) collective-permute-start(bf16[3,48,384]{2,1,0:T(8,128)(2,1)S(1)} %get-tuple-element.76), channel_id=1, source_target_pairs={{0,2},{2,0},{1,3},{3,1},{4,6},{6,4},{5,7},{7,5},{8,10},{10,8},{9,1... | collective-permute-start | bytes 331784 | tf_op jit(solution)/shard_map/ppermute | solution.py:244

commit v3 on v2

--- a/solution.py
+++ b/solution.py
@@ -57,21 +57,32 @@
     return jax.ShapeDtypeStruct(dims, dtype)
 
 
-def prepare_kernel(count, q_hbm, k_hbm, v_hbm, h_hbm, cot_hbm, w_hbm, *refs):
-    outs, (act_ref, h_ref, cot_ref, w_ref, sems) = refs[: count + 1], refs[count + 1 :]
-    s = lax.axis_index("seq")
-    near = [pltpu.make_async_copy(h_hbm, h_ref, sems.at[0])]
-    for d in range(count + 1):
-        b = lax.rem(s + d, count) if d < count else count - 1 - s
-        for j, ref in enumerate((q_hbm, k_hbm, v_hbm)):
-            near.append(
-                pltpu.make_async_copy(ref.at[b], outs[d].at[j], sems.at[1 + 3 * d + j])
-            )
-    near.append(pltpu.make_async_copy(cot_hbm, cot_ref, sems.at[4 + 3 * count]))
-    near.append(pltpu.make_async_copy(w_hbm, w_ref, sems.at[5 + 3 * count]))
-    for copy in near:
+def fetch(pairs, sems):
+    copies = [pltpu.make_async_copy(src, dst, sems.at[i]) for i, (src, dst) in enumerate(pairs)]
+    for copy in copies:
         copy.start()
-    near[0].wait()
+    return copies
+
+
+def near_kernel(count, cot, q, k, v, down, up, sems):
+    s = lax.axis_index("seq")
+    blocks = cot.shape[0]
+    pairs = []
+    for out, d in ((down, 1), (up, count - 1)):
+        pairs.append((cot, out.at[pl.ds(0, blocks)]))
+        pairs += [(x.at[lax.rem(s + d, count)], out.at[blocks + j]) for j, x in enumerate((q, k, v))]
+    for copy in fetch(pairs, sems):
+        copy.wait()
+
+
+def rest_kernel(count, hidden, q, k, v, w, h_ref, own, opposite, end, w_ref, act_ref, sems):
+    s = lax.axis_index("seq")
+    pairs = [(hidden, h_ref)]
+    for out, b in ((own, s), (opposite, lax.rem(s + 2, count)), (end, count - 1 - s)):
+        pairs += [(x.at[b], out.at[j]) for j, x in enumerate((q, k, v))]
+    pairs.append((w, w_ref))
+    copies = fetch(pairs, sems)
+    copies[0].wait()
     blocks, rows, width = h_ref.shape
     act = tanh_gelu(h_ref[...].astype(F32)).reshape(blocks * rows, width)
     act_t = act.T.astype(BF)
@@ -82,19 +93,14 @@
             act_ref[i // parts * 2 + h, :, pl.ds(i % parts * lanes, lanes)] = act_t[
                 i * rows : (i + 1) * rows, h * lanes : (h + 1) * lanes
             ]
-    for copy in near[1:]:
+    for copy in copies[1:]:
         copy.wait()
 
 
-def conv_kernel(
-    cot_ref, left_ref, right_ref, w_ref, act_ref, mine_ref, other_ref, inner_ref, outer_ref
-):
-    first = lax.axis_index("seq") < 2
-    inner_ref[...] = jnp.where(first, right_ref[...], left_ref[...])
-    outer_ref[...] = jnp.where(first, left_ref[...], right_ref[...])
+def conv_kernel(cot_ref, down_ref, up_ref, w_ref, act_ref, mine_ref, other_ref):
     c = lax.axis_index("chan")
-    blocks, rows, width = cot_ref.shape
-    taps = [r[...].reshape(blocks * rows, width) for r in (right_ref, cot_ref, left_ref)]
+    blocks, rows, width = mine_ref.shape
+    taps = [r[:blocks].reshape(blocks * rows, width) for r in (up_ref, cot_ref, down_ref)]
     for out_ref, side in ((other_ref, 1 - c), (mine_ref, c)):
         start = pl.multiple_of(side * width, width)
         total = None
@@ -107,37 +113,68 @@
             )
             total = term if total is None else total + term
         out_ref[:blocks] = total.astype(BF).reshape(blocks, rows, width)
-    other_ref[blocks:] = act_ref[...]
-
-
-def grad_kernel(count, cot_ref, h_ref, mine_ref, other_ref, act_ref, *pieces):
+    for k in range(2):
+        other_ref[blocks + k] = act_ref[2 * k + 1 - c]
+
+
+def grad_kernel(
+    count, cot_ref, h_ref, mine_ref, got_ref, act_ref, down_ref, up_ref, end_qkv,
+    own, down, opposite, up, end,
+):
     s = lax.axis_index("seq")
     c = lax.axis_index("chan")
-    blocks = cot_ref.shape[0]
+    blocks = h_ref.shape[0]
+
+    def sequence(b):
+        back = mine_ref[b].astype(F32) + got_ref[b].astype(F32)
+        slope = gelu_slope(h_ref[b].astype(F32))
+        grad = (cot_ref[b].astype(F32) + back * slope).astype(BF)
+        k = lax.rem(b, 2)
+        act = jnp.where(lax.div(b, 2) == c, act_ref[2 * k + c], got_ref[blocks + k])
+        return grad, act
+
+    for d, out in ((0, own), (1, down), (2, opposite), (3, up)):
+        out[0], out[1] = sequence(lax.rem(s + d, count))
+    end[:3] = end_qkv[...]
+    first = s == 0
+    end[3] = jnp.where(first, up[0], down[0])
+    end[4] = jnp.where(first, up[1], down[1])
+    down[2:] = down_ref[:blocks]
+    up[2:] = up_ref[:blocks]
+
+
+def pick_kernel(down_ref, up_ref, out_ref):
+    out_ref[...] = jnp.where(lax.axis_index("seq") < 2, up_ref[2:], down_ref[2:])
+
+
+def attention_kernel(
+    count, own_qkv, own, down_qkv, up_qkv, opposite_qkv, end, down, up, opposite, *outs
+):
+    outs, act_ref = outs[:count], outs[count]
+    rows, width = own.shape[1:]
+    near = down_qkv.shape[0] - 3
+    scale = 1.0 / math.sqrt(HD)
+    s = lax.axis_index("seq")
+    at_first, at_last = s == 0, s == count - 1
+
+    def positions(j):
+        before = jnp.where(at_first, end[j], down_qkv[near + j])
+        behind = jnp.where(at_last, end[j], up_qkv[near + j])
+        return jnp.concatenate([own_qkv[j], before, opposite_qkv[j], behind], axis=0)
+
+    query, key, value = (positions(j) for j in range(3))
+    grad, act = (
+        (
+            own[j],
+            jnp.where(at_first, end[3 + j], down[j]),
+            opposite[j],
+            jnp.where(at_last, end[3 + j], up[j]),
+        )
+        for j in range(2)
+    )
+    grad = jnp.concatenate(grad, axis=0)
     for d in range(count):
-        b = lax.rem(s + d, count)
-        back = mine_ref[b].astype(F32) + other_ref[b].astype(F32)
-        slope = gelu_slope(h_ref[b].astype(F32))
-        pieces[d][0] = (cot_ref[b].astype(F32) + back * slope).astype(BF)
-        here = lax.div(b, 2) == c
-        for h in range(2):
-            k = 2 * lax.rem(b, 2) + h
-            pieces[d][1 + h] = jnp.where(here, act_ref[k], other_ref[blocks + k])
-
-
-def attention_kernel(count, own, down, opposite, up, ends, *refs):
-    grads, outs = refs[:count], refs[count:]
-    _, rows, width = grads[0].shape
-    scale = 1.0 / math.sqrt(HD)
-    s = lax.axis_index("seq")
-
-    def positions(j):
-        before = jnp.where(s == 0, ends[j], down[j])
-        behind = jnp.where(s == count - 1, ends[j], up[j])
-        return jnp.concatenate([own[j], before, opposite[j], behind], axis=0)
-
-    query, key, value = (positions(j) for j in range(3))
-    grad = jnp.concatenate([grads[d][0] for d in range(count)], axis=0)
+        act_ref[d] = act[d]
     nt = (((1,), (1,)), ((), ()))
     nn = (((1,), (0,)), ((), ()))
     tn = (((0,), (0,)), ((), ()))
@@ -161,45 +198,41 @@
             outs[d][j] = whole[d * rows : (d + 1) * rows]
 
 
-def weight_kernel(count, factor, *refs):
-    cots, grads, got = refs[:6], refs[6 : 6 + count], (refs[6], *refs[6 + count : 5 + 2 * count])
-    own_ref, sent0_ref, sent1_ref, grad_ref, act_buf, cot_buf = refs[5 + 2 * count :]
-    s = lax.axis_index("seq")
+def weight_kernel(
+    count, factor, cot_ref, down, up, down2, up2, farthest, act_ref, act_peer, own, to_down,
+    to_opposite, to_up, own_ref, sent0_ref, sent1_ref, grad_ref, act_buf, cot_buf,
+):
+    s = lax.axis_index("seq")
+    c = lax.axis_index("chan")
     b = lax.axis_index("batch")
-    _, rows, width = got[0].shape
+    blocks, rows, width = grad_ref.shape
+    for d, piece in enumerate((own, to_down, to_opposite, to_up)):
+        grad_ref[lax.rem(s + d, count)] = piece[0]
     lanes = act_buf.shape[2] // 2
     for d in range(count):
         j = lax.rem(s - d + count, count)
+        halves = (
+            jnp.where(c == 0, act_ref[d], act_peer[d]),
+            jnp.where(c == 0, act_peer[d], act_ref[d]),
+        )
         for r in range(width // lanes):
             for h in range(2):
-                act_buf[j, pl.ds(r * rows, rows), pl.ds(h * lanes, lanes)] = got[d][
-                    1 + h, :, pl.ds(r * lanes, lanes)
+                act_buf[j, pl.ds(r * rows, rows), pl.ds(h * lanes, lanes)] = halves[h][
+                    :, r * lanes : (r + 1) * lanes
                 ]
-    own_cot, left, right, far, across, farthest = cots
     flat = cot_buf.shape[1:]
-    cot_buf[s] = own_cot[...].reshape(flat)
-
-    @pl.when(s > 0)
-    def _():
-        cot_buf[s - 1] = left[...].reshape(flat)
-
-    @pl.when(s < count - 1)
-    def _():
-        cot_buf[s + 1] = right[...].reshape(flat)
-
-    low = s < 2
-
-    @pl.when(jnp.logical_or(s == 0, s == 3))
-    def _():
-        cot_buf[jnp.where(low, 2, 1)] = far[...].reshape(flat)
-        cot_buf[jnp.where(low, 3, 0)] = farthest[...].reshape(flat)
-
-    @pl.when(jnp.logical_or(s == 1, s == 2))
-    def _():
-        cot_buf[jnp.where(low, 3, 0)] = across[...].reshape(flat)
-
-    for d in range(count):
-        grad_ref[lax.rem(s + d, count)] = grads[d][0]
+
+    def put(position, holds, value):
+        @pl.when(holds)
+        def _():
+            cot_buf[position] = value().reshape(flat)
+
+    cot_buf[s] = cot_ref[:blocks].reshape(flat)
+    put(s - 1, s > 0, lambda: down[:blocks])
+    put(s + 1, s < count - 1, lambda: up[:blocks])
+    put(s - 2, s >= 2, lambda: down2[2:])
+    put(s + 2, s < 2, lambda: up2[2:])
+    put(count - 1 - s, jnp.logical_or(s == 0, s == count - 1), lambda: farthest[...])
 
     half = own_ref.shape[1]
     for t in range(3):
@@ -255,68 +288,81 @@
     tokens = blocks * rows
     factor = 1.0 / math.sqrt(tokens * count * lax.axis_size("batch"))
     weights = conv_weight.transpose(1, 0, 2)
-    piece = shape((rows, width))
-    piece3 = shape((3, rows, width))
-    full = shape((blocks, rows, width))
     part = width // 2
 
-    left = shift(cotangent, "seq", 1, False)
-    right = shift(cotangent, "seq", -1, False)
-    own_qkv, to_down, to_opposite, to_up, to_end, act, hidden, own_cot, weights = kernel_call(
-        functools.partial(prepare_kernel, count),
-        [piece3] * (count + 1) + [full] * 3 + [shape(weights.shape)],
-        name="prepare",
-        scratch=[pltpu.SemaphoreType.DMA((3 * count + 6,))],
+    def units(n):
+        return shape((n, rows, width))
+
+    def along(x, by):
+        return shift(x, "seq", by, False)
+
+    def between_ends(x):
+        return lax.ppermute(x, "seq", [(0, count - 1), (count - 1, 0)])
+
+    to_down, to_up = kernel_call(
+        functools.partial(near_kernel, count),
+        [units(blocks + 3)] * 2,
+        name="near",
+        scratch=[pltpu.SemaphoreType.DMA((8,))],
         space=pltpu.HBM,
-    )(query_vectors, key_vectors, value_vectors, hidden, cotangent, weights)
-
-    down = shift(to_down, "seq", 1, False)
-    up = shift(to_up, "seq", -1, False)
+    )(cotangent, query_vectors, key_vectors, value_vectors)
+    down, up = along(to_down, 1), along(to_up, -1)
+    (hidden,) = after(to_down, hidden)
+    hidden, own_qkv, to_opposite, to_end, weights, act = kernel_call(
+        functools.partial(rest_kernel, count),
+        [units(blocks), units(3), units(3), units(3), shape(weights.shape), units(blocks)],
+        name="rest",
+        scratch=[pltpu.SemaphoreType.DMA((11,))],
+        space=pltpu.HBM,
+    )(hidden, query_vectors, key_vectors, value_vectors, weights)
     opposite = shift(to_opposite, "seq", 2, True)
-    ends = lax.ppermute(to_end, "seq", [(0, count - 1), (count - 1, 0)])
-    near_left, right = after(down, left, right)
-    near_left, right = after(up, near_left, right)
-    mine, other, inner, outer = kernel_call(
-        conv_kernel, [full, shape((2 * blocks, rows, width)), full, full], name="conv_back"
-    )(own_cot, near_left, right, weights, act)
+
+    mine, other = kernel_call(conv_kernel, [units(blocks), units(blocks + 2)], name="conv_back")(
+        to_down, down, up, weights, act
+    )
     got = shift(other, "chan", 1, True)
-    grads = kernel_call(
-        functools.partial(grad_kernel, count), [piece3] * count, name="hidden_grad"
-    )(own_cot, hidden, mine, got, act)
-    got_grads = [grads[0]] + [shift(grads[d], "seq", d, True) for d in range(1, count)]
-
-    inner, outer = after(grads[0], *after(opposite, inner, outer))
-    far = lax.ppermute(inner, "seq", [(1, 0), (2, 3)])
-    across = lax.ppermute(outer, "seq", [(1, 2), (2, 1)])
-    farthest = lax.ppermute(across, "seq", [(1, 0), (2, 3)])
-    (own_qkv,) = after(across, own_qkv)
+    own, to_down2, to_opposite2, to_up2, to_end2 = kernel_call(
+        functools.partial(grad_kernel, count),
+        [units(2), units(blocks + 2), units(2), units(blocks + 2), units(5)],
+        name="hidden_grad",
+    )(to_down, hidden, mine, got, act, down, up, to_end)
+    down2, up2 = along(to_down2, 1), along(to_up2, -1)
+    far_opposite, far_end = after(opposite, to_opposite2, to_end2)
+    opposite2 = shift(far_opposite, "seq", 2, True)
+    end2 = between_ends(far_end)
+    (far,) = kernel_call(pick_kernel, [units(blocks)], name="pick")(down2, up2)
+    farthest = lax.ppermute(far, "seq", [(1, 0), (2, 3)])
+
     item = 5 * (count * rows) ** 2 * width
-    returned = kernel_call(
+    *returned, act_held = kernel_call(
         functools.partial(attention_kernel, count),
-        [piece3] * count,
+        [units(3)] * count + [units(count)],
         flops=COST * 2 * item,
         transcendentals=(count * rows) ** 2 * (width // HD),
         name="attention",
-    )(own_qkv, down, opposite, up, ends, *got_grads)
+    )(own_qkv, own, down, up, opposite, end2, down2, up2, opposite2)
     back = [returned[0]] + [shift(returned[d], "seq", -d, True) for d in range(1, count)]
 
-    own_cot, near_left = after(returned[0], own_cot, near_left)
-    own, sent0, sent1, hidden_grad = kernel_call(
+    act_peer = shift(act_held, "chan", 1, True)
+    total, sent0, sent1, hidden_grad = kernel_call(
         functools.partial(weight_kernel, count, factor),
-        [shape((3, part // 2, width), F32)] + [shape((3, part // 4, width))] * 2 + [full],
+        [shape((3, part // 2, width), F32)] + [shape((3, part // 4, width))] * 2 + [units(blocks)],
         name="weight_grad",
         scratch=[
             pltpu.VMEM((count, part, tokens), BF),
             pltpu.VMEM((count, tokens, width), BF),
         ],
-    )(own_cot, near_left, right, far, across, farthest, *grads, *got_grads[1:])
+    )(
+        to_down, down, up, down2, up2, farthest, act_held, act_peer, own, to_down2, to_opposite2,
+        to_up2,
+    )
     got_sums = [shift(x, "batch", 1, True) for x in (sent0, sent1)]
     (weight_grad,) = kernel_call(add_kernel, [shape((3, part // 2, width), F32)], name="add_weight")(
-        own, *got_sums
+        total, *got_sums
     )
     (back[0],) = after(weight_grad, back[0])
     query_grad, key_grad, value_grad = kernel_call(
-        functools.partial(place_kernel, count), [full] * 3, name="place"
+        functools.partial(place_kernel, count), [units(blocks)] * 3, name="place"
     )(*back)
     return (query_grad, key_grad, value_grad, hidden_grad, weight_grad.transpose(1, 0, 2))
 

time: 73.3 us -> 64.2 us (0.88)
  waiting for transfers between devices: 32.1 us -> 26.2 us
  starting transfers between devices: 31.5 us -> 27.3 us
  Pallas kernels: 8.66 us -> 9.66 us
    ppermute x14 -> x13, starting transfers between devices: 25.1 us -> 20.4 us  [shift(): return lax.ppermute(x, axis, pairs)]
    ppermute x14 -> x13, waiting for transfers between devices: 29.4 us -> 26.2 us  [shift(): return lax.ppermute(x, axis, pairs)]
    ppermute x4 -> x2, waiting for transfers between devices: 2.66 us -> 0.01 us  [the longest x1 0.01 us: between_ends(): return lax.ppermute(x, 'seq', [(0, count - 1), (count - 1, 0)])]
    pallas_call x7 -> x9, Pallas kernels: 8.66 us -> 9.66 us  [call(): pl.pallas_call(body, out_shape=list(outs), in_specs=[given] * len(args),...]
    ppermute x4 -> x2, starting transfers between devices: 6.43 us -> 6.85 us  [the longest x1 5.56 us: between_ends(): return lax.ppermute(x, 'seq', [(0, count - 1), (count - 1, 0)])]
  transfers between devices with their start and end apart: 18 -> 15, of which waited for: 10 -> 8; matrix products, arithmetic and copies ran while one was open for 0% -> 0% of each run, Pallas kernels for 9% -> 10%
where the time goes in v3:
time: 64.2 us; the launch traced here: 63.9 us
  starting transfers between devices  27.3 us (43%)
  waiting for transfers between devices  26.2 us (41%)
  Pallas kernels  9.66 us (15%)
  between operations  0.75 us (1%)
    ppermute x13, waiting for transfers between devices, shift(): return lax.ppermute(x, axis, pairs)  26.2 us
    ppermute x13, starting transfers between devices, shift(): return lax.ppermute(x, axis, pairs)  20.4 us
    pallas_call x9, Pallas kernels, call(): pl.pallas_call(body, out_shape=list(outs), in_specs=[given] * len(args),...  9.66 us
    ppermute x1, starting transfers between devices, between_ends(): return lax.ppermute(x, 'seq', [(0, count - 1), (count - 1, 0)])  5.56 us
    ppermute x1, starting transfers between devices, per_device(): farthest = lax.ppermute(far, 'seq', [(1, 0), (2, 3)])  1.29 us
  transfers between devices with their start and end apart: 15, of which 8 were waited for; matrix products, arithmetic and copies ran while one was open for 0% of the time, Pallas kernels for 10%

profile of v3, /device:TPU:0, one launch (start us, length us, event | category | flops | bytes accessed | tf_op | source)
XLA Modules:
  0.0 63.9 jit_solution(1347161774675074525)
XLA Ops:
  0.6 1.2 %near.1 = (bf16[7,64,384]{2,1,0:T(8,128)(2,1)S(1)}, bf16[7,64,384]{2,1,0:T(8,128)(2,1)S(1)}) custom-call(bf16[4,64,384]{2,1,0:T(8,128)(2,1)} %cot.1, bf16[4,64,384]{2,1,0:T(8,128)(2,1)} %q.3, bf16[4,64,384]{2,1,0:T(8,128)(2,1)} %k.3, bf16[4,64,384]{2,1,0:T(8,128)(2,1)} %v.3), custom_call_target="tpu_custom_call" | custom-call | bytes 1474560 | tf_op jit(solution)/shard_map/near/pallas_call | solution.py:40
  1.8 1.3 %collective-permute-start.1 = (bf16[7,64,384]{2,1,0:T(8,128)(2,1)S(1)}, bf16[7,64,384]{2,1,0:T(8,128)(2,1)S(1)}, u32[]{:S(2)}, u32[]{:S(2)}) collective-permute-start(bf16[7,64,384]{2,1,0:T(8,128)(2,1)S(1)} %get-tuple-element.37), channel_id=1, source_target_pairs={{4,0},{8,4},{12,8},{5,1},{9,5},{13,9},{6,2},{10,6},{14,10},{7,3},{... | collective-permute-start | bytes 1032200 | tf_op jit(solution)/shard_map/ppermute | solution.py:277
  3.1 5.6 %collective-permute-start = (bf16[7,64,384]{2,1,0:T(8,128)(2,1)S(1)}, bf16[7,64,384]{2,1,0:T(8,128)(2,1)S(1)}, u32[]{:S(2)}, u32[]{:S(2)}) collective-permute-start(bf16[7,64,384]{2,1,0:T(8,128)(2,1)S(1)} %get-tuple-element.36.cot_ref), channel_id=1, source_target_pairs={{0,4},{4,8},{8,12},{1,5},{5,9},{9,13},{2,6},{6,10},{10,14},{3,7},{... | collective-permute-start | bytes 1032200 | tf_op jit(solution)/shard_map/ppermute | solution.py:277
  8.7 1.9 %rest.1 = (bf16[4,64,384]{2,1,0:T(8,128)(2,1)S(1)}, bf16[3,64,384]{2,1,0:T(8,128)(2,1)S(1)}, bf16[3,64,384]{2,1,0:T(8,128)(2,1)S(1)}, bf16[3,64,384]{2,1,0:T(8,1...) custom-call(bf16[4,64,384]{2,1,0:T(8,128)(2,1)} %hidden, bf16[4,64,384]{2,1,0:T(8,128)(2,1)} %q.3, ...), custom_call_target="tpu_custom_call" | custom-call | bytes 5160960 | tf_op jit(solution)/shard_map/rest/pallas_call | solution.py:40
  10.6 4.2 %collective-permute-done.1.up_ref.up_qkv.up = bf16[7,64,384]{2,1,0:T(8,128)(2,1)S(1)} collective-permute-done((bf16[7,64,384]{2,1,0:T(8,128)(2,1)S(1)}, bf16[7,64,384]{2,1,0:T(8,128)(2,1)S(1)}, u32[]{:S(2)}, u32[]{:S(2)}) %collective-permute-start.1) | collective-permute-done | bytes 344096 | tf_op jit(solution)/shard_map/ppermute | solution.py:277
  14.8 1.2 %collective-permute-done.down_ref.down_qkv.down = bf16[7,64,384]{2,1,0:T(8,128)(2,1)S(1)} collective-permute-done((bf16[7,64,384]{2,1,0:T(8,128)(2,1)S(1)}, bf16[7,64,384]{2,1,0:T(8,128)(2,1)S(1)}, u32[]{:S(2)}, u32[]{:S(2)}) %collective-permute-start) | collective-permute-done | bytes 344096 | tf_op jit(solution)/shard_map/ppermute | solution.py:277
  16.0 0.9 %conv_back.1 = (bf16[4,64,384]{2,1,0:T(8,128)(2,1)S(1)}, bf16[6,64,384]{2,1,0:T(8,128)(2,1)S(1)}) custom-call(bf16[7,64,384]{2,1,0:T(8,128)(2,1)S(1)} %get-tuple-element.36.cot_ref, bf16[7,64,384]{2,1,0:T(8,128)(2,1)S(1)} %collective-permute-done.down_ref.down_qkv.down, bf16[7,64,384]{2,1,0:T(8,128)(2,1)S(1)} %collective-permute-done.1.up_ref.up_qkv.up, ...), custom_call_target="tpu_custom_call" | custom-call | bytes 3489792 | tf_op jit(solution)/shard_map/conv_back/pallas_call | solution.py:40
  16.9 0.1 collective-permute-start.2
  17.0 3.7 %collective-permute-start.6 = (bf16[3,64,384]{2,1,0:T(8,128)(2,1)S(1)}, bf16[3,64,384]{2,1,0:T(8,128)(2,1)S(1)}, u32[]{:S(2)}, u32[]{:S(2)}) collective-permute-start(bf16[3,64,384]{2,1,0:T(8,128)(2,1)S(1)} %get-tuple-element.49), channel_id=1, source_target_pairs={{0,8},{4,12},{8,0},{12,4},{1,9},{5,13},{9,1},{13,5},{2,10},{6,14},... | collective-permute-start | bytes 442376 | tf_op jit(solution)/shard_map/ppermute | solution.py:277
  20.7 0.0 collective-permute-done.2.got_ref
  20.7 0.4 hidden_grad.1
  21.1 3.5 %collective-permute-start.3 = (bf16[6,64,384]{2,1,0:T(8,128)(2,1)S(1)}, bf16[6,64,384]{2,1,0:T(8,128)(2,1)S(1)}, u32[]{:S(2)}, u32[]{:S(2)}) collective-permute-start(bf16[6,64,384]{2,1,0:T(8,128)(2,1)S(1)} %get-tuple-element.45.to_down), channel_id=1, source_target_pairs={{0,4},{4,8},{8,12},{1,5},{5,9},{9,13},{2,6},{6,10},{10,14},{3,7},{... | collective-permute-start | bytes 884744 | tf_op jit(solution)/shard_map/ppermute | solution.py:277
  24.6 1.3 %collective-permute-start.4 = (bf16[6,64,384]{2,1,0:T(8,128)(2,1)S(1)}, bf16[6,64,384]{2,1,0:T(8,128)(2,1)S(1)}, u32[]{:S(2)}, u32[]{:S(2)}) collective-permute-start(bf16[6,64,384]{2,1,0:T(8,128)(2,1)S(1)} %get-tuple-element.46.to_up), channel_id=1, source_target_pairs={{4,0},{8,4},{12,8},{5,1},{9,5},{13,9},{6,2},{10,6},{14,10},{7,3},{... | collective-permute-start | bytes 884744 | tf_op jit(solution)/shard_map/ppermute | solution.py:277
  25.9 2.4 %collective-permute-done.6.opposite_qkv = bf16[3,64,384]{2,1,0:T(8,128)(2,1)S(1)} collective-permute-done((bf16[3,64,384]{2,1,0:T(8,128)(2,1)S(1)}, bf16[3,64,384]{2,1,0:T(8,128)(2,1)S(1)}, u32[]{:S(2)}, u32[]{:S(2)}) %collective-permute-start.6) | collective-permute-done | bytes 147488 | tf_op jit(solution)/shard_map/ppermute | solution.py:277
  28.3 5.6 %collective-permute-start.7 = (bf16[5,64,384]{2,1,0:T(8,128)(2,1)S(1)}, bf16[5,64,384]{2,1,0:T(8,128)(2,1)S(1)}, u32[]{:S(2)}, u32[]{:S(2)}) collective-permute-start(bf16[5,64,384]{2,1,0:T(8,128)(2,1)S(1)} %get-tuple-element.52), channel_id=1, source_target_pairs={{0,12},{12,0},{1,13},{13,1},{2,14},{14,2},{3,15},{15,3},{16,28},{2... | collective-permute-start | bytes 737288 | tf_op jit(solution)/shard_map/ppermute | solution.py:300
  33.9 0.1 collective-permute-start.8
  33.9 0.0 collective-permute-done.3.down_ref.down.down2
  34.0 1.6 %collective-permute-done.4.up_ref.up.up2 = bf16[6,64,384]{2,1,0:T(8,128)(2,1)S(1)} collective-permute-done((bf16[6,64,384]{2,1,0:T(8,128)(2,1)S(1)}, bf16[6,64,384]{2,1,0:T(8,128)(2,1)S(1)}, u32[]{:S(2)}, u32[]{:S(2)}) %collective-permute-start.4) | collective-permute-done | bytes 294944 | tf_op jit(solution)/shard_map/ppermute | solution.py:277
  35.6 1.3 %collective-permute-start.5 = (bf16[4,64,384]{2,1,0:T(8,128)(2,1)S(1)}, bf16[4,64,384]{2,1,0:T(8,128)(2,1)S(1)}, u32[]{:S(2)}, u32[]{:S(2)}) collective-permute-start(bf16[4,64,384]{2,1,0:T(8,128)(2,1)S(1)} %pick.1), channel_id=1, source_target_pairs={{4,0},{8,12},{5,1},{9,13},{6,2},{10,14},{7,3},{11,15},{20,16},{24,... | collective-permute-start | bytes 589832 | tf_op jit(solution)/shard_map/ppermute | solution.py:334
  36.9 8.8 %collective-permute-done.8.opposite = bf16[2,64,384]{2,1,0:T(8,128)(2,1)S(1)} collective-permute-done((bf16[2,64,384]{2,1,0:T(8,128)(2,1)S(1)}, bf16[2,64,384]{2,1,0:T(8,128)(2,1)S(1)}, u32[]{:S(2)}, u32[]{:S(2)}) %collective-permute-start.8) | collective-permute-done | bytes 98336 | tf_op jit(solution)/shard_map/ppermute | solution.py:277
  45.7 0.0 collective-permute-done.7.end
  45.7 2.0 %attention.1 = (bf16[3,64,384]{2,1,0:T(8,128)(2,1)S(1)}, bf16[3,64,384]{2,1,0:T(8,128)(2,1)S(1)}, bf16[3,64,384]{2,1,0:T(8,128)(2,1)S(1)}, bf16[3,64,384]{2,1,0:T(8,128)(2,1)S(1)}, bf16[4,64,384]{2,1,0:T(8,128)(2,1)S(1)}) custom-call(bf16[3,64,384]{2,1,0:T(8,128)(2,1)S(1)} %get-tuple-element.47.own_qkv, bf16[2,64,384]{2,1,0:T(8,128)(2,1)S(1)} %get-tuple-element.48.own, ...), custom_call_target="tpu_custom_call" | custom-call | flops 2013265920 | bytes 2801664 | tf_op jit(solution)/shard_map/attention/pallas_call | solution.py:40
  47.7 0.1 collective-permute-start.9
  47.8 2.1 %collective-permute-start.12 = (bf16[3,64,384]{2,1,0:T(8,128)(2,1)S(1)}, bf16[3,64,384]{2,1,0:T(8,128)(2,1)S(1)}, u32[]{:S(2)}, u32[]{:S(2)}) collective-permute-start(bf16[3,64,384]{2,1,0:T(8,128)(2,1)S(1)} %get-tuple-element.60), channel_id=1, source_target_pairs={{0,12},{4,0},{8,4},{12,8},{1,13},{5,1},{9,5},{13,9},{2,14},{6,2},{... | collective-permute-start | bytes 442376 | tf_op jit(solution)/shard_map/ppermute | solution.py:277
  49.9 0.0 collective-permute-start.13
  49.9 0.7 %collective-permute-start.14 = (bf16[3,64,384]{2,1,0:T(8,128)(2,1)S(1)}, bf16[3,64,384]{2,1,0:T(8,128)(2,1)S(1)}, u32[]{:S(2)}, u32[]{:S(2)}) collective-permute-start(bf16[3,64,384]{2,1,0:T(8,128)(2,1)S(1)} %get-tuple-element.62), channel_id=1, source_target_pairs={{0,4},{4,8},{8,12},{12,0},{1,5},{5,9},{9,13},{13,1},{2,6},{6,10},{... | collective-permute-start | bytes 442376 | tf_op jit(solution)/shard_map/ppermute | solution.py:277
  50.6 0.0 collective-permute-done.5.farthest
  50.6 0.0 collective-permute-done.9.act_peer
  50.6 1.5 %weight_grad.1 = (f32[3,96,384]{2,1,0:T(8,128)S(1)}, bf16[3,48,384]{2,1,0:T(8,128)(2,1)S(1)}, bf16[3,48,384]{2,1,0:T(8,128)(2,1)S(1)}, bf16[4,64,384]{2,1,0:T(8,128)(2,1)}) custom-call(bf16[7,64,384]{2,1,0:T(8,128)(2,1)S(1)} %get-tuple-element.36.cot_ref, bf16[7,64,384]{2,1,0:T(8,128)(2,1)S(1)} %collective-permute-done.down_ref.down_qkv.down, ...), custom_call_target="tpu_custom_call" | custom-call | bytes 3858432 | tf_op jit(solution)/shard_map/weight_grad/pallas_call | solution.py:40
  52.1 1.5 %collective-permute-start.10 = (bf16[3,48,384]{2,1,0:T(8,128)(2,1)S(1)}, bf16[3,48,384]{2,1,0:T(8,128)(2,1)S(1)}, u32[]{:S(2)}, u32[]{:S(2)}) collective-permute-start(bf16[3,48,384]{2,1,0:T(8,128)(2,1)S(1)} %get-tuple-element.56), channel_id=1, source_target_pairs={{0,2},{2,0},{1,3},{3,1},{4,6},{6,4},{5,7},{7,5},{8,10},{10,8},{9,1... | collective-permute-start | bytes 331784 | tf_op jit(solution)/shard_map/ppermute | solution.py:277
  53.6 0.5 collective-permute-start.11
  54.2 3.9 %collective-permute-done.10.got0_ref = bf16[3,48,384]{2,1,0:T(8,128)(2,1)S(1)} collective-permute-done((bf16[3,48,384]{2,1,0:T(8,128)(2,1)S(1)}, bf16[3,48,384]{2,1,0:T(8,128)(2,1)S(1)}, u32[]{:S(2)}, u32[]{:S(2)}) %collective-permute-start.10) | collective-permute-done | bytes 110624 | tf_op jit(solution)/shard_map/ppermute | solution.py:277
  58.0 1.2 %collective-permute-done.11.got1_ref = bf16[3,48,384]{2,1,0:T(8,128)(2,1)S(1)} collective-permute-done((bf16[3,48,384]{2,1,0:T(8,128)(2,1)S(1)}, bf16[3,48,384]{2,1,0:T(8,128)(2,1)S(1)}, u32[]{:S(2)}, u32[]{:S(2)}) %collective-permute-start.11) | collective-permute-done | bytes 110624 | tf_op jit(solution)/shard_map/ppermute | solution.py:277
  59.3 0.8 %add_weight.1 = f32[3,96,384]{2,1,0:T(8,128)} custom-call(f32[3,96,384]{2,1,0:T(8,128)S(1)} %get-tuple-element.55.own_ref, bf16[3,48,384]{2,1,0:T(8,128)(2,1)S(1)} %collective-permute-done.10.got0_ref, bf16[3,48,384]{2,1,0:T(8,128)(2,1)S(1)} %collective-permute-done.11.got1_ref), custom_call_target="tpu_custom_call" | custom-call | bytes 1105920 | tf_op jit(solution)/shard_map/add_weight/pallas_call | solution.py:40
  60.1 0.0 collective-permute-done.12.refs_1_
  60.1 3.0 %collective-permute-done.13.refs_2_ = bf16[3,64,384]{2,1,0:T(8,128)(2,1)S(1)} collective-permute-done((bf16[3,64,384]{2,1,0:T(8,128)(2,1)S(1)}, bf16[3,64,384]{2,1,0:T(8,128)(2,1)S(1)}, u32[]{:S(2)}, u32[]{:S(2)}) %collective-permute-start.13) | collective-permute-done | bytes 147488 | tf_op jit(solution)/shard_map/ppermute | solution.py:277
  63.1 0.0 collective-permute-done.14.refs_3_
  63.1 0.9 %place.1 = (bf16[4,64,384]{2,1,0:T(8,128)(2,1)}, bf16[4,64,384]{2,1,0:T(8,128)(2,1)}, bf16[4,64,384]{2,1,0:T(8,128)(2,1)}) custom-call(bf16[3,64,384]{2,1,0:T(8,128)(2,1)S(1)} %get-tuple-element.59.refs_0_, bf16[3,64,384]{2,1,0:T(8,128)(2,1)S(1)} %collective-permute-done.12.refs_1_, bf16[3,64,384]{2,1,0:T(8,128)(2,1)S(1)} %collective-permute-done.13.refs_2_, ...), custom_call_target="tpu_custom_call" | custom-call | bytes 1179648 | tf_op jit(solution)/shard_map/place/pallas_call | solution.py:40
  (1 shorter events, 0.0 us)
Async XLA Ops:
  1.8 13.0 %collective-permute-start.1 = (bf16[7,64,384]{2,1,0:T(8,128)(2,1)S(1)}, bf16[7,64,384]{2,1,0:T(8,128)(2,1)S(1)}, u32[]{:S(2)}, u32[]{:S(2)}) collective-permute-start(bf16[7,64,384]{2,1,0:T(8,128)(2,1)S(1)} %get-tuple-element.37), channel_id=1, source_target_pairs={{4,0},{8,4},{12,8},{5,1},{9,5},{13,9},{6,2},{10,6},{14,10},{7,3},{... | collective-permute-start | bytes 1032200 | tf_op jit(solution)/shard_map/ppermute | solution.py:277
  3.1 12.9 %collective-permute-start = (bf16[7,64,384]{2,1,0:T(8,128)(2,1)S(1)}, bf16[7,64,384]{2,1,0:T(8,128)(2,1)S(1)}, u32[]{:S(2)}, u32[]{:S(2)}) collective-permute-start(bf16[7,64,384]{2,1,0:T(8,128)(2,1)S(1)} %get-tuple-element.36.cot_ref), channel_id=1, source_target_pairs={{0,4},{4,8},{8,12},{1,5},{5,9},{9,13},{2,6},{6,10},{10,14},{3,7},{... | collective-permute-start | bytes 1032200 | tf_op jit(solution)/shard_map/ppermute | solution.py:277
  16.9 3.8 %collective-permute-start.2 = (bf16[6,64,384]{2,1,0:T(8,128)(2,1)S(1)}, bf16[6,64,384]{2,1,0:T(8,128)(2,1)S(1)}, u32[]{:S(2)}, u32[]{:S(2)}) collective-permute-start(bf16[6,64,384]{2,1,0:T(8,128)(2,1)S(1)} %get-tuple-element.43), channel_id=1, source_target_pairs={{0,1},{1,0},{2,3},{3,2},{4,5},{5,4},{6,7},{7,6},{8,9},{9,8},{10,11... | collective-permute-start | bytes 884744 | tf_op jit(solution)/shard_map/ppermute | solution.py:277
  17.0 11.3 %collective-permute-start.6 = (bf16[3,64,384]{2,1,0:T(8,128)(2,1)S(1)}, bf16[3,64,384]{2,1,0:T(8,128)(2,1)S(1)}, u32[]{:S(2)}, u32[]{:S(2)}) collective-permute-start(bf16[3,64,384]{2,1,0:T(8,128)(2,1)S(1)} %get-tuple-element.49), channel_id=1, source_target_pairs={{0,8},{4,12},{8,0},{12,4},{1,9},{5,13},{9,1},{13,5},{2,10},{6,14},... | collective-permute-start | bytes 442376 | tf_op jit(solution)/shard_map/ppermute | solution.py:277
  21.1 12.8 %collective-permute-start.3 = (bf16[6,64,384]{2,1,0:T(8,128)(2,1)S(1)}, bf16[6,64,384]{2,1,0:T(8,128)(2,1)S(1)}, u32[]{:S(2)}, u32[]{:S(2)}) collective-permute-start(bf16[6,64,384]{2,1,0:T(8,128)(2,1)S(1)} %get-tuple-element.45.to_down), channel_id=1, source_target_pairs={{0,4},{4,8},{8,12},{1,5},{5,9},{9,13},{2,6},{6,10},{10,14},{3,7},{... | collective-permute-start | bytes 884744 | tf_op jit(solution)/shard_map/ppermute | solution.py:277
  24.6 10.9 %collective-permute-start.4 = (bf16[6,64,384]{2,1,0:T(8,128)(2,1)S(1)}, bf16[6,64,384]{2,1,0:T(8,128)(2,1)S(1)}, u32[]{:S(2)}, u32[]{:S(2)}) collective-permute-start(bf16[6,64,384]{2,1,0:T(8,128)(2,1)S(1)} %get-tuple-element.46.to_up), channel_id=1, source_target_pairs={{4,0},{8,4},{12,8},{5,1},{9,5},{13,9},{6,2},{10,6},{14,10},{7,3},{... | collective-permute-start | bytes 884744 | tf_op jit(solution)/shard_map/ppermute | solution.py:277
  28.3 17.4 %collective-permute-start.7 = (bf16[5,64,384]{2,1,0:T(8,128)(2,1)S(1)}, bf16[5,64,384]{2,1,0:T(8,128)(2,1)S(1)}, u32[]{:S(2)}, u32[]{:S(2)}) collective-permute-start(bf16[5,64,384]{2,1,0:T(8,128)(2,1)S(1)} %get-tuple-element.52), channel_id=1, source_target_pairs={{0,12},{12,0},{1,13},{13,1},{2,14},{14,2},{3,15},{15,3},{16,28},{2... | collective-permute-start | bytes 737288 | tf_op jit(solution)/shard_map/ppermute | solution.py:300
  33.9 11.8 %collective-permute-start.8 = (bf16[2,64,384]{2,1,0:T(8,128)(2,1)S(1)}, bf16[2,64,384]{2,1,0:T(8,128)(2,1)S(1)}, u32[]{:S(2)}, u32[]{:S(2)}) collective-permute-start(bf16[2,64,384]{2,1,0:T(8,128)(2,1)S(1)} %get-tuple-element.53.to_opposite), channel_id=1, source_target_pairs={{0,8},{4,12},{8,0},{12,4},{1,9},{5,13},{9,1},{13,5},{2,10},{6,14},... | collective-permute-start | bytes 294920 | tf_op jit(solution)/shard_map/ppermute | solution.py:277
  35.6 15.0 %collective-permute-start.5 = (bf16[4,64,384]{2,1,0:T(8,128)(2,1)S(1)}, bf16[4,64,384]{2,1,0:T(8,128)(2,1)S(1)}, u32[]{:S(2)}, u32[]{:S(2)}) collective-permute-start(bf16[4,64,384]{2,1,0:T(8,128)(2,1)S(1)} %pick.1), channel_id=1, source_target_pairs={{4,0},{8,12},{5,1},{9,13},{6,2},{10,14},{7,3},{11,15},{20,16},{24,... | collective-permute-start | bytes 589832 | tf_op jit(solution)/shard_map/ppermute | solution.py:334
  47.7 2.9 %collective-permute-start.9 = (bf16[4,64,384]{2,1,0:T(8,128)(2,1)S(1)}, bf16[4,64,384]{2,1,0:T(8,128)(2,1)S(1)}, u32[]{:S(2)}, u32[]{:S(2)}) collective-permute-start(bf16[4,64,384]{2,1,0:T(8,128)(2,1)S(1)} %get-tuple-element.54.act_ref), channel_id=1, source_target_pairs={{0,1},{1,0},{2,3},{3,2},{4,5},{5,4},{6,7},{7,6},{8,9},{9,8},{10,11... | collective-permute-start | bytes 589832 | tf_op jit(solution)/shard_map/ppermute | solution.py:277
  47.8 12.3 %collective-permute-start.12 = (bf16[3,64,384]{2,1,0:T(8,128)(2,1)S(1)}, bf16[3,64,384]{2,1,0:T(8,128)(2,1)S(1)}, u32[]{:S(2)}, u32[]{:S(2)}) collective-permute-start(bf16[3,64,384]{2,1,0:T(8,128)(2,1)S(1)} %get-tuple-element.60), channel_id=1, source_target_pairs={{0,12},{4,0},{8,4},{12,8},{1,13},{5,1},{9,5},{13,9},{2,14},{6,2},{... | collective-permute-start | bytes 442376 | tf_op jit(solution)/shard_map/ppermute | solution.py:277
  49.9 13.1 %collective-permute-start.13 = (bf16[3,64,384]{2,1,0:T(8,128)(2,1)S(1)}, bf16[3,64,384]{2,1,0:T(8,128)(2,1)S(1)}, u32[]{:S(2)}, u32[]{:S(2)}) collective-permute-start(bf16[3,64,384]{2,1,0:T(8,128)(2,1)S(1)} %get-tuple-element.61), channel_id=1, source_target_pairs={{0,8},{4,12},{8,0},{12,4},{1,9},{5,13},{9,1},{13,5},{2,10},{6,14},... | collective-permute-start | bytes 442376 | tf_op jit(solution)/shard_map/ppermute | solution.py:277
  49.9 13.1 %collective-permute-start.14 = (bf16[3,64,384]{2,1,0:T(8,128)(2,1)S(1)}, bf16[3,64,384]{2,1,0:T(8,128)(2,1)S(1)}, u32[]{:S(2)}, u32[]{:S(2)}) collective-permute-start(bf16[3,64,384]{2,1,0:T(8,128)(2,1)S(1)} %get-tuple-element.62), channel_id=1, source_target_pairs={{0,4},{4,8},{8,12},{12,0},{1,5},{5,9},{9,13},{13,1},{2,6},{6,10},{... | collective-permute-start | bytes 442376 | tf_op jit(solution)/shard_map/ppermute | solution.py:277
  52.1 5.9 %collective-permute-start.10 = (bf16[3,48,384]{2,1,0:T(8,128)(2,1)S(1)}, bf16[3,48,384]{2,1,0:T(8,128)(2,1)S(1)}, u32[]{:S(2)}, u32[]{:S(2)}) collective-permute-start(bf16[3,48,384]{2,1,0:T(8,128)(2,1)S(1)} %get-tuple-element.56), channel_id=1, source_target_pairs={{0,2},{2,0},{1,3},{3,1},{4,6},{6,4},{5,7},{7,5},{8,10},{10,8},{9,1... | collective-permute-start | bytes 331784 | tf_op jit(solution)/shard_map/ppermute | solution.py:277
  53.6 5.6 %collective-permute-start.11 = (bf16[3,48,384]{2,1,0:T(8,128)(2,1)S(1)}, bf16[3,48,384]{2,1,0:T(8,128)(2,1)S(1)}, u32[]{:S(2)}, u32[]{:S(2)}) collective-permute-start(bf16[3,48,384]{2,1,0:T(8,128)(2,1)S(1)} %get-tuple-element.57), channel_id=1, source_target_pairs={{0,2},{2,0},{1,3},{3,1},{4,6},{6,4},{5,7},{7,5},{8,10},{10,8},{9,1... | collective-permute-start | bytes 331784 | tf_op jit(solution)/shard_map/ppermute | solution.py:277

commit v4 on v3

--- a/solution.py
+++ b/solution.py
@@ -28,9 +28,11 @@
     )
 
 
-def kernel_call(body, outs, flops=0, transcendentals=0, name=None, scratch=(), space=pltpu.VMEM):
-    vmem = pl.BlockSpec(memory_space=pltpu.VMEM)
-    given = pl.BlockSpec(memory_space=space)
+def kernel_call(
+    body, outs, flops=0, transcendentals=0, name=None, scratch=(), space=pltpu.VMEM,
+    out_space=pltpu.VMEM,
+):
+    given, made = (pl.BlockSpec(memory_space=x) for x in (space, out_space))
 
     def call(*args):
         if space == pltpu.HBM:
@@ -41,7 +43,7 @@
             body,
             out_shape=list(outs),
             in_specs=[given] * len(args),
-            out_specs=[vmem] * len(outs),
+            out_specs=[made] * len(outs),
             scratch_shapes=list(scratch),
             compiler_params=pltpu.CompilerParams(vmem_limit_bytes=VMEM_LIMIT),
             cost_estimate=pl.CostEstimate(
@@ -64,112 +66,116 @@
     return copies
 
 
-def near_kernel(count, cot, q, k, v, down, up, sems):
+def near_kernel(cot, q, k, v, beside, mirror, sems):
     s = lax.axis_index("seq")
     blocks = cot.shape[0]
     pairs = []
-    for out, d in ((down, 1), (up, count - 1)):
+    for out, d in ((beside, 1), (mirror, 3)):
         pairs.append((cot, out.at[pl.ds(0, blocks)]))
-        pairs += [(x.at[lax.rem(s + d, count)], out.at[blocks + j]) for j, x in enumerate((q, k, v))]
+        pairs += [(x.at[s ^ d], out.at[blocks + j]) for j, x in enumerate((q, k, v))]
     for copy in fetch(pairs, sems):
         copy.wait()
 
 
-def rest_kernel(count, hidden, q, k, v, w, h_ref, own, opposite, end, w_ref, act_ref, sems):
+def rest_kernel(hidden, q, k, v, w, own, opposite, w_ref, slope_ref, act_ref, sent_ref, h_ref, sems):
     s = lax.axis_index("seq")
+    c = lax.axis_index("chan")
     pairs = [(hidden, h_ref)]
-    for out, b in ((own, s), (opposite, lax.rem(s + 2, count)), (end, count - 1 - s)):
+    for out, b in ((opposite, s ^ 2), (own, s)):
         pairs += [(x.at[b], out.at[j]) for j, x in enumerate((q, k, v))]
     pairs.append((w, w_ref))
     copies = fetch(pairs, sems)
     copies[0].wait()
     blocks, rows, width = h_ref.shape
-    act = tanh_gelu(h_ref[...].astype(F32)).reshape(blocks * rows, width)
-    act_t = act.T.astype(BF)
+    signal = h_ref[...].astype(F32)
+    slope_ref[...] = gelu_slope(signal)
+    act_t = tanh_gelu(signal).reshape(blocks * rows, width).T.astype(BF)
     lanes = act_t.shape[1] // 2
     parts = width // lanes
-    for i in range(2 * parts):
-        for h in range(2):
-            act_ref[i // parts * 2 + h, :, pl.ds(i % parts * lanes, lanes)] = act_t[
-                i * rows : (i + 1) * rows, h * lanes : (h + 1) * lanes
-            ]
+    halves = act_t[:, :lanes], act_t[:, lanes:]
+    first = c == 0
+    kept, sent = jnp.where(first, *halves), jnp.where(first, halves[1], halves[0])
+    for out, half in ((act_ref, kept), (sent_ref, sent)):
+        for i in range(2 * parts):
+            out[i // parts, :, pl.ds(i % parts * lanes, lanes)] = half[i * rows : (i + 1) * rows]
     for copy in copies[1:]:
         copy.wait()
 
 
-def conv_kernel(cot_ref, down_ref, up_ref, w_ref, act_ref, mine_ref, other_ref):
+def conv_term(tap, w_ref, t, side):
+    width = w_ref.shape[2]
+    start = pl.multiple_of(side * width, width)
+    return lax.dot_general(
+        tap,
+        w_ref[t, pl.ds(start, width), :],
+        (((1,), (1,)), ((), ())),
+        preferred_element_type=F32,
+    )
+
+
+def centre_kernel(cot_ref, w_ref, mine_ref, other_ref):
     c = lax.axis_index("chan")
-    blocks, rows, width = mine_ref.shape
-    taps = [r[:blocks].reshape(blocks * rows, width) for r in (up_ref, cot_ref, down_ref)]
-    for out_ref, side in ((other_ref, 1 - c), (mine_ref, c)):
-        start = pl.multiple_of(side * width, width)
-        total = None
-        for t in range(3):
-            term = lax.dot_general(
-                taps[t],
-                w_ref[t, pl.ds(start, width), :],
-                (((1,), (1,)), ((), ())),
-                preferred_element_type=F32,
-            )
-            total = term if total is None else total + term
-        out_ref[:blocks] = total.astype(BF).reshape(blocks, rows, width)
-    for k in range(2):
-        other_ref[blocks + k] = act_ref[2 * k + 1 - c]
+    blocks = cot_ref.shape[0] - 3
+    tap = cot_ref[:blocks].reshape(mine_ref.shape)
+    mine_ref[...] = conv_term(tap, w_ref, 1, c)
+    other_ref[...] = conv_term(tap, w_ref, 1, 1 - c)
+
+
+def conv_kernel(mine, beside_ref, mirror_ref, w_ref, centre_ref, out_ref):
+    c = lax.axis_index("chan")
+    even = lax.rem(lax.axis_index("seq"), 2) == 0
+    blocks = out_ref.shape[0]
+    beside = beside_ref[:blocks].reshape(centre_ref.shape)
+    mirror = mirror_ref[:blocks].reshape(centre_ref.shape)
+    side = c if mine else 1 - c
+    total = (
+        centre_ref[...]
+        + conv_term(jnp.where(even, beside, mirror), w_ref, 0, side)
+        + conv_term(jnp.where(even, mirror, beside), w_ref, 2, side)
+    )
+    out_ref[...] = total.astype(BF).reshape(out_ref.shape)
 
 
 def grad_kernel(
-    count, cot_ref, h_ref, mine_ref, got_ref, act_ref, down_ref, up_ref, end_qkv,
-    own, down, opposite, up, end,
+    cot_ref, slope_ref, mine_ref, got_ref, act_ref, act_peer, beside_ref, mirror_ref, to_mirror,
+    own, beside, opposite, mirror, end,
 ):
     s = lax.axis_index("seq")
     c = lax.axis_index("chan")
-    blocks = h_ref.shape[0]
-
-    def sequence(b):
+    blocks = mine_ref.shape[0]
+    for d, out in ((1, beside), (3, mirror), (2, opposite), (0, own)):
+        b = s ^ d
         back = mine_ref[b].astype(F32) + got_ref[b].astype(F32)
-        slope = gelu_slope(h_ref[b].astype(F32))
-        grad = (cot_ref[b].astype(F32) + back * slope).astype(BF)
+        out[0] = (cot_ref[b].astype(F32) + back * slope_ref[b]).astype(BF)
         k = lax.rem(b, 2)
-        act = jnp.where(lax.div(b, 2) == c, act_ref[2 * k + c], got_ref[blocks + k])
-        return grad, act
-
-    for d, out in ((0, own), (1, down), (2, opposite), (3, up)):
-        out[0], out[1] = sequence(lax.rem(s + d, count))
-    end[:3] = end_qkv[...]
-    first = s == 0
-    end[3] = jnp.where(first, up[0], down[0])
-    end[4] = jnp.where(first, up[1], down[1])
-    down[2:] = down_ref[:blocks]
-    up[2:] = up_ref[:blocks]
-
-
-def pick_kernel(down_ref, up_ref, out_ref):
-    out_ref[...] = jnp.where(lax.axis_index("seq") < 2, up_ref[2:], down_ref[2:])
+        out[1] = jnp.where(lax.div(b, 2) == c, act_ref[k], act_peer[k])
+    end[:3] = to_mirror[blocks:]
+    end[3:] = mirror[:2]
+    beside[2:] = mirror_ref[:blocks]
+    mirror[2:] = beside_ref[:blocks]
+
+
+def pick_kernel(held_ref, out_ref):
+    out_ref[...] = held_ref[2:]
 
 
 def attention_kernel(
-    count, own_qkv, own, down_qkv, up_qkv, opposite_qkv, end, down, up, opposite, *outs
+    count, own_qkv, own, beside_qkv, mirror_qkv, opposite_qkv, end, beside, mirror, opposite, *outs
 ):
     outs, act_ref = outs[:count], outs[count]
     rows, width = own.shape[1:]
-    near = down_qkv.shape[0] - 3
+    near = beside_qkv.shape[0] - 3
     scale = 1.0 / math.sqrt(HD)
     s = lax.axis_index("seq")
-    at_first, at_last = s == 0, s == count - 1
+    at_end = jnp.logical_or(s == 0, s == count - 1)
 
     def positions(j):
-        before = jnp.where(at_first, end[j], down_qkv[near + j])
-        behind = jnp.where(at_last, end[j], up_qkv[near + j])
-        return jnp.concatenate([own_qkv[j], before, opposite_qkv[j], behind], axis=0)
+        facing = jnp.where(at_end, end[j], mirror_qkv[near + j])
+        return jnp.concatenate([own_qkv[j], beside_qkv[near + j], opposite_qkv[j], facing], axis=0)
 
     query, key, value = (positions(j) for j in range(3))
     grad, act = (
-        (
-            own[j],
-            jnp.where(at_first, end[3 + j], down[j]),
-            opposite[j],
-            jnp.where(at_last, end[3 + j], up[j]),
-        )
+        (own[j], beside[j], opposite[j], jnp.where(at_end, end[3 + j], mirror[j]))
         for j in range(2)
     )
     grad = jnp.concatenate(grad, axis=0)
@@ -199,40 +205,32 @@
 
 
 def weight_kernel(
-    count, factor, cot_ref, down, up, down2, up2, farthest, act_ref, act_peer, own, to_down,
-    to_opposite, to_up, own_ref, sent0_ref, sent1_ref, grad_ref, act_buf, cot_buf,
+    count, factor, cot_ref, beside, mirror, beside2, mirror2, farthest, act_ref, act_peer, own,
+    to_beside, to_opposite, to_mirror, own_ref, sent0_ref, sent1_ref, grad_ref, act_buf, cot_buf,
 ):
     s = lax.axis_index("seq")
     c = lax.axis_index("chan")
     b = lax.axis_index("batch")
     blocks, rows, width = grad_ref.shape
-    for d, piece in enumerate((own, to_down, to_opposite, to_up)):
-        grad_ref[lax.rem(s + d, count)] = piece[0]
+    for d, piece in enumerate((own, to_beside, to_opposite, to_mirror)):
+        grad_ref[s ^ d] = piece[0]
     lanes = act_buf.shape[2] // 2
     for d in range(count):
-        j = lax.rem(s - d + count, count)
         halves = (
             jnp.where(c == 0, act_ref[d], act_peer[d]),
             jnp.where(c == 0, act_peer[d], act_ref[d]),
         )
         for r in range(width // lanes):
             for h in range(2):
-                act_buf[j, pl.ds(r * rows, rows), pl.ds(h * lanes, lanes)] = halves[h][
+                act_buf[s ^ d, pl.ds(r * rows, rows), pl.ds(h * lanes, lanes)] = halves[h][
                     :, r * lanes : (r + 1) * lanes
                 ]
     flat = cot_buf.shape[1:]
-
-    def put(position, holds, value):
-        @pl.when(holds)
-        def _():
-            cot_buf[position] = value().reshape(flat)
-
+    at_end = jnp.logical_or(s == 0, s == count - 1)
     cot_buf[s] = cot_ref[:blocks].reshape(flat)
-    put(s - 1, s > 0, lambda: down[:blocks])
-    put(s + 1, s < count - 1, lambda: up[:blocks])
-    put(s - 2, s >= 2, lambda: down2[2:])
-    put(s + 2, s < 2, lambda: up2[2:])
-    put(count - 1 - s, jnp.logical_or(s == 0, s == count - 1), lambda: farthest[...])
+    cot_buf[s ^ 1] = beside[:blocks].reshape(flat)
+    cot_buf[s ^ 3] = jnp.where(at_end, farthest[...], mirror[:blocks]).reshape(flat)
+    cot_buf[s ^ 2] = jnp.where(at_end, beside2[2:], mirror2[2:]).reshape(flat)
 
     half = own_ref.shape[1]
     for t in range(3):
@@ -263,18 +261,16 @@
 
 
 def place_kernel(count, *refs):
-    pieces, outs = refs[:count], refs[count:]
+    pieces, outs, sems = refs[:count], refs[count:-1], refs[-1]
     s = lax.axis_index("seq")
-    for d in range(count):
-        b = lax.rem(s + d, count)
-        for j in range(3):
-            outs[j][b] = pieces[d][j]
-
-
-def shift(x, axis, by, wrap):
+    pairs = [(pieces[d].at[j], outs[j].at[s ^ d]) for d in range(count) for j in range(3)]
+    for copy in fetch(pairs, sems):
+        copy.wait()
+
+
+def swap(x, axis, by, only=None):
     n = lax.axis_size(axis)
-    pairs = [(i, (i + by) % n) for i in range(n) if wrap or 0 <= i + by < n]
-    return lax.ppermute(x, axis, pairs)
+    return lax.ppermute(x, axis, [(i, i ^ by) for i in range(n) if only is None or i in only])
 
 
 def after(first, *then):
@@ -289,48 +285,54 @@
     factor = 1.0 / math.sqrt(tokens * count * lax.axis_size("batch"))
     weights = conv_weight.transpose(1, 0, 2)
     part = width // 2
+    middle, ends = (1, 2), (0, 3)
 
     def units(n):
         return shape((n, rows, width))
 
-    def along(x, by):
-        return shift(x, "seq", by, False)
-
-    def between_ends(x):
-        return lax.ppermute(x, "seq", [(0, count - 1), (count - 1, 0)])
-
-    to_down, to_up = kernel_call(
-        functools.partial(near_kernel, count),
+    to_beside, to_mirror = kernel_call(
+        near_kernel,
         [units(blocks + 3)] * 2,
         name="near",
         scratch=[pltpu.SemaphoreType.DMA((8,))],
         space=pltpu.HBM,
     )(cotangent, query_vectors, key_vectors, value_vectors)
-    down, up = along(to_down, 1), along(to_up, -1)
-    (hidden,) = after(to_down, hidden)
-    hidden, own_qkv, to_opposite, to_end, weights, act = kernel_call(
-        functools.partial(rest_kernel, count),
-        [units(blocks), units(3), units(3), units(3), shape(weights.shape), units(blocks)],
+    beside = swap(to_beside, "seq", 1)
+    mirror = swap(to_mirror, "seq", 3, middle)
+    (hidden,) = after(to_beside, hidden)
+    own_qkv, to_opposite, weights, slope, act, act_sent = kernel_call(
+        rest_kernel,
+        [units(3)] * 2 + [shape(weights.shape), shape(hidden.shape, F32), units(2), units(2)],
         name="rest",
-        scratch=[pltpu.SemaphoreType.DMA((11,))],
+        scratch=[pltpu.VMEM(hidden.shape, BF), pltpu.SemaphoreType.DMA((8,))],
         space=pltpu.HBM,
     )(hidden, query_vectors, key_vectors, value_vectors, weights)
-    opposite = shift(to_opposite, "seq", 2, True)
-
-    mine, other = kernel_call(conv_kernel, [units(blocks), units(blocks + 2)], name="conv_back")(
-        to_down, down, up, weights, act
-    )
-    got = shift(other, "chan", 1, True)
-    own, to_down2, to_opposite2, to_up2, to_end2 = kernel_call(
-        functools.partial(grad_kernel, count),
+    act_got = swap(act_sent, "chan", 1)
+    opposite = swap(to_opposite, "seq", 2)
+
+    flat = shape((tokens, width), F32)
+    centre_mine, centre_other = kernel_call(centre_kernel, [flat] * 2, name="conv_centre")(
+        to_beside, weights
+    )
+    (other,) = kernel_call(
+        functools.partial(conv_kernel, False), [units(blocks)], name="conv_other"
+    )(beside, mirror, weights, centre_other)
+    got = swap(other, "chan", 1)
+    (centre_mine,) = after(other, centre_mine)
+    (mine,) = kernel_call(functools.partial(conv_kernel, True), [units(blocks)], name="conv_mine")(
+        beside, mirror, weights, centre_mine
+    )
+    own, to_beside2, to_opposite2, to_mirror2, to_end2 = kernel_call(
+        grad_kernel,
         [units(2), units(blocks + 2), units(2), units(blocks + 2), units(5)],
         name="hidden_grad",
-    )(to_down, hidden, mine, got, act, down, up, to_end)
-    down2, up2 = along(to_down2, 1), along(to_up2, -1)
+    )(to_beside, slope, mine, got, act, act_got, beside, mirror, to_mirror)
+    beside2 = swap(to_beside2, "seq", 1)
+    mirror2 = swap(to_mirror2, "seq", 3, middle)
     far_opposite, far_end = after(opposite, to_opposite2, to_end2)
-    opposite2 = shift(far_opposite, "seq", 2, True)
-    end2 = between_ends(far_end)
-    (far,) = kernel_call(pick_kernel, [units(blocks)], name="pick")(down2, up2)
+    opposite2 = swap(far_opposite, "seq", 2)
+    end2 = swap(far_end, "seq", 3, ends)
+    (far,) = kernel_call(pick_kernel, [units(blocks)], name="pick")(mirror2)
     farthest = lax.ppermute(far, "seq", [(1, 0), (2, 3)])
 
     item = 5 * (count * rows) ** 2 * width
@@ -340,10 +342,10 @@
         flops=COST * 2 * item,
         transcendentals=(count * rows) ** 2 * (width // HD),
         name="attention",
-    )(own_qkv, own, down, up, opposite, end2, down2, up2, opposite2)
-    back = [returned[0]] + [shift(returned[d], "seq", -d, True) for d in range(1, count)]
-
-    act_peer = shift(act_held, "chan", 1, True)
+    )(own_qkv, own, beside, mirror, opposite, end2, beside2, mirror2, opposite2)
+    back = [returned[0]] + [swap(returned[d], "seq", d) for d in range(1, count)]
+
+    act_peer = swap(act_held, "chan", 1)
     total, sent0, sent1, hidden_grad = kernel_call(
         functools.partial(weight_kernel, count, factor),
         [shape((3, part // 2, width), F32)] + [shape((3, part // 4, width))] * 2 + [units(blocks)],
@@ -353,16 +355,20 @@
             pltpu.VMEM((count, tokens, width), BF),
         ],
     )(
-        to_down, down, up, down2, up2, farthest, act_held, act_peer, own, to_down2, to_opposite2,
-        to_up2,
-    )
-    got_sums = [shift(x, "batch", 1, True) for x in (sent0, sent1)]
+        to_beside, beside, mirror, beside2, mirror2, farthest, act_held, act_peer, own, to_beside2,
+        to_opposite2, to_mirror2,
+    )
+    got_sums = [swap(x, "batch", 1) for x in (sent0, sent1)]
     (weight_grad,) = kernel_call(add_kernel, [shape((3, part // 2, width), F32)], name="add_weight")(
         total, *got_sums
     )
     (back[0],) = after(weight_grad, back[0])
     query_grad, key_grad, value_grad = kernel_call(
-        functools.partial(place_kernel, count), [units(blocks)] * 3, name="place"
+        functools.partial(place_kernel, count),
+        [units(blocks)] * 3,
+        name="place",
+        scratch=[pltpu.SemaphoreType.DMA((3 * count,))],
+        out_space=pltpu.HBM,
     )(*back)
     return (query_grad, key_grad, value_grad, hidden_grad, weight_grad.transpose(1, 0, 2))
 

time: 64.2 us -> 60.6 us (0.944)
  starting transfers between devices: 27.3 us -> 23.7 us
    ppermute x14 -> x15, starting transfers between devices: 26 us -> 22.5 us  [swap(): lax.ppermute(x, axis, [(i, i ^ by) for i in range(n) if only is None or i...]
    ppermute x14 -> x15, waiting for transfers between devices: 26.2 us -> 26.2 us  [swap(): lax.ppermute(x, axis, [(i, i ^ by) for i in range(n) if only is None or i...]
    pallas_call x9 -> x11, Pallas kernels: 9.66 us -> 9.67 us  [call(): pl.pallas_call(body, out_shape=list(outs), in_specs=[given] * len(args),...]
  transfers between devices with their start and end apart: 15 -> 16, of which waited for: 8 -> 6; matrix products, arithmetic and copies ran while one was open for 0% -> 0% of each run, Pallas kernels for 10% -> 12%
where the time goes in v4:
time: 60.6 us; the launch traced here: 60.4 us
  waiting for transfers between devices  26.2 us (43%)
  starting transfers between devices  23.7 us (39%)
  Pallas kernels  9.67 us (16%)
  between operations  0.78 us (1%)
    ppermute x15, waiting for transfers between devices, swap(): lax.ppermute(x, axis, [(i, i ^ by) for i in range(n) if only is None or i...  26.2 us
    ppermute x15, starting transfers between devices, swap(): lax.ppermute(x, axis, [(i, i ^ by) for i in range(n) if only is None or i...  22.5 us
    pallas_call x11, Pallas kernels, call(): pl.pallas_call(body, out_shape=list(outs), in_specs=[given] * len(args),...  9.67 us
    ppermute x1, starting transfers between devices, per_device(): farthest = lax.ppermute(far, 'seq', [(1, 0), (2, 3)])  1.29 us
  transfers between devices with their start and end apart: 16, of which 6 were waited for; matrix products, arithmetic and copies ran while one was open for 0% of the time, Pallas kernels for 12%

profile of v4, /device:TPU:0, one launch (start us, length us, event | category | flops | bytes accessed | tf_op | source)
XLA Modules:
  0.0 60.4 jit_solution(3673271927436661636)
XLA Ops:
  0.6 1.2 %near.1 = (bf16[7,64,384]{2,1,0:T(8,128)(2,1)S(1)}, bf16[7,64,384]{2,1,0:T(8,128)(2,1)S(1)}) custom-call(bf16[4,64,384]{2,1,0:T(8,128)(2,1)} %cot.1, bf16[4,64,384]{2,1,0:T(8,128)(2,1)} %q.3, bf16[4,64,384]{2,1,0:T(8,128)(2,1)} %k.3, bf16[4,64,384]{2,1,0:T(8,128)(2,1)} %v.3), custom_call_target="tpu_custom_call" | custom-call | bytes 1474560 | tf_op jit(solution)/shard_map/near/pallas_call | solution.py:42
  1.8 0.7 %collective-permute-start.1 = (bf16[7,64,384]{2,1,0:T(8,128)(2,1)S(1)}, bf16[7,64,384]{2,1,0:T(8,128)(2,1)S(1)}, u32[]{:S(2)}, u32[]{:S(2)}) collective-permute-start(bf16[7,64,384]{2,1,0:T(8,128)(2,1)S(1)} %get-tuple-element.38.to_mirror), channel_id=1, source_target_pairs={{4,8},{8,4},{5,9},{9,5},{6,10},{10,6},{7,11},{11,7},{20,24},{24,20... | collective-permute-start | bytes 1032200 | tf_op jit(solution)/shard_map/ppermute | solution.py:273
  2.5 5.9 %collective-permute-start = (bf16[7,64,384]{2,1,0:T(8,128)(2,1)S(1)}, bf16[7,64,384]{2,1,0:T(8,128)(2,1)S(1)}, u32[]{:S(2)}, u32[]{:S(2)}) collective-permute-start(bf16[7,64,384]{2,1,0:T(8,128)(2,1)S(1)} %get-tuple-element.37.cot_ref), channel_id=1, source_target_pairs={{0,4},{4,0},{8,12},{12,8},{1,5},{5,1},{9,13},{13,9},{2,6},{6,2},{1... | collective-permute-start | bytes 1032200 | tf_op jit(solution)/shard_map/ppermute | solution.py:273
  8.4 1.8 %rest.1 = (bf16[3,64,384]{2,1,0:T(8,128)(2,1)S(1)}, bf16[3,64,384]{2,1,0:T(8,128)(2,1)S(1)}, bf16[3,768,384]{2,1,0:T(8,128)(2,1)S(1)}, f32[4,64,384]{2,1,0:T(8,1...) custom-call(bf16[4,64,384]{2,1,0:T(8,128)(2,1)} %hidden, bf16[4,64,384]{2,1,0:T(8,128)(2,1)} %q.3, ...), custom_call_target="tpu_custom_call" | custom-call | bytes 5210112 | tf_op jit(solution)/shard_map/rest/pallas_call | solution.py:42
  10.2 0.4 conv_centre.1
  10.7 0.0 collective-permute-done.1.mirror_ref.mirror_qkv.mirror
  10.7 5.5 %collective-permute-done.beside_ref.beside_qkv.beside = bf16[7,64,384]{2,1,0:T(8,128)(2,1)S(1)} collective-permute-done((bf16[7,64,384]{2,1,0:T(8,128)(2,1)S(1)}, bf16[7,64,384]{2,1,0:T(8,128)(2,1)S(1)}, u32[]{:S(2)}, u32[]{:S(2)}) %collective-permute-start) | collective-permute-done | bytes 344096 | tf_op jit(solution)/shard_map/ppermute | solution.py:273
  16.2 0.4 conv_other.1
  16.6 0.1 collective-permute-start.2
  16.7 0.5 collective-permute-start.3
  17.2 1.6 %collective-permute-start.7 = (bf16[3,64,384]{2,1,0:T(8,128)(2,1)S(1)}, bf16[3,64,384]{2,1,0:T(8,128)(2,1)S(1)}, u32[]{:S(2)}, u32[]{:S(2)}) collective-permute-start(bf16[3,64,384]{2,1,0:T(8,128)(2,1)S(1)} %get-tuple-element.51), channel_id=1, source_target_pairs={{0,8},{4,12},{8,0},{12,4},{1,9},{5,13},{9,1},{13,5},{2,10},{6,14},... | collective-permute-start | bytes 442376 | tf_op jit(solution)/shard_map/ppermute | solution.py:273
  18.8 0.4 conv_mine.1.mine_ref
  19.2 0.0 collective-permute-done.3.act_peer
  19.2 0.0 collective-permute-done.2.got_ref
  19.2 0.2 hidden_grad.1
  19.4 0.7 %collective-permute-start.5 = (bf16[6,64,384]{2,1,0:T(8,128)(2,1)S(1)}, bf16[6,64,384]{2,1,0:T(8,128)(2,1)S(1)}, u32[]{:S(2)}, u32[]{:S(2)}) collective-permute-start(bf16[6,64,384]{2,1,0:T(8,128)(2,1)S(1)} %get-tuple-element.48.to_mirror), channel_id=1, source_target_pairs={{4,8},{8,4},{5,9},{9,5},{6,10},{10,6},{7,11},{11,7},{20,24},{24,20... | collective-permute-start | bytes 884744 | tf_op jit(solution)/shard_map/ppermute | solution.py:273
  20.1 3.2 %collective-permute-start.4 = (bf16[6,64,384]{2,1,0:T(8,128)(2,1)S(1)}, bf16[6,64,384]{2,1,0:T(8,128)(2,1)S(1)}, u32[]{:S(2)}, u32[]{:S(2)}) collective-permute-start(bf16[6,64,384]{2,1,0:T(8,128)(2,1)S(1)} %get-tuple-element.47.to_beside), channel_id=1, source_target_pairs={{0,4},{4,0},{8,12},{12,8},{1,5},{5,1},{9,13},{13,9},{2,6},{6,2},{1... | collective-permute-start | bytes 884744 | tf_op jit(solution)/shard_map/ppermute | solution.py:273
  23.3 4.7 %collective-permute-done.7.opposite_qkv = bf16[3,64,384]{2,1,0:T(8,128)(2,1)S(1)} collective-permute-done((bf16[3,64,384]{2,1,0:T(8,128)(2,1)S(1)}, bf16[3,64,384]{2,1,0:T(8,128)(2,1)S(1)}, u32[]{:S(2)}, u32[]{:S(2)}) %collective-permute-start.7) | collective-permute-done | bytes 147488 | tf_op jit(solution)/shard_map/ppermute | solution.py:273
  28.0 3.2 %collective-permute-start.8 = (bf16[5,64,384]{2,1,0:T(8,128)(2,1)S(1)}, bf16[5,64,384]{2,1,0:T(8,128)(2,1)S(1)}, u32[]{:S(2)}, u32[]{:S(2)}) collective-permute-start(bf16[5,64,384]{2,1,0:T(8,128)(2,1)S(1)} %get-tuple-element.54), channel_id=1, source_target_pairs={{0,12},{12,0},{1,13},{13,1},{2,14},{14,2},{3,15},{15,3},{16,28},{2... | collective-permute-start | bytes 737288 | tf_op jit(solution)/shard_map/ppermute | solution.py:273
  31.2 0.1 collective-permute-start.9
  31.3 0.0 collective-permute-done.5.held_ref.mirror.mirror2
  31.3 1.3 %collective-permute-start.6 = (bf16[4,64,384]{2,1,0:T(8,128)(2,1)S(1)}, bf16[4,64,384]{2,1,0:T(8,128)(2,1)S(1)}, u32[]{:S(2)}, u32[]{:S(2)}) collective-permute-start(bf16[4,64,384]{2,1,0:T(8,128)(2,1)S(1)} %pick.1), channel_id=1, source_target_pairs={{4,0},{8,12},{5,1},{9,13},{6,2},{10,14},{7,3},{11,15},{20,16},{24,... | collective-permute-start | bytes 589832 | tf_op jit(solution)/shard_map/ppermute | solution.py:336
  32.6 10.3 %collective-permute-done.9.opposite = bf16[2,64,384]{2,1,0:T(8,128)(2,1)S(1)} collective-permute-done((bf16[2,64,384]{2,1,0:T(8,128)(2,1)S(1)}, bf16[2,64,384]{2,1,0:T(8,128)(2,1)S(1)}, u32[]{:S(2)}, u32[]{:S(2)}) %collective-permute-start.9) | collective-permute-done | bytes 98336 | tf_op jit(solution)/shard_map/ppermute | solution.py:273
  42.9 0.0 collective-permute-done.8.end
  42.9 0.0 collective-permute-done.4.beside.beside2
  42.9 2.0 %attention.1 = (bf16[3,64,384]{2,1,0:T(8,128)(2,1)S(1)}, bf16[3,64,384]{2,1,0:T(8,128)(2,1)S(1)}, bf16[3,64,384]{2,1,0:T(8,128)(2,1)S(1)}, bf16[3,64,384]{2,1,0:T(8,128)(2,1)S(1)}, bf16[4,64,384]{2,1,0:T(8,128)(2,1)S(1)}) custom-call(bf16[3,64,384]{2,1,0:T(8,128)(2,1)S(1)} %get-tuple-element.49.own_qkv, bf16[2,64,384]{2,1,0:T(8,128)(2,1)S(1)} %get-tuple-element.50.own, ...), custom_call_target="tpu_custom_call" | custom-call | flops 2013265920 | bytes 2801664 | tf_op jit(solution)/shard_map/attention/pallas_call | solution.py:42
  44.9 0.1 collective-permute-start.10
  45.0 0.5 collective-permute-start.13
  45.5 1.6 %collective-permute-start.14 = (bf16[3,64,384]{2,1,0:T(8,128)(2,1)S(1)}, bf16[3,64,384]{2,1,0:T(8,128)(2,1)S(1)}, u32[]{:S(2)}, u32[]{:S(2)}) collective-permute-start(bf16[3,64,384]{2,1,0:T(8,128)(2,1)S(1)} %get-tuple-element.63), channel_id=1, source_target_pairs={{0,8},{4,12},{8,0},{12,4},{1,9},{5,13},{9,1},{13,5},{2,10},{6,14},... | collective-permute-start | bytes 442376 | tf_op jit(solution)/shard_map/ppermute | solution.py:273
  47.1 2.4 %collective-permute-start.15 = (bf16[3,64,384]{2,1,0:T(8,128)(2,1)S(1)}, bf16[3,64,384]{2,1,0:T(8,128)(2,1)S(1)}, u32[]{:S(2)}, u32[]{:S(2)}) collective-permute-start(bf16[3,64,384]{2,1,0:T(8,128)(2,1)S(1)} %get-tuple-element.64), channel_id=1, source_target_pairs={{0,12},{4,8},{8,4},{12,0},{1,13},{5,9},{9,5},{13,1},{2,14},{6,10},... | collective-permute-start | bytes 442376 | tf_op jit(solution)/shard_map/ppermute | solution.py:273
  49.4 0.0 collective-permute-done.6.farthest
  49.4 0.0 collective-permute-done.10.act_peer
  49.4 1.5 %weight_grad.1 = (f32[3,96,384]{2,1,0:T(8,128)S(1)}, bf16[3,48,384]{2,1,0:T(8,128)(2,1)S(1)}, bf16[3,48,384]{2,1,0:T(8,128)(2,1)S(1)}, bf16[4,64,384]{2,1,0:T(8,128)(2,1)}) custom-call(bf16[7,64,384]{2,1,0:T(8,128)(2,1)S(1)} %get-tuple-element.37.cot_ref, bf16[7,64,384]{2,1,0:T(8,128)(2,1)S(1)} %collective-permute-done.beside_ref.beside_qkv.beside, ...), custom_call_target="tpu_custom_call" | custom-call | bytes 3858432 | tf_op jit(solution)/shard_map/weight_grad/pallas_call | solution.py:42
  51.0 1.5 %collective-permute-start.11 = (bf16[3,48,384]{2,1,0:T(8,128)(2,1)S(1)}, bf16[3,48,384]{2,1,0:T(8,128)(2,1)S(1)}, u32[]{:S(2)}, u32[]{:S(2)}) collective-permute-start(bf16[3,48,384]{2,1,0:T(8,128)(2,1)S(1)} %get-tuple-element.58), channel_id=1, source_target_pairs={{0,2},{2,0},{1,3},{3,1},{4,6},{6,4},{5,7},{7,5},{8,10},{10,8},{9,1... | collective-permute-start | bytes 331784 | tf_op jit(solution)/shard_map/ppermute | solution.py:273
  52.5 0.5 collective-permute-start.12
  53.0 3.8 %collective-permute-done.11.got0_ref = bf16[3,48,384]{2,1,0:T(8,128)(2,1)S(1)} collective-permute-done((bf16[3,48,384]{2,1,0:T(8,128)(2,1)S(1)}, bf16[3,48,384]{2,1,0:T(8,128)(2,1)S(1)}, u32[]{:S(2)}, u32[]{:S(2)}) %collective-permute-start.11) | collective-permute-done | bytes 110624 | tf_op jit(solution)/shard_map/ppermute | solution.py:273
  56.8 1.2 %collective-permute-done.12.got1_ref = bf16[3,48,384]{2,1,0:T(8,128)(2,1)S(1)} collective-permute-done((bf16[3,48,384]{2,1,0:T(8,128)(2,1)S(1)}, bf16[3,48,384]{2,1,0:T(8,128)(2,1)S(1)}, u32[]{:S(2)}, u32[]{:S(2)}) %collective-permute-start.12) | collective-permute-done | bytes 110624 | tf_op jit(solution)/shard_map/ppermute | solution.py:273
  57.9 0.8 %add_weight.1 = f32[3,96,384]{2,1,0:T(8,128)} custom-call(f32[3,96,384]{2,1,0:T(8,128)S(1)} %get-tuple-element.57.own_ref, bf16[3,48,384]{2,1,0:T(8,128)(2,1)S(1)} %collective-permute-done.11.got0_ref, bf16[3,48,384]{2,1,0:T(8,128)(2,1)S(1)} %collective-permute-done.12.got1_ref), custom_call_target="tpu_custom_call" | custom-call | bytes 1105920 | tf_op jit(solution)/shard_map/add_weight/pallas_call | solution.py:42
  58.8 0.0 collective-permute-done.13.refs_1_
  58.8 0.7 %collective-permute-done.14.refs_2_ = bf16[3,64,384]{2,1,0:T(8,128)(2,1)S(1)} collective-permute-done((bf16[3,64,384]{2,1,0:T(8,128)(2,1)S(1)}, bf16[3,64,384]{2,1,0:T(8,128)(2,1)S(1)}, u32[]{:S(2)}, u32[]{:S(2)}) %collective-permute-start.14) | collective-permute-done | bytes 147488 | tf_op jit(solution)/shard_map/ppermute | solution.py:273
  59.5 0.0 collective-permute-done.15.refs_3_
  59.5 0.9 %place.1 = (bf16[4,64,384]{2,1,0:T(8,128)(2,1)}, bf16[4,64,384]{2,1,0:T(8,128)(2,1)}, bf16[4,64,384]{2,1,0:T(8,128)(2,1)}) custom-call(bf16[3,64,384]{2,1,0:T(8,128)(2,1)S(1)} %get-tuple-element.61.refs_0_, bf16[3,64,384]{2,1,0:T(8,128)(2,1)S(1)} %collective-permute-done.13.refs_1_, bf16[3,64,384]{2,1,0:T(8,128)(2,1)S(1)} %collective-permute-done.14.refs_2_, ...), custom_call_target="tpu_custom_call" | custom-call | bytes 1179648 | tf_op jit(solution)/shard_map/place/pallas_call | solution.py:42
  (1 shorter events, 0.0 us)
Async XLA Ops:
  1.8 8.9 %collective-permute-start.1 = (bf16[7,64,384]{2,1,0:T(8,128)(2,1)S(1)}, bf16[7,64,384]{2,1,0:T(8,128)(2,1)S(1)}, u32[]{:S(2)}, u32[]{:S(2)}) collective-permute-start(bf16[7,64,384]{2,1,0:T(8,128)(2,1)S(1)} %get-tuple-element.38.to_mirror), channel_id=1, source_target_pairs={{4,8},{8,4},{5,9},{9,5},{6,10},{10,6},{7,11},{11,7},{20,24},{24,20... | collective-permute-start | bytes 1032200 | tf_op jit(solution)/shard_map/ppermute | solution.py:273
  2.5 13.7 %collective-permute-start = (bf16[7,64,384]{2,1,0:T(8,128)(2,1)S(1)}, bf16[7,64,384]{2,1,0:T(8,128)(2,1)S(1)}, u32[]{:S(2)}, u32[]{:S(2)}) collective-permute-start(bf16[7,64,384]{2,1,0:T(8,128)(2,1)S(1)} %get-tuple-element.37.cot_ref), channel_id=1, source_target_pairs={{0,4},{4,0},{8,12},{12,8},{1,5},{5,1},{9,13},{13,9},{2,6},{6,2},{1... | collective-permute-start | bytes 1032200 | tf_op jit(solution)/shard_map/ppermute | solution.py:273
  16.6 2.6 %collective-permute-start.2 = (bf16[4,64,384]{2,1,0:T(8,128)(2,1)S(1)}, bf16[4,64,384]{2,1,0:T(8,128)(2,1)S(1)}, u32[]{:S(2)}, u32[]{:S(2)}) collective-permute-start(bf16[4,64,384]{2,1,0:T(8,128)(2,1)S(1)} %conv_other.1), channel_id=1, source_target_pairs={{0,1},{1,0},{2,3},{3,2},{4,5},{5,4},{6,7},{7,6},{8,9},{9,8},{10,11... | collective-permute-start | bytes 589832 | tf_op jit(solution)/shard_map/ppermute | solution.py:273
  16.7 2.5 %collective-permute-start.3 = (bf16[2,64,384]{2,1,0:T(8,128)(2,1)S(1)}, bf16[2,64,384]{2,1,0:T(8,128)(2,1)S(1)}, u32[]{:S(2)}, u32[]{:S(2)}) collective-permute-start(bf16[2,64,384]{2,1,0:T(8,128)(2,1)S(1)} %get-tuple-element.46), channel_id=1, source_target_pairs={{0,1},{1,0},{2,3},{3,2},{4,5},{5,4},{6,7},{7,6},{8,9},{9,8},{10,11... | collective-permute-start | bytes 294920 | tf_op jit(solution)/shard_map/ppermute | solution.py:273
  17.2 10.8 %collective-permute-start.7 = (bf16[3,64,384]{2,1,0:T(8,128)(2,1)S(1)}, bf16[3,64,384]{2,1,0:T(8,128)(2,1)S(1)}, u32[]{:S(2)}, u32[]{:S(2)}) collective-permute-start(bf16[3,64,384]{2,1,0:T(8,128)(2,1)S(1)} %get-tuple-element.51), channel_id=1, source_target_pairs={{0,8},{4,12},{8,0},{12,4},{1,9},{5,13},{9,1},{13,5},{2,10},{6,14},... | collective-permute-start | bytes 442376 | tf_op jit(solution)/shard_map/ppermute | solution.py:273
  19.4 11.9 %collective-permute-start.5 = (bf16[6,64,384]{2,1,0:T(8,128)(2,1)S(1)}, bf16[6,64,384]{2,1,0:T(8,128)(2,1)S(1)}, u32[]{:S(2)}, u32[]{:S(2)}) collective-permute-start(bf16[6,64,384]{2,1,0:T(8,128)(2,1)S(1)} %get-tuple-element.48.to_mirror), channel_id=1, source_target_pairs={{4,8},{8,4},{5,9},{9,5},{6,10},{10,6},{7,11},{11,7},{20,24},{24,20... | collective-permute-start | bytes 884744 | tf_op jit(solution)/shard_map/ppermute | solution.py:273
  20.1 22.8 %collective-permute-start.4 = (bf16[6,64,384]{2,1,0:T(8,128)(2,1)S(1)}, bf16[6,64,384]{2,1,0:T(8,128)(2,1)S(1)}, u32[]{:S(2)}, u32[]{:S(2)}) collective-permute-start(bf16[6,64,384]{2,1,0:T(8,128)(2,1)S(1)} %get-tuple-element.47.to_beside), channel_id=1, source_target_pairs={{0,4},{4,0},{8,12},{12,8},{1,5},{5,1},{9,13},{13,9},{2,6},{6,2},{1... | collective-permute-start | bytes 884744 | tf_op jit(solution)/shard_map/ppermute | solution.py:273
  28.0 14.9 %collective-permute-start.8 = (bf16[5,64,384]{2,1,0:T(8,128)(2,1)S(1)}, bf16[5,64,384]{2,1,0:T(8,128)(2,1)S(1)}, u32[]{:S(2)}, u32[]{:S(2)}) collective-permute-start(bf16[5,64,384]{2,1,0:T(8,128)(2,1)S(1)} %get-tuple-element.54), channel_id=1, source_target_pairs={{0,12},{12,0},{1,13},{13,1},{2,14},{14,2},{3,15},{15,3},{16,28},{2... | collective-permute-start | bytes 737288 | tf_op jit(solution)/shard_map/ppermute | solution.py:273
  31.2 11.7 %collective-permute-start.9 = (bf16[2,64,384]{2,1,0:T(8,128)(2,1)S(1)}, bf16[2,64,384]{2,1,0:T(8,128)(2,1)S(1)}, u32[]{:S(2)}, u32[]{:S(2)}) collective-permute-start(bf16[2,64,384]{2,1,0:T(8,128)(2,1)S(1)} %get-tuple-element.55.to_opposite), channel_id=1, source_target_pairs={{0,8},{4,12},{8,0},{12,4},{1,9},{5,13},{9,1},{13,5},{2,10},{6,14},... | collective-permute-start | bytes 294920 | tf_op jit(solution)/shard_map/ppermute | solution.py:273
  31.3 18.1 %collective-permute-start.6 = (bf16[4,64,384]{2,1,0:T(8,128)(2,1)S(1)}, bf16[4,64,384]{2,1,0:T(8,128)(2,1)S(1)}, u32[]{:S(2)}, u32[]{:S(2)}) collective-permute-start(bf16[4,64,384]{2,1,0:T(8,128)(2,1)S(1)} %pick.1), channel_id=1, source_target_pairs={{4,0},{8,12},{5,1},{9,13},{6,2},{10,14},{7,3},{11,15},{20,16},{24,... | collective-permute-start | bytes 589832 | tf_op jit(solution)/shard_map/ppermute | solution.py:336
  44.9 4.5 %collective-permute-start.10 = (bf16[4,64,384]{2,1,0:T(8,128)(2,1)S(1)}, bf16[4,64,384]{2,1,0:T(8,128)(2,1)S(1)}, u32[]{:S(2)}, u32[]{:S(2)}) collective-permute-start(bf16[4,64,384]{2,1,0:T(8,128)(2,1)S(1)} %get-tuple-element.56.act_ref), channel_id=1, source_target_pairs={{0,1},{1,0},{2,3},{3,2},{4,5},{5,4},{6,7},{7,6},{8,9},{9,8},{10,11... | collective-permute-start | bytes 589832 | tf_op jit(solution)/shard_map/ppermute | solution.py:273
  45.0 13.8 %collective-permute-start.13 = (bf16[3,64,384]{2,1,0:T(8,128)(2,1)S(1)}, bf16[3,64,384]{2,1,0:T(8,128)(2,1)S(1)}, u32[]{:S(2)}, u32[]{:S(2)}) collective-permute-start(bf16[3,64,384]{2,1,0:T(8,128)(2,1)S(1)} %get-tuple-element.62), channel_id=1, source_target_pairs={{0,4},{4,0},{8,12},{12,8},{1,5},{5,1},{9,13},{13,9},{2,6},{6,2},{1... | collective-permute-start | bytes 442376 | tf_op jit(solution)/shard_map/ppermute | solution.py:273
  45.5 14.0 %collective-permute-start.14 = (bf16[3,64,384]{2,1,0:T(8,128)(2,1)S(1)}, bf16[3,64,384]{2,1,0:T(8,128)(2,1)S(1)}, u32[]{:S(2)}, u32[]{:S(2)}) collective-permute-start(bf16[3,64,384]{2,1,0:T(8,128)(2,1)S(1)} %get-tuple-element.63), channel_id=1, source_target_pairs={{0,8},{4,12},{8,0},{12,4},{1,9},{5,13},{9,1},{13,5},{2,10},{6,14},... | collective-permute-start | bytes 442376 | tf_op jit(solution)/shard_map/ppermute | solution.py:273
  47.1 12.4 %collective-permute-start.15 = (bf16[3,64,384]{2,1,0:T(8,128)(2,1)S(1)}, bf16[3,64,384]{2,1,0:T(8,128)(2,1)S(1)}, u32[]{:S(2)}, u32[]{:S(2)}) collective-permute-start(bf16[3,64,384]{2,1,0:T(8,128)(2,1)S(1)} %get-tuple-element.64), channel_id=1, source_target_pairs={{0,12},{4,8},{8,4},{12,0},{1,13},{5,9},{9,5},{13,1},{2,14},{6,10},... | collective-permute-start | bytes 442376 | tf_op jit(solution)/shard_map/ppermute | solution.py:273
  51.0 5.8 %collective-permute-start.11 = (bf16[3,48,384]{2,1,0:T(8,128)(2,1)S(1)}, bf16[3,48,384]{2,1,0:T(8,128)(2,1)S(1)}, u32[]{:S(2)}, u32[]{:S(2)}) collective-permute-start(bf16[3,48,384]{2,1,0:T(8,128)(2,1)S(1)} %get-tuple-element.58), channel_id=1, source_target_pairs={{0,2},{2,0},{1,3},{3,1},{4,6},{6,4},{5,7},{7,5},{8,10},{10,8},{9,1... | collective-permute-start | bytes 331784 | tf_op jit(solution)/shard_map/ppermute | solution.py:273
  52.5 5.5 %collective-permute-start.12 = (bf16[3,48,384]{2,1,0:T(8,128)(2,1)S(1)}, bf16[3,48,384]{2,1,0:T(8,128)(2,1)S(1)}, u32[]{:S(2)}, u32[]{:S(2)}) collective-permute-start(bf16[3,48,384]{2,1,0:T(8,128)(2,1)S(1)} %get-tuple-element.59), channel_id=1, source_target_pairs={{0,2},{2,0},{1,3},{3,1},{4,6},{6,4},{5,7},{7,5},{8,10},{10,8},{9,1... | collective-permute-start | bytes 331784 | tf_op jit(solution)/shard_map/ppermute | solution.py:273

commit v5 on v4

--- a/solution.py
+++ b/solution.py
@@ -113,18 +113,25 @@
     )
 
 
-def centre_kernel(cot_ref, w_ref, mine_ref, other_ref):
+def chosen(block, act_ref, act_peer):
+    k = lax.rem(block, 2)
+    return jnp.where(lax.div(block, 2) == lax.axis_index("chan"), act_ref[k], act_peer[k])
+
+
+def centre_kernel(cot_ref, w_ref, qkv, act_ref, act_peer, mine_ref, other_ref, opposite):
     c = lax.axis_index("chan")
     blocks = cot_ref.shape[0] - 3
+    opposite[:3] = qkv[...]
+    opposite[3] = chosen(lax.axis_index("seq") ^ 2, act_ref, act_peer)
     tap = cot_ref[:blocks].reshape(mine_ref.shape)
     mine_ref[...] = conv_term(tap, w_ref, 1, c)
     other_ref[...] = conv_term(tap, w_ref, 1, 1 - c)
 
 
-def conv_kernel(mine, beside_ref, mirror_ref, w_ref, centre_ref, out_ref):
+def conv_kernel(mine, beside_ref, mirror_ref, w_ref, centre_ref, *outs):
     c = lax.axis_index("chan")
     even = lax.rem(lax.axis_index("seq"), 2) == 0
-    blocks = out_ref.shape[0]
+    blocks = beside_ref.shape[0] - 3
     beside = beside_ref[:blocks].reshape(centre_ref.shape)
     mirror = mirror_ref[:blocks].reshape(centre_ref.shape)
     side = c if mine else 1 - c
@@ -132,23 +139,26 @@
         centre_ref[...]
         + conv_term(jnp.where(even, beside, mirror), w_ref, 0, side)
         + conv_term(jnp.where(even, mirror, beside), w_ref, 2, side)
-    )
-    out_ref[...] = total.astype(BF).reshape(out_ref.shape)
+    ).astype(BF)
+    rows = total.shape[0] // len(outs)
+    for i, out in enumerate(outs):
+        out[...] = total[i * rows : (i + 1) * rows].reshape(out.shape)
 
 
 def grad_kernel(
-    cot_ref, slope_ref, mine_ref, got_ref, act_ref, act_peer, beside_ref, mirror_ref, to_mirror,
-    own, beside, opposite, mirror, end,
+    cot_ref, slope_ref, mine_ref, got0_ref, got1_ref, act_ref, act_peer, beside_ref, mirror_ref,
+    to_mirror, own, beside, opposite, mirror, end,
 ):
     s = lax.axis_index("seq")
-    c = lax.axis_index("chan")
     blocks = mine_ref.shape[0]
     for d, out in ((1, beside), (3, mirror), (2, opposite), (0, own)):
         b = s ^ d
-        back = mine_ref[b].astype(F32) + got_ref[b].astype(F32)
+        i = lax.rem(b, 2)
+        got = jnp.where(b < 2, got0_ref[i], got1_ref[i])
+        back = mine_ref[b].astype(F32) + got.astype(F32)
         out[0] = (cot_ref[b].astype(F32) + back * slope_ref[b]).astype(BF)
-        k = lax.rem(b, 2)
-        out[1] = jnp.where(lax.div(b, 2) == c, act_ref[k], act_peer[k])
+        if d != 2:
+            out[1] = chosen(b, act_ref, act_peer)
     end[:3] = to_mirror[blocks:]
     end[3:] = mirror[:2]
     beside[2:] = mirror_ref[:blocks]
@@ -157,6 +167,11 @@
 
 def pick_kernel(held_ref, out_ref):
     out_ref[...] = held_ref[2:]
+
+
+def gather_kernel(own, beside, opposite, out_ref):
+    for d, piece in enumerate((own[1], beside[1], opposite[3])):
+        out_ref[d] = piece
 
 
 def attention_kernel(
@@ -174,13 +189,8 @@
         return jnp.concatenate([own_qkv[j], beside_qkv[near + j], opposite_qkv[j], facing], axis=0)
 
     query, key, value = (positions(j) for j in range(3))
-    grad, act = (
-        (own[j], beside[j], opposite[j], jnp.where(at_end, end[3 + j], mirror[j]))
-        for j in range(2)
-    )
-    grad = jnp.concatenate(grad, axis=0)
-    for d in range(count):
-        act_ref[d] = act[d]
+    facing, act_ref[0] = (jnp.where(at_end, end[3 + j], mirror[j]) for j in range(2))
+    grad = jnp.concatenate([own[0], beside[0], opposite[0], facing], axis=0)
     nt = (((1,), (1,)), ((), ()))
     nn = (((1,), (0,)), ((), ()))
     tn = (((0,), (0,)), ((), ()))
@@ -205,8 +215,8 @@
 
 
 def weight_kernel(
-    count, factor, cot_ref, beside, mirror, beside2, mirror2, farthest, act_ref, act_peer, own,
-    to_beside, to_opposite, to_mirror, own_ref, sent0_ref, sent1_ref, grad_ref, act_buf, cot_buf,
+    count, factor, cot_ref, beside, mirror, beside2, mirror2, farthest, act_ref, act_peer,
+    act_last, peer_last, own, to_beside, to_opposite, to_mirror, own_ref, sent0_ref, sent1_ref, grad_ref, act_buf, cot_buf,
 ):
     s = lax.axis_index("seq")
     c = lax.axis_index("chan")
@@ -216,10 +226,8 @@
         grad_ref[s ^ d] = piece[0]
     lanes = act_buf.shape[2] // 2
     for d in range(count):
-        halves = (
-            jnp.where(c == 0, act_ref[d], act_peer[d]),
-            jnp.where(c == 0, act_peer[d], act_ref[d]),
-        )
+        held, came = (act_ref[d], act_peer[d]) if d < 3 else (act_last[0], peer_last[0])
+        halves = jnp.where(c == 0, held, came), jnp.where(c == 0, came, held)
         for r in range(width // lanes):
             for h in range(2):
                 act_buf[s ^ d, pl.ds(r * rows, rows), pl.ds(h * lanes, lanes)] = halves[h][
@@ -300,7 +308,7 @@
     beside = swap(to_beside, "seq", 1)
     mirror = swap(to_mirror, "seq", 3, middle)
     (hidden,) = after(to_beside, hidden)
-    own_qkv, to_opposite, weights, slope, act, act_sent = kernel_call(
+    own_qkv, opposite_qkv, weights, slope, act, act_sent = kernel_call(
         rest_kernel,
         [units(3)] * 2 + [shape(weights.shape), shape(hidden.shape, F32), units(2), units(2)],
         name="rest",
@@ -308,25 +316,24 @@
         space=pltpu.HBM,
     )(hidden, query_vectors, key_vectors, value_vectors, weights)
     act_got = swap(act_sent, "chan", 1)
+    flat = shape((tokens, width), F32)
+    centre_mine, centre_other, to_opposite = kernel_call(
+        centre_kernel, [flat, flat, units(4)], name="conv_centre"
+    )(to_beside, weights, opposite_qkv, act, act_got)
     opposite = swap(to_opposite, "seq", 2)
-
-    flat = shape((tokens, width), F32)
-    centre_mine, centre_other = kernel_call(centre_kernel, [flat] * 2, name="conv_centre")(
-        to_beside, weights
-    )
-    (other,) = kernel_call(
-        functools.partial(conv_kernel, False), [units(blocks)], name="conv_other"
+    others = kernel_call(
+        functools.partial(conv_kernel, False), [units(blocks // 2)] * 2, name="conv_other"
     )(beside, mirror, weights, centre_other)
-    got = swap(other, "chan", 1)
-    (centre_mine,) = after(other, centre_mine)
+    got = [swap(x, "chan", 1) for x in others]
+    (centre_mine,) = after(others[0], centre_mine)
     (mine,) = kernel_call(functools.partial(conv_kernel, True), [units(blocks)], name="conv_mine")(
         beside, mirror, weights, centre_mine
     )
     own, to_beside2, to_opposite2, to_mirror2, to_end2 = kernel_call(
         grad_kernel,
-        [units(2), units(blocks + 2), units(2), units(blocks + 2), units(5)],
+        [units(2), units(blocks + 2), units(1), units(blocks + 2), units(5)],
         name="hidden_grad",
-    )(to_beside, slope, mine, got, act, act_got, beside, mirror, to_mirror)
+    )(to_beside, slope, mine, *got, act, act_got, beside, mirror, to_mirror)
     beside2 = swap(to_beside2, "seq", 1)
     mirror2 = swap(to_mirror2, "seq", 3, middle)
     far_opposite, far_end = after(opposite, to_opposite2, to_end2)
@@ -335,17 +342,21 @@
     (far,) = kernel_call(pick_kernel, [units(blocks)], name="pick")(mirror2)
     farthest = lax.ppermute(far, "seq", [(1, 0), (2, 3)])
 
+    (act_held,) = kernel_call(gather_kernel, [units(3)], name="gather")(own, beside2, opposite)
+    act_peer = swap(act_held, "chan", 1)
+    (own_qkv,) = after(act_held, own_qkv)
+
     item = 5 * (count * rows) ** 2 * width
-    *returned, act_held = kernel_call(
+    *returned, act_last = kernel_call(
         functools.partial(attention_kernel, count),
-        [units(3)] * count + [units(count)],
+        [units(3)] * count + [units(1)],
         flops=COST * 2 * item,
         transcendentals=(count * rows) ** 2 * (width // HD),
         name="attention",
     )(own_qkv, own, beside, mirror, opposite, end2, beside2, mirror2, opposite2)
     back = [returned[0]] + [swap(returned[d], "seq", d) for d in range(1, count)]
 
-    act_peer = swap(act_held, "chan", 1)
+    peer_last = swap(act_last, "chan", 1)
     total, sent0, sent1, hidden_grad = kernel_call(
         functools.partial(weight_kernel, count, factor),
         [shape((3, part // 2, width), F32)] + [shape((3, part // 4, width))] * 2 + [units(blocks)],
@@ -355,8 +366,8 @@
             pltpu.VMEM((count, tokens, width), BF),
         ],
     )(
-        to_beside, beside, mirror, beside2, mirror2, farthest, act_held, act_peer, own, to_beside2,
-        to_opposite2, to_mirror2,
+        to_beside, beside, mirror, beside2, mirror2, farthest, act_held, act_peer, act_last,
+        peer_last, own, to_beside2, to_opposite2, to_mirror2,
     )
     got_sums = [swap(x, "batch", 1) for x in (sent0, sent1)]
     (weight_grad,) = kernel_call(add_kernel, [shape((3, part // 2, width), F32)], name="add_weight")(

time: 60.6 us -> 58.2 us (0.960)
  waiting for transfers between devices: 26.2 us -> 24.6 us
  starting transfers between devices: 23.7 us -> 22.9 us
    ppermute x15 -> x17, waiting for transfers between devices: 26.2 us -> 24.6 us  [swap(): lax.ppermute(x, axis, [(i, i ^ by) for i in range(n) if only is None or i...]
    ppermute x15 -> x17, starting transfers between devices: 22.5 us -> 21.6 us  [swap(): lax.ppermute(x, axis, [(i, i ^ by) for i in range(n) if only is None or i...]
    pallas_call x11 -> x12, Pallas kernels: 9.67 us -> 9.69 us  [call(): pl.pallas_call(body, out_shape=list(outs), in_specs=[given] * len(args),...]
  transfers between devices with their start and end apart: 16 -> 18, of which waited for: 6 -> 10; matrix products, arithmetic and copies ran while one was open for 0% -> 0% of each run, Pallas kernels for 12% -> 13%
where the time goes in v5:
time: 58.2 us; the launch traced here: 57.9 us
  waiting for transfers between devices  24.6 us (42%)
  starting transfers between devices  22.9 us (39%)
  Pallas kernels  9.69 us (17%)
  between operations  0.78 us (1%)
    ppermute x17, waiting for transfers between devices, swap(): lax.ppermute(x, axis, [(i, i ^ by) for i in range(n) if only is None or i...  24.6 us
    ppermute x17, starting transfers between devices, swap(): lax.ppermute(x, axis, [(i, i ^ by) for i in range(n) if only is None or i...  21.6 us
    pallas_call x12, Pallas kernels, call(): pl.pallas_call(body, out_shape=list(outs), in_specs=[given] * len(args),...  9.69 us
    ppermute x1, starting transfers between devices, per_device(): farthest = lax.ppermute(far, 'seq', [(1, 0), (2, 3)])  1.29 us
  transfers between devices with their start and end apart: 18, of which 10 were waited for; matrix products, arithmetic and copies ran while one was open for 0% of the time, Pallas kernels for 13%

profile of v5, /device:TPU:0, one launch (start us, length us, event | category | flops | bytes accessed | tf_op | source)
XLA Modules:
  0.0 57.9 jit_solution(159187567903948604)
XLA Ops:
  0.6 1.2 %near.1 = (bf16[7,64,384]{2,1,0:T(8,128)(2,1)S(1)}, bf16[7,64,384]{2,1,0:T(8,128)(2,1)S(1)}) custom-call(bf16[4,64,384]{2,1,0:T(8,128)(2,1)} %cot.1, bf16[4,64,384]{2,1,0:T(8,128)(2,1)} %q.3, bf16[4,64,384]{2,1,0:T(8,128)(2,1)} %k.3, bf16[4,64,384]{2,1,0:T(8,128)(2,1)} %v.3), custom_call_target="tpu_custom_call" | custom-call | bytes 1474560 | tf_op jit(solution)/shard_map/near/pallas_call | solution.py:42
  1.8 0.7 %collective-permute-start.1 = (bf16[7,64,384]{2,1,0:T(8,128)(2,1)S(1)}, bf16[7,64,384]{2,1,0:T(8,128)(2,1)S(1)}, u32[]{:S(2)}, u32[]{:S(2)}) collective-permute-start(bf16[7,64,384]{2,1,0:T(8,128)(2,1)S(1)} %get-tuple-element.42.to_mirror), channel_id=1, source_target_pairs={{4,8},{8,4},{5,9},{9,5},{6,10},{10,6},{7,11},{11,7},{20,24},{24,20... | collective-permute-start | bytes 1032200 | tf_op jit(solution)/shard_map/ppermute | solution.py:281
  2.5 5.9 %collective-permute-start = (bf16[7,64,384]{2,1,0:T(8,128)(2,1)S(1)}, bf16[7,64,384]{2,1,0:T(8,128)(2,1)S(1)}, u32[]{:S(2)}, u32[]{:S(2)}) collective-permute-start(bf16[7,64,384]{2,1,0:T(8,128)(2,1)S(1)} %get-tuple-element.41.cot_ref), channel_id=1, source_target_pairs={{0,4},{4,0},{8,12},{12,8},{1,5},{5,1},{9,13},{13,9},{2,6},{6,2},{1... | collective-permute-start | bytes 1032200 | tf_op jit(solution)/shard_map/ppermute | solution.py:281
  8.4 1.8 %rest.1 = (bf16[3,64,384]{2,1,0:T(8,128)(2,1)S(1)}, bf16[3,64,384]{2,1,0:T(8,128)(2,1)S(1)}, bf16[3,768,384]{2,1,0:T(8,128)(2,1)S(1)}, f32[4,64,384]{2,1,0:T(8,1...) custom-call(bf16[4,64,384]{2,1,0:T(8,128)(2,1)} %hidden, bf16[4,64,384]{2,1,0:T(8,128)(2,1)} %q.3, ...), custom_call_target="tpu_custom_call" | custom-call | bytes 5210112 | tf_op jit(solution)/shard_map/rest/pallas_call | solution.py:42
  10.2 0.1 collective-permute-start.2
  10.3 1.3 %collective-permute-done.2.act_peer = bf16[2,64,384]{2,1,0:T(8,128)(2,1)S(1)} collective-permute-done((bf16[2,64,384]{2,1,0:T(8,128)(2,1)S(1)}, bf16[2,64,384]{2,1,0:T(8,128)(2,1)S(1)}, u32[]{:S(2)}, u32[]{:S(2)}) %collective-permute-start.2) | collective-permute-done | bytes 98336 | tf_op jit(solution)/shard_map/ppermute | solution.py:281
  11.6 0.4 conv_centre.1
  12.0 0.1 collective-permute-start.8
  12.1 0.0 collective-permute-done.1.mirror_ref.mirror_qkv.mirror
  12.1 4.8 %collective-permute-done.beside_ref.beside_qkv.beside = bf16[7,64,384]{2,1,0:T(8,128)(2,1)S(1)} collective-permute-done((bf16[7,64,384]{2,1,0:T(8,128)(2,1)S(1)}, bf16[7,64,384]{2,1,0:T(8,128)(2,1)S(1)}, u32[]{:S(2)}, u32[]{:S(2)}) %collective-permute-start) | collective-permute-done | bytes 344096 | tf_op jit(solution)/shard_map/ppermute | solution.py:281
  16.9 0.4 conv_other.1
  17.3 0.1 collective-permute-start.4
  17.4 0.5 collective-permute-start.3
  17.9 0.4 conv_mine.1.mine_ref
  18.3 0.4 collective-permute-done.4.got1_ref
  18.7 0.2 collective-permute-done.3.got0_ref
  18.8 0.2 hidden_grad.1
  19.0 2.6 %collective-permute-start.5 = (bf16[6,64,384]{2,1,0:T(8,128)(2,1)S(1)}, bf16[6,64,384]{2,1,0:T(8,128)(2,1)S(1)}, u32[]{:S(2)}, u32[]{:S(2)}) collective-permute-start(bf16[6,64,384]{2,1,0:T(8,128)(2,1)S(1)} %get-tuple-element.54.to_beside), channel_id=1, source_target_pairs={{0,4},{4,0},{8,12},{12,8},{1,5},{5,1},{9,13},{13,9},{2,6},{6,2},{1... | collective-permute-start | bytes 884744 | tf_op jit(solution)/shard_map/ppermute | solution.py:281
  21.6 0.7 %collective-permute-start.6 = (bf16[6,64,384]{2,1,0:T(8,128)(2,1)S(1)}, bf16[6,64,384]{2,1,0:T(8,128)(2,1)S(1)}, u32[]{:S(2)}, u32[]{:S(2)}) collective-permute-start(bf16[6,64,384]{2,1,0:T(8,128)(2,1)S(1)} %get-tuple-element.55.to_mirror), channel_id=1, source_target_pairs={{4,8},{8,4},{5,9},{9,5},{6,10},{10,6},{7,11},{11,7},{20,24},{24,20... | collective-permute-start | bytes 884744 | tf_op jit(solution)/shard_map/ppermute | solution.py:281
  22.2 2.3 %collective-permute-done.8.opposite.opposite_qkv = bf16[4,64,384]{2,1,0:T(8,128)(2,1)S(1)} collective-permute-done((bf16[4,64,384]{2,1,0:T(8,128)(2,1)S(1)}, bf16[4,64,384]{2,1,0:T(8,128)(2,1)S(1)}, u32[]{:S(2)}, u32[]{:S(2)}) %collective-permute-start.8) | collective-permute-done | bytes 196640 | tf_op jit(solution)/shard_map/ppermute | solution.py:281
  24.5 4.4 %collective-permute-start.10 = (bf16[5,64,384]{2,1,0:T(8,128)(2,1)S(1)}, bf16[5,64,384]{2,1,0:T(8,128)(2,1)S(1)}, u32[]{:S(2)}, u32[]{:S(2)}) collective-permute-start(bf16[5,64,384]{2,1,0:T(8,128)(2,1)S(1)} %get-tuple-element.62), channel_id=1, source_target_pairs={{0,12},{12,0},{1,13},{13,1},{2,14},{14,2},{3,15},{15,3},{16,28},{2... | collective-permute-start | bytes 737288 | tf_op jit(solution)/shard_map/ppermute | solution.py:281
  28.9 0.1 collective-permute-start.11
  29.0 1.8 %collective-permute-done.5.beside.beside2 = bf16[6,64,384]{2,1,0:T(8,128)(2,1)S(1)} collective-permute-done((bf16[6,64,384]{2,1,0:T(8,128)(2,1)S(1)}, bf16[6,64,384]{2,1,0:T(8,128)(2,1)S(1)}, u32[]{:S(2)}, u32[]{:S(2)}) %collective-permute-start.5) | collective-permute-done | bytes 294944 | tf_op jit(solution)/shard_map/ppermute | solution.py:281
  30.8 0.1 collective-permute-start.9
  30.9 0.0 collective-permute-done.6.held_ref.mirror.mirror2
  30.9 1.3 %collective-permute-start.7 = (bf16[4,64,384]{2,1,0:T(8,128)(2,1)S(1)}, bf16[4,64,384]{2,1,0:T(8,128)(2,1)S(1)}, u32[]{:S(2)}, u32[]{:S(2)}) collective-permute-start(bf16[4,64,384]{2,1,0:T(8,128)(2,1)S(1)} %pick.1), channel_id=1, source_target_pairs={{4,0},{8,12},{5,1},{9,13},{6,2},{10,14},{7,3},{11,15},{20,16},{24,... | collective-permute-start | bytes 589832 | tf_op jit(solution)/shard_map/ppermute | solution.py:343
  32.2 7.3 %collective-permute-done.11.opposite = bf16[1,64,384]{2,1,0:T(8,128)(2,1)S(1)} collective-permute-done((bf16[1,64,384]{2,1,0:T(8,128)(2,1)S(1)}, bf16[1,64,384]{2,1,0:T(8,128)(2,1)S(1)}, u32[]{:S(2)}, u32[]{:S(2)}) %collective-permute-start.11) | collective-permute-done | bytes 49184 | tf_op jit(solution)/shard_map/ppermute | solution.py:281
  39.5 0.0 collective-permute-done.10.end
  39.5 2.0 %attention.1 = (bf16[3,64,384]{2,1,0:T(8,128)(2,1)S(1)}, bf16[3,64,384]{2,1,0:T(8,128)(2,1)S(1)}, bf16[3,64,384]{2,1,0:T(8,128)(2,1)S(1)}, bf16[3,64,384]{2,1,0:T(8,128)(2,1)S(1)}, bf16[1,64,384]{2,1,0:T(8,128)(2,1)S(1)}) custom-call(bf16[3,64,384]{2,1,0:T(8,128)(2,1)S(1)} %get-tuple-element.59.own_qkv, bf16[2,64,384]{2,1,0:T(8,128)(2,1)S(1)} %get-tuple-element.56.own, ...), custom_call_target="tpu_custom_call" | custom-call | flops 2013265920 | bytes 2654208 | tf_op jit(solution)/shard_map/attention/pallas_call | solution.py:42
  41.5 0.1 collective-permute-start.12
  41.6 1.5 %collective-permute-start.15 = (bf16[3,64,384]{2,1,0:T(8,128)(2,1)S(1)}, bf16[3,64,384]{2,1,0:T(8,128)(2,1)S(1)}, u32[]{:S(2)}, u32[]{:S(2)}) collective-permute-start(bf16[3,64,384]{2,1,0:T(8,128)(2,1)S(1)} %get-tuple-element.70), channel_id=1, source_target_pairs={{0,4},{4,0},{8,12},{12,8},{1,5},{5,1},{9,13},{13,9},{2,6},{6,2},{1... | collective-permute-start | bytes 442376 | tf_op jit(solution)/shard_map/ppermute | solution.py:281
  43.1 1.3 %collective-permute-start.16 = (bf16[3,64,384]{2,1,0:T(8,128)(2,1)S(1)}, bf16[3,64,384]{2,1,0:T(8,128)(2,1)S(1)}, u32[]{:S(2)}, u32[]{:S(2)}) collective-permute-start(bf16[3,64,384]{2,1,0:T(8,128)(2,1)S(1)} %get-tuple-element.71), channel_id=1, source_target_pairs={{0,8},{4,12},{8,0},{12,4},{1,9},{5,13},{9,1},{13,5},{2,10},{6,14},... | collective-permute-start | bytes 442376 | tf_op jit(solution)/shard_map/ppermute | solution.py:281
  44.4 0.0 collective-permute-done.12.peer_last
  44.4 1.7 %collective-permute-start.17 = (bf16[3,64,384]{2,1,0:T(8,128)(2,1)S(1)}, bf16[3,64,384]{2,1,0:T(8,128)(2,1)S(1)}, u32[]{:S(2)}, u32[]{:S(2)}) collective-permute-start(bf16[3,64,384]{2,1,0:T(8,128)(2,1)S(1)} %get-tuple-element.72), channel_id=1, source_target_pairs={{0,12},{4,8},{8,4},{12,0},{1,13},{5,9},{9,5},{13,1},{2,14},{6,10},... | collective-permute-start | bytes 442376 | tf_op jit(solution)/shard_map/ppermute | solution.py:281
  46.1 0.0 collective-permute-done.9.act_peer
  46.1 0.0 collective-permute-done.7.farthest
  46.1 1.5 %weight_grad.1 = (f32[3,96,384]{2,1,0:T(8,128)S(1)}, bf16[3,48,384]{2,1,0:T(8,128)(2,1)S(1)}, bf16[3,48,384]{2,1,0:T(8,128)(2,1)S(1)}, bf16[4,64,384]{2,1,0:T(8,128)(2,1)}) custom-call(bf16[7,64,384]{2,1,0:T(8,128)(2,1)S(1)} %get-tuple-element.41.cot_ref, bf16[7,64,384]{2,1,0:T(8,128)(2,1)S(1)} %collective-permute-done.beside_ref.beside_qkv.beside, ...), custom_call_target="tpu_custom_call" | custom-call | bytes 3809280 | tf_op jit(solution)/shard_map/weight_grad/pallas_call | solution.py:42
  47.6 1.5 %collective-permute-start.13 = (bf16[3,48,384]{2,1,0:T(8,128)(2,1)S(1)}, bf16[3,48,384]{2,1,0:T(8,128)(2,1)S(1)}, u32[]{:S(2)}, u32[]{:S(2)}) collective-permute-start(bf16[3,48,384]{2,1,0:T(8,128)(2,1)S(1)} %get-tuple-element.66), channel_id=1, source_target_pairs={{0,2},{2,0},{1,3},{3,1},{4,6},{6,4},{5,7},{7,5},{8,10},{10,8},{9,1... | collective-permute-start | bytes 331784 | tf_op jit(solution)/shard_map/ppermute | solution.py:281
  49.1 0.5 collective-permute-start.14
  49.6 3.8 %collective-permute-done.13.got0_ref = bf16[3,48,384]{2,1,0:T(8,128)(2,1)S(1)} collective-permute-done((bf16[3,48,384]{2,1,0:T(8,128)(2,1)S(1)}, bf16[3,48,384]{2,1,0:T(8,128)(2,1)S(1)}, u32[]{:S(2)}, u32[]{:S(2)}) %collective-permute-start.13) | collective-permute-done | bytes 110624 | tf_op jit(solution)/shard_map/ppermute | solution.py:281
  53.4 1.2 %collective-permute-done.14.got1_ref = bf16[3,48,384]{2,1,0:T(8,128)(2,1)S(1)} collective-permute-done((bf16[3,48,384]{2,1,0:T(8,128)(2,1)S(1)}, bf16[3,48,384]{2,1,0:T(8,128)(2,1)S(1)}, u32[]{:S(2)}, u32[]{:S(2)}) %collective-permute-start.14) | collective-permute-done | bytes 110624 | tf_op jit(solution)/shard_map/ppermute | solution.py:281
  54.6 0.8 %add_weight.1 = f32[3,96,384]{2,1,0:T(8,128)} custom-call(f32[3,96,384]{2,1,0:T(8,128)S(1)} %get-tuple-element.65.own_ref, bf16[3,48,384]{2,1,0:T(8,128)(2,1)S(1)} %collective-permute-done.13.got0_ref, bf16[3,48,384]{2,1,0:T(8,128)(2,1)S(1)} %collective-permute-done.14.got1_ref), custom_call_target="tpu_custom_call" | custom-call | bytes 1105920 | tf_op jit(solution)/shard_map/add_weight/pallas_call | solution.py:42
  55.4 0.0 collective-permute-done.15.refs_1_
  55.4 1.6 %collective-permute-done.16.refs_2_ = bf16[3,64,384]{2,1,0:T(8,128)(2,1)S(1)} collective-permute-done((bf16[3,64,384]{2,1,0:T(8,128)(2,1)S(1)}, bf16[3,64,384]{2,1,0:T(8,128)(2,1)S(1)}, u32[]{:S(2)}, u32[]{:S(2)}) %collective-permute-start.16) | collective-permute-done | bytes 147488 | tf_op jit(solution)/shard_map/ppermute | solution.py:281
  57.0 0.0 collective-permute-done.17.refs_3_
  57.0 0.9 %place.1 = (bf16[4,64,384]{2,1,0:T(8,128)(2,1)}, bf16[4,64,384]{2,1,0:T(8,128)(2,1)}, bf16[4,64,384]{2,1,0:T(8,128)(2,1)}) custom-call(bf16[3,64,384]{2,1,0:T(8,128)(2,1)S(1)} %get-tuple-element.69.refs_0_, bf16[3,64,384]{2,1,0:T(8,128)(2,1)S(1)} %collective-permute-done.15.refs_1_, bf16[3,64,384]{2,1,0:T(8,128)(2,1)S(1)} %collective-permute-done.16.refs_2_, ...), custom_call_target="tpu_custom_call" | custom-call | bytes 1179648 | tf_op jit(solution)/shard_map/place/pallas_call | solution.py:42
  (2 shorter events, 0.0 us)
Async XLA Ops:
  1.8 10.3 %collective-permute-start.1 = (bf16[7,64,384]{2,1,0:T(8,128)(2,1)S(1)}, bf16[7,64,384]{2,1,0:T(8,128)(2,1)S(1)}, u32[]{:S(2)}, u32[]{:S(2)}) collective-permute-start(bf16[7,64,384]{2,1,0:T(8,128)(2,1)S(1)} %get-tuple-element.42.to_mirror), channel_id=1, source_target_pairs={{4,8},{8,4},{5,9},{9,5},{6,10},{10,6},{7,11},{11,7},{20,24},{24,20... | collective-permute-start | bytes 1032200 | tf_op jit(solution)/shard_map/ppermute | solution.py:281
  2.5 14.4 %collective-permute-start = (bf16[7,64,384]{2,1,0:T(8,128)(2,1)S(1)}, bf16[7,64,384]{2,1,0:T(8,128)(2,1)S(1)}, u32[]{:S(2)}, u32[]{:S(2)}) collective-permute-start(bf16[7,64,384]{2,1,0:T(8,128)(2,1)S(1)} %get-tuple-element.41.cot_ref), channel_id=1, source_target_pairs={{0,4},{4,0},{8,12},{12,8},{1,5},{5,1},{9,13},{13,9},{2,6},{6,2},{1... | collective-permute-start | bytes 1032200 | tf_op jit(solution)/shard_map/ppermute | solution.py:281
  10.2 1.4 %collective-permute-start.2 = (bf16[2,64,384]{2,1,0:T(8,128)(2,1)S(1)}, bf16[2,64,384]{2,1,0:T(8,128)(2,1)S(1)}, u32[]{:S(2)}, u32[]{:S(2)}) collective-permute-start(bf16[2,64,384]{2,1,0:T(8,128)(2,1)S(1)} %get-tuple-element.48), channel_id=1, source_target_pairs={{0,1},{1,0},{2,3},{3,2},{4,5},{5,4},{6,7},{7,6},{8,9},{9,8},{10,11... | collective-permute-start | bytes 294920 | tf_op jit(solution)/shard_map/ppermute | solution.py:281
  12.0 12.5 %collective-permute-start.8 = (bf16[4,64,384]{2,1,0:T(8,128)(2,1)S(1)}, bf16[4,64,384]{2,1,0:T(8,128)(2,1)S(1)}, u32[]{:S(2)}, u32[]{:S(2)}) collective-permute-start(bf16[4,64,384]{2,1,0:T(8,128)(2,1)S(1)} %get-tuple-element.57), channel_id=1, source_target_pairs={{0,8},{4,12},{8,0},{12,4},{1,9},{5,13},{9,1},{13,5},{2,10},{6,14},... | collective-permute-start | bytes 589832 | tf_op jit(solution)/shard_map/ppermute | solution.py:281
  17.3 1.4 %collective-permute-start.4 = (bf16[2,64,384]{2,1,0:T(8,128)(2,1)S(1)}, bf16[2,64,384]{2,1,0:T(8,128)(2,1)S(1)}, u32[]{:S(2)}, u32[]{:S(2)}) collective-permute-start(bf16[2,64,384]{2,1,0:T(8,128)(2,1)S(1)} %get-tuple-element.53), channel_id=1, source_target_pairs={{0,1},{1,0},{2,3},{3,2},{4,5},{5,4},{6,7},{7,6},{8,9},{9,8},{10,11... | collective-permute-start | bytes 294920 | tf_op jit(solution)/shard_map/ppermute | solution.py:281
  17.4 1.4 %collective-permute-start.3 = (bf16[2,64,384]{2,1,0:T(8,128)(2,1)S(1)}, bf16[2,64,384]{2,1,0:T(8,128)(2,1)S(1)}, u32[]{:S(2)}, u32[]{:S(2)}) collective-permute-start(bf16[2,64,384]{2,1,0:T(8,128)(2,1)S(1)} %get-tuple-element.50), channel_id=1, source_target_pairs={{0,1},{1,0},{2,3},{3,2},{4,5},{5,4},{6,7},{7,6},{8,9},{9,8},{10,11... | collective-permute-start | bytes 294920 | tf_op jit(solution)/shard_map/ppermute | solution.py:281
  19.0 11.8 %collective-permute-start.5 = (bf16[6,64,384]{2,1,0:T(8,128)(2,1)S(1)}, bf16[6,64,384]{2,1,0:T(8,128)(2,1)S(1)}, u32[]{:S(2)}, u32[]{:S(2)}) collective-permute-start(bf16[6,64,384]{2,1,0:T(8,128)(2,1)S(1)} %get-tuple-element.54.to_beside), channel_id=1, source_target_pairs={{0,4},{4,0},{8,12},{12,8},{1,5},{5,1},{9,13},{13,9},{2,6},{6,2},{1... | collective-permute-start | bytes 884744 | tf_op jit(solution)/shard_map/ppermute | solution.py:281
  21.6 9.4 %collective-permute-start.6 = (bf16[6,64,384]{2,1,0:T(8,128)(2,1)S(1)}, bf16[6,64,384]{2,1,0:T(8,128)(2,1)S(1)}, u32[]{:S(2)}, u32[]{:S(2)}) collective-permute-start(bf16[6,64,384]{2,1,0:T(8,128)(2,1)S(1)} %get-tuple-element.55.to_mirror), channel_id=1, source_target_pairs={{4,8},{8,4},{5,9},{9,5},{6,10},{10,6},{7,11},{11,7},{20,24},{24,20... | collective-permute-start | bytes 884744 | tf_op jit(solution)/shard_map/ppermute | solution.py:281
  24.5 15.0 %collective-permute-start.10 = (bf16[5,64,384]{2,1,0:T(8,128)(2,1)S(1)}, bf16[5,64,384]{2,1,0:T(8,128)(2,1)S(1)}, u32[]{:S(2)}, u32[]{:S(2)}) collective-permute-start(bf16[5,64,384]{2,1,0:T(8,128)(2,1)S(1)} %get-tuple-element.62), channel_id=1, source_target_pairs={{0,12},{12,0},{1,13},{13,1},{2,14},{14,2},{3,15},{15,3},{16,28},{2... | collective-permute-start | bytes 737288 | tf_op jit(solution)/shard_map/ppermute | solution.py:281
  28.9 10.7 %collective-permute-start.11 = (bf16[1,64,384]{2,1,0:T(8,128)(2,1)S(1)}, bf16[1,64,384]{2,1,0:T(8,128)(2,1)S(1)}, u32[]{:S(2)}, u32[]{:S(2)}) collective-permute-start(bf16[1,64,384]{2,1,0:T(8,128)(2,1)S(1)} %get-tuple-element.63.to_opposite), channel_id=1, source_target_pairs={{0,8},{4,12},{8,0},{12,4},{1,9},{5,13},{9,1},{13,5},{2,10},{6,14},... | collective-permute-start | bytes 147464 | tf_op jit(solution)/shard_map/ppermute | solution.py:281
  30.8 15.3 %collective-permute-start.9 = (bf16[3,64,384]{2,1,0:T(8,128)(2,1)S(1)}, bf16[3,64,384]{2,1,0:T(8,128)(2,1)S(1)}, u32[]{:S(2)}, u32[]{:S(2)}) collective-permute-start(bf16[3,64,384]{2,1,0:T(8,128)(2,1)S(1)} %gather.1.act_ref), channel_id=1, source_target_pairs={{0,1},{1,0},{2,3},{3,2},{4,5},{5,4},{6,7},{7,6},{8,9},{9,8},{10,11... | collective-permute-start | bytes 442376 | tf_op jit(solution)/shard_map/ppermute | solution.py:281
  30.9 15.1 %collective-permute-start.7 = (bf16[4,64,384]{2,1,0:T(8,128)(2,1)S(1)}, bf16[4,64,384]{2,1,0:T(8,128)(2,1)S(1)}, u32[]{:S(2)}, u32[]{:S(2)}) collective-permute-start(bf16[4,64,384]{2,1,0:T(8,128)(2,1)S(1)} %pick.1), channel_id=1, source_target_pairs={{4,0},{8,12},{5,1},{9,13},{6,2},{10,14},{7,3},{11,15},{20,16},{24,... | collective-permute-start | bytes 589832 | tf_op jit(solution)/shard_map/ppermute | solution.py:343
  41.5 2.8 %collective-permute-start.12 = (bf16[1,64,384]{2,1,0:T(8,128)(2,1)S(1)}, bf16[1,64,384]{2,1,0:T(8,128)(2,1)S(1)}, u32[]{:S(2)}, u32[]{:S(2)}) collective-permute-start(bf16[1,64,384]{2,1,0:T(8,128)(2,1)S(1)} %get-tuple-element.64.act_last), channel_id=1, source_target_pairs={{0,1},{1,0},{2,3},{3,2},{4,5},{5,4},{6,7},{7,6},{8,9},{9,8},{10,11... | collective-permute-start | bytes 147464 | tf_op jit(solution)/shard_map/ppermute | solution.py:281
  41.6 13.8 %collective-permute-start.15 = (bf16[3,64,384]{2,1,0:T(8,128)(2,1)S(1)}, bf16[3,64,384]{2,1,0:T(8,128)(2,1)S(1)}, u32[]{:S(2)}, u32[]{:S(2)}) collective-permute-start(bf16[3,64,384]{2,1,0:T(8,128)(2,1)S(1)} %get-tuple-element.70), channel_id=1, source_target_pairs={{0,4},{4,0},{8,12},{12,8},{1,5},{5,1},{9,13},{13,9},{2,6},{6,2},{1... | collective-permute-start | bytes 442376 | tf_op jit(solution)/shard_map/ppermute | solution.py:281
  43.1 14.0 %collective-permute-start.16 = (bf16[3,64,384]{2,1,0:T(8,128)(2,1)S(1)}, bf16[3,64,384]{2,1,0:T(8,128)(2,1)S(1)}, u32[]{:S(2)}, u32[]{:S(2)}) collective-permute-start(bf16[3,64,384]{2,1,0:T(8,128)(2,1)S(1)} %get-tuple-element.71), channel_id=1, source_target_pairs={{0,8},{4,12},{8,0},{12,4},{1,9},{5,13},{9,1},{13,5},{2,10},{6,14},... | collective-permute-start | bytes 442376 | tf_op jit(solution)/shard_map/ppermute | solution.py:281
  44.4 12.7 %collective-permute-start.17 = (bf16[3,64,384]{2,1,0:T(8,128)(2,1)S(1)}, bf16[3,64,384]{2,1,0:T(8,128)(2,1)S(1)}, u32[]{:S(2)}, u32[]{:S(2)}) collective-permute-start(bf16[3,64,384]{2,1,0:T(8,128)(2,1)S(1)} %get-tuple-element.72), channel_id=1, source_target_pairs={{0,12},{4,8},{8,4},{12,0},{1,13},{5,9},{9,5},{13,1},{2,14},{6,10},... | collective-permute-start | bytes 442376 | tf_op jit(solution)/shard_map/ppermute | solution.py:281
  47.6 5.8 %collective-permute-start.13 = (bf16[3,48,384]{2,1,0:T(8,128)(2,1)S(1)}, bf16[3,48,384]{2,1,0:T(8,128)(2,1)S(1)}, u32[]{:S(2)}, u32[]{:S(2)}) collective-permute-start(bf16[3,48,384]{2,1,0:T(8,128)(2,1)S(1)} %get-tuple-element.66), channel_id=1, source_target_pairs={{0,2},{2,0},{1,3},{3,1},{4,6},{6,4},{5,7},{7,5},{8,10},{10,8},{9,1... | collective-permute-start | bytes 331784 | tf_op jit(solution)/shard_map/ppermute | solution.py:281
  49.1 5.5 %collective-permute-start.14 = (bf16[3,48,384]{2,1,0:T(8,128)(2,1)S(1)}, bf16[3,48,384]{2,1,0:T(8,128)(2,1)S(1)}, u32[]{:S(2)}, u32[]{:S(2)}) collective-permute-start(bf16[3,48,384]{2,1,0:T(8,128)(2,1)S(1)} %get-tuple-element.67), channel_id=1, source_target_pairs={{0,2},{2,0},{1,3},{3,1},{4,6},{6,4},{5,7},{7,5},{8,10},{10,8},{9,1... | collective-permute-start | bytes 331784 | tf_op jit(solution)/shard_map/ppermute | solution.py:281

commit v6 on v5

--- a/solution.py
+++ b/solution.py
@@ -30,7 +30,7 @@
 
 def kernel_call(
     body, outs, flops=0, transcendentals=0, name=None, scratch=(), space=pltpu.VMEM,
-    out_space=pltpu.VMEM,
+    out_space=pltpu.VMEM, bytes_too=True,
 ):
     given, made = (pl.BlockSpec(memory_space=x) for x in (space, out_space))
 
@@ -47,7 +47,7 @@
             scratch_shapes=list(scratch),
             compiler_params=pltpu.CompilerParams(vmem_limit_bytes=VMEM_LIMIT),
             cost_estimate=pl.CostEstimate(
-                flops=flops, bytes_accessed=moved, transcendentals=transcendentals
+                flops=flops, bytes_accessed=moved * bytes_too, transcendentals=transcendentals
             ),
             name=name,
         )(*args)
@@ -195,19 +195,20 @@
     nn = (((1,), (0,)), ((), ()))
     tn = (((0,), (0,)), ((), ()))
     dot = functools.partial(lax.dot_general, preferred_element_type=F32)
-    results = ([], [], [])
+    heads = []
     for h in range(width // HD):
         cols = slice(h * HD, (h + 1) * HD)
-        q, k, v, g = query[:, cols], key[:, cols], value[:, cols], grad[:, cols]
-        scores = dot(k, q, nt) * scale
-        raised = jnp.exp(scores - jnp.max(scores, axis=0, keepdims=True))
-        prob = raised * (1.0 / jnp.sum(raised, axis=0, keepdims=True))
-        d_prob = dot(v, g, nt)
-        row_total = jnp.sum(prob * d_prob, axis=0, keepdims=True)
-        d_score = (prob * (d_prob - row_total)).astype(BF)
-        results[0].append((dot(d_score, k, tn) * scale).astype(BF))
-        results[1].append((dot(d_score, q, nn) * scale).astype(BF))
-        results[2].append(dot(prob.astype(BF), g, nn).astype(BF))
+        heads.append([x[:, cols] for x in (query, key, value, grad)])
+    scores = [dot(k, q, nt) * scale for q, k, _, _ in heads]
+    d_probs = [dot(v, g, nt) for _, _, v, g in heads]
+    raised = [jnp.exp(x - jnp.max(x, axis=0, keepdims=True)) for x in scores]
+    probs = [x * (1.0 / jnp.sum(x, axis=0, keepdims=True)) for x in raised]
+    v_grads = [dot(p.astype(BF), g, nn).astype(BF) for p, (_, _, _, g) in zip(probs, heads)]
+    totals = [jnp.sum(p * d, axis=0, keepdims=True) for p, d in zip(probs, d_probs)]
+    d_scores = [(p * (d - t)).astype(BF) for p, d, t in zip(probs, d_probs, totals)]
+    k_grads = [(dot(d, q, nn) * scale).astype(BF) for d, (q, _, _, _) in zip(d_scores, heads)]
+    q_grads = [(dot(d, k, tn) * scale).astype(BF) for d, (_, k, _, _) in zip(d_scores, heads)]
+    results = q_grads, k_grads, v_grads
     for j in range(3):
         whole = jnp.concatenate(results[j], axis=1)
         for d in range(count):
@@ -268,10 +269,10 @@
     out_ref[:, half:] = own_ref[:, half:] + got1_ref[...].astype(F32)
 
 
-def place_kernel(count, *refs):
-    pieces, outs, sems = refs[:count], refs[count:-1], refs[-1]
+def place_kernel(*refs):
+    pieces, outs, sems = refs[:-4], refs[-4:-1], refs[-1]
     s = lax.axis_index("seq")
-    pairs = [(pieces[d].at[j], outs[j].at[s ^ d]) for d in range(count) for j in range(3)]
+    pairs = [(piece.at[j], outs[j].at[s ^ d]) for d, piece in zip((0, 2, 1, 3), pieces) for j in range(3)]
     for copy in fetch(pairs, sems):
         copy.wait()
 
@@ -354,13 +355,14 @@
         transcendentals=(count * rows) ** 2 * (width // HD),
         name="attention",
     )(own_qkv, own, beside, mirror, opposite, end2, beside2, mirror2, opposite2)
-    back = [returned[0]] + [swap(returned[d], "seq", d) for d in range(1, count)]
+    back = {d: swap(returned[d], "seq", d) for d in (2, 1, 3)}
 
     peer_last = swap(act_last, "chan", 1)
     total, sent0, sent1, hidden_grad = kernel_call(
         functools.partial(weight_kernel, count, factor),
         [shape((3, part // 2, width), F32)] + [shape((3, part // 4, width))] * 2 + [units(blocks)],
         name="weight_grad",
+        bytes_too=False,
         scratch=[
             pltpu.VMEM((count, part, tokens), BF),
             pltpu.VMEM((count, tokens, width), BF),
@@ -370,17 +372,18 @@
         peer_last, own, to_beside2, to_opposite2, to_mirror2,
     )
     got_sums = [swap(x, "batch", 1) for x in (sent0, sent1)]
-    (weight_grad,) = kernel_call(add_kernel, [shape((3, part // 2, width), F32)], name="add_weight")(
+    (weight_grad,) = kernel_call(add_kernel, [shape((3, part // 2, width), F32)], name="add_weight", bytes_too=False)(
         total, *got_sums
     )
-    (back[0],) = after(weight_grad, back[0])
+    pieces = [returned[0], *back.values()]
+    (pieces[0],) = after(weight_grad, pieces[0])
     query_grad, key_grad, value_grad = kernel_call(
-        functools.partial(place_kernel, count),
+        place_kernel,
         [units(blocks)] * 3,
         name="place",
         scratch=[pltpu.SemaphoreType.DMA((3 * count,))],
         out_space=pltpu.HBM,
-    )(*back)
+    )(*pieces)
     return (query_grad, key_grad, value_grad, hidden_grad, weight_grad.transpose(1, 0, 2))
 
 

time: 58.2 us -> 56.5 us (0.971)
  waiting for transfers between devices: 24.6 us -> 23.6 us
  Pallas kernels: 9.69 us -> 9 us
    ppermute x17, waiting for transfers between devices: 24.6 us -> 23.6 us  [swap(): lax.ppermute(x, axis, [(i, i ^ by) for i in range(n) if only is None or i...]
    pallas_call x12, Pallas kernels: 9.69 us -> 9 us  [call(): pl.pallas_call(body, out_shape=list(outs), in_specs=[given] * len(args),...]
  transfers between devices with their start and end apart: 18 -> 18, of which waited for: 10 -> 10; matrix products, arithmetic and copies ran while one was open for 0% -> 0% of each run, Pallas kernels for 13% -> 12%
where the time goes in v6:
time: 56.5 us; the launch traced here: 56.3 us
  waiting for transfers between devices  23.6 us (42%)
  starting transfers between devices  22.9 us (41%)
  Pallas kernels  9 us (16%)
  between operations  0.78 us (1%)
    ppermute x17, waiting for transfers between devices, swap(): lax.ppermute(x, axis, [(i, i ^ by) for i in range(n) if only is None or i...  23.6 us
    ppermute x17, starting transfers between devices, swap(): lax.ppermute(x, axis, [(i, i ^ by) for i in range(n) if only is None or i...  21.6 us
    pallas_call x12, Pallas kernels, call(): pl.pallas_call(body, out_shape=list(outs), in_specs=[given] * len(args),...  9 us
    ppermute x1, starting transfers between devices, per_device(): farthest = lax.ppermute(far, 'seq', [(1, 0), (2, 3)])  1.29 us
  transfers between devices with their start and end apart: 18, of which 10 were waited for; matrix products, arithmetic and copies ran while one was open for 0% of the time, Pallas kernels for 12%

profile of v6, /device:TPU:0, one launch (start us, length us, event | category | flops | bytes accessed | tf_op | source)
XLA Modules:
  0.0 56.3 jit_solution(12902446143586401635)
XLA Ops:
  0.6 1.2 %near.1 = (bf16[7,64,384]{2,1,0:T(8,128)(2,1)S(1)}, bf16[7,64,384]{2,1,0:T(8,128)(2,1)S(1)}) custom-call(bf16[4,64,384]{2,1,0:T(8,128)(2,1)} %cot.1, bf16[4,64,384]{2,1,0:T(8,128)(2,1)} %q.3, bf16[4,64,384]{2,1,0:T(8,128)(2,1)} %k.3, bf16[4,64,384]{2,1,0:T(8,128)(2,1)} %v.3), custom_call_target="tpu_custom_call" | custom-call | bytes 1474560 | tf_op jit(solution)/shard_map/near/pallas_call | solution.py:42
  1.8 0.7 %collective-permute-start.1 = (bf16[7,64,384]{2,1,0:T(8,128)(2,1)S(1)}, bf16[7,64,384]{2,1,0:T(8,128)(2,1)S(1)}, u32[]{:S(2)}, u32[]{:S(2)}) collective-permute-start(bf16[7,64,384]{2,1,0:T(8,128)(2,1)S(1)} %get-tuple-element.42.to_mirror), channel_id=1, source_target_pairs={{4,8},{8,4},{5,9},{9,5},{6,10},{10,6},{7,11},{11,7},{20,24},{24,20... | collective-permute-start | bytes 1032200 | tf_op jit(solution)/shard_map/ppermute | solution.py:282
  2.5 5.9 %collective-permute-start = (bf16[7,64,384]{2,1,0:T(8,128)(2,1)S(1)}, bf16[7,64,384]{2,1,0:T(8,128)(2,1)S(1)}, u32[]{:S(2)}, u32[]{:S(2)}) collective-permute-start(bf16[7,64,384]{2,1,0:T(8,128)(2,1)S(1)} %get-tuple-element.41.cot_ref), channel_id=1, source_target_pairs={{0,4},{4,0},{8,12},{12,8},{1,5},{5,1},{9,13},{13,9},{2,6},{6,2},{1... | collective-permute-start | bytes 1032200 | tf_op jit(solution)/shard_map/ppermute | solution.py:282
  8.4 1.8 %rest.1 = (bf16[3,64,384]{2,1,0:T(8,128)(2,1)S(1)}, bf16[3,64,384]{2,1,0:T(8,128)(2,1)S(1)}, bf16[3,768,384]{2,1,0:T(8,128)(2,1)S(1)}, f32[4,64,384]{2,1,0:T(8,1...) custom-call(bf16[4,64,384]{2,1,0:T(8,128)(2,1)} %hidden, bf16[4,64,384]{2,1,0:T(8,128)(2,1)} %q.3, ...), custom_call_target="tpu_custom_call" | custom-call | bytes 5210112 | tf_op jit(solution)/shard_map/rest/pallas_call | solution.py:42
  10.2 0.1 collective-permute-start.2
  10.3 1.3 %collective-permute-done.2.act_peer = bf16[2,64,384]{2,1,0:T(8,128)(2,1)S(1)} collective-permute-done((bf16[2,64,384]{2,1,0:T(8,128)(2,1)S(1)}, bf16[2,64,384]{2,1,0:T(8,128)(2,1)S(1)}, u32[]{:S(2)}, u32[]{:S(2)}) %collective-permute-start.2) | collective-permute-done | bytes 98336 | tf_op jit(solution)/shard_map/ppermute | solution.py:282
  11.6 0.4 conv_centre.1
  12.0 0.1 collective-permute-start.8
  12.1 0.0 collective-permute-done.1.mirror_ref.mirror_qkv.mirror
  12.1 4.8 %collective-permute-done.beside_ref.beside_qkv.beside = bf16[7,64,384]{2,1,0:T(8,128)(2,1)S(1)} collective-permute-done((bf16[7,64,384]{2,1,0:T(8,128)(2,1)S(1)}, bf16[7,64,384]{2,1,0:T(8,128)(2,1)S(1)}, u32[]{:S(2)}, u32[]{:S(2)}) %collective-permute-start) | collective-permute-done | bytes 344096 | tf_op jit(solution)/shard_map/ppermute | solution.py:282
  16.9 0.4 conv_other.1
  17.3 0.1 collective-permute-start.4
  17.4 0.5 collective-permute-start.3
  17.9 0.4 conv_mine.1.mine_ref
  18.3 0.4 collective-permute-done.4.got1_ref
  18.7 0.2 collective-permute-done.3.got0_ref
  18.8 0.2 hidden_grad.1
  19.0 2.6 %collective-permute-start.5 = (bf16[6,64,384]{2,1,0:T(8,128)(2,1)S(1)}, bf16[6,64,384]{2,1,0:T(8,128)(2,1)S(1)}, u32[]{:S(2)}, u32[]{:S(2)}) collective-permute-start(bf16[6,64,384]{2,1,0:T(8,128)(2,1)S(1)} %get-tuple-element.54.to_beside), channel_id=1, source_target_pairs={{0,4},{4,0},{8,12},{12,8},{1,5},{5,1},{9,13},{13,9},{2,6},{6,2},{1... | collective-permute-start | bytes 884744 | tf_op jit(solution)/shard_map/ppermute | solution.py:282
  21.6 0.7 %collective-permute-start.6 = (bf16[6,64,384]{2,1,0:T(8,128)(2,1)S(1)}, bf16[6,64,384]{2,1,0:T(8,128)(2,1)S(1)}, u32[]{:S(2)}, u32[]{:S(2)}) collective-permute-start(bf16[6,64,384]{2,1,0:T(8,128)(2,1)S(1)} %get-tuple-element.55.to_mirror), channel_id=1, source_target_pairs={{4,8},{8,4},{5,9},{9,5},{6,10},{10,6},{7,11},{11,7},{20,24},{24,20... | collective-permute-start | bytes 884744 | tf_op jit(solution)/shard_map/ppermute | solution.py:282
  22.2 2.3 %collective-permute-done.8.opposite.opposite_qkv = bf16[4,64,384]{2,1,0:T(8,128)(2,1)S(1)} collective-permute-done((bf16[4,64,384]{2,1,0:T(8,128)(2,1)S(1)}, bf16[4,64,384]{2,1,0:T(8,128)(2,1)S(1)}, u32[]{:S(2)}, u32[]{:S(2)}) %collective-permute-start.8) | collective-permute-done | bytes 196640 | tf_op jit(solution)/shard_map/ppermute | solution.py:282
  24.5 4.4 %collective-permute-start.10 = (bf16[5,64,384]{2,1,0:T(8,128)(2,1)S(1)}, bf16[5,64,384]{2,1,0:T(8,128)(2,1)S(1)}, u32[]{:S(2)}, u32[]{:S(2)}) collective-permute-start(bf16[5,64,384]{2,1,0:T(8,128)(2,1)S(1)} %get-tuple-element.62), channel_id=1, source_target_pairs={{0,12},{12,0},{1,13},{13,1},{2,14},{14,2},{3,15},{15,3},{16,28},{2... | collective-permute-start | bytes 737288 | tf_op jit(solution)/shard_map/ppermute | solution.py:282
  28.9 0.1 collective-permute-start.11
  29.0 1.8 %collective-permute-done.5.beside.beside2 = bf16[6,64,384]{2,1,0:T(8,128)(2,1)S(1)} collective-permute-done((bf16[6,64,384]{2,1,0:T(8,128)(2,1)S(1)}, bf16[6,64,384]{2,1,0:T(8,128)(2,1)S(1)}, u32[]{:S(2)}, u32[]{:S(2)}) %collective-permute-start.5) | collective-permute-done | bytes 294944 | tf_op jit(solution)/shard_map/ppermute | solution.py:282
  30.8 0.1 collective-permute-start.9
  30.9 0.0 collective-permute-done.6.held_ref.mirror.mirror2
  30.9 1.3 %collective-permute-start.7 = (bf16[4,64,384]{2,1,0:T(8,128)(2,1)S(1)}, bf16[4,64,384]{2,1,0:T(8,128)(2,1)S(1)}, u32[]{:S(2)}, u32[]{:S(2)}) collective-permute-start(bf16[4,64,384]{2,1,0:T(8,128)(2,1)S(1)} %pick.1), channel_id=1, source_target_pairs={{4,0},{8,12},{5,1},{9,13},{6,2},{10,14},{7,3},{11,15},{20,16},{24,... | collective-permute-start | bytes 589832 | tf_op jit(solution)/shard_map/ppermute | solution.py:344
  32.2 7.3 %collective-permute-done.11.opposite = bf16[1,64,384]{2,1,0:T(8,128)(2,1)S(1)} collective-permute-done((bf16[1,64,384]{2,1,0:T(8,128)(2,1)S(1)}, bf16[1,64,384]{2,1,0:T(8,128)(2,1)S(1)}, u32[]{:S(2)}, u32[]{:S(2)}) %collective-permute-start.11) | collective-permute-done | bytes 49184 | tf_op jit(solution)/shard_map/ppermute | solution.py:282
  39.5 0.0 collective-permute-done.10.end
  39.5 1.3 %attention.1 = (bf16[3,64,384]{2,1,0:T(8,128)(2,1)S(1)}, bf16[3,64,384]{2,1,0:T(8,128)(2,1)S(1)}, bf16[3,64,384]{2,1,0:T(8,128)(2,1)S(1)}, bf16[3,64,384]{2,1,0:T(8,128)(2,1)S(1)}, bf16[1,64,384]{2,1,0:T(8,128)(2,1)S(1)}) custom-call(bf16[3,64,384]{2,1,0:T(8,128)(2,1)S(1)} %get-tuple-element.59.own_qkv, bf16[2,64,384]{2,1,0:T(8,128)(2,1)S(1)} %get-tuple-element.56.own, ...), custom_call_target="tpu_custom_call" | custom-call | flops 2013265920 | bytes 2654208 | tf_op jit(solution)/shard_map/attention/pallas_call | solution.py:42
  40.9 0.1 collective-permute-start.12
  40.9 2.1 %collective-permute-start.15 = (bf16[3,64,384]{2,1,0:T(8,128)(2,1)S(1)}, bf16[3,64,384]{2,1,0:T(8,128)(2,1)S(1)}, u32[]{:S(2)}, u32[]{:S(2)}) collective-permute-start(bf16[3,64,384]{2,1,0:T(8,128)(2,1)S(1)} %get-tuple-element.70), channel_id=1, source_target_pairs={{0,8},{4,12},{8,0},{12,4},{1,9},{5,13},{9,1},{13,5},{2,10},{6,14},... | collective-permute-start | bytes 442376 | tf_op jit(solution)/shard_map/ppermute | solution.py:282
  43.0 0.6 %collective-permute-start.16 = (bf16[3,64,384]{2,1,0:T(8,128)(2,1)S(1)}, bf16[3,64,384]{2,1,0:T(8,128)(2,1)S(1)}, u32[]{:S(2)}, u32[]{:S(2)}) collective-permute-start(bf16[3,64,384]{2,1,0:T(8,128)(2,1)S(1)} %get-tuple-element.71), channel_id=1, source_target_pairs={{0,4},{4,0},{8,12},{12,8},{1,5},{5,1},{9,13},{13,9},{2,6},{6,2},{1... | collective-permute-start | bytes 442376 | tf_op jit(solution)/shard_map/ppermute | solution.py:282
  43.7 0.0 collective-permute-done.12.peer_last
  43.7 1.7 %collective-permute-start.17 = (bf16[3,64,384]{2,1,0:T(8,128)(2,1)S(1)}, bf16[3,64,384]{2,1,0:T(8,128)(2,1)S(1)}, u32[]{:S(2)}, u32[]{:S(2)}) collective-permute-start(bf16[3,64,384]{2,1,0:T(8,128)(2,1)S(1)} %get-tuple-element.72), channel_id=1, source_target_pairs={{0,12},{4,8},{8,4},{12,0},{1,13},{5,9},{9,5},{13,1},{2,14},{6,10},... | collective-permute-start | bytes 442376 | tf_op jit(solution)/shard_map/ppermute | solution.py:282
  45.4 0.0 collective-permute-done.9.act_peer
  45.4 0.0 collective-permute-done.7.farthest
  45.4 1.5 %weight_grad.1 = (f32[3,96,384]{2,1,0:T(8,128)S(1)}, bf16[3,48,384]{2,1,0:T(8,128)(2,1)S(1)}, bf16[3,48,384]{2,1,0:T(8,128)(2,1)S(1)}, bf16[4,64,384]{2,1,0:T(8,128)(2,1)}) custom-call(bf16[7,64,384]{2,1,0:T(8,128)(2,1)S(1)} %get-tuple-element.41.cot_ref, bf16[7,64,384]{2,1,0:T(8,128)(2,1)S(1)} %collective-permute-done.beside_ref.beside_qkv.beside, ...), custom_call_target="tpu_custom_call" | custom-call | tf_op jit(solution)/shard_map/weight_grad/pallas_call | solution.py:42
  46.9 1.5 %collective-permute-start.13 = (bf16[3,48,384]{2,1,0:T(8,128)(2,1)S(1)}, bf16[3,48,384]{2,1,0:T(8,128)(2,1)S(1)}, u32[]{:S(2)}, u32[]{:S(2)}) collective-permute-start(bf16[3,48,384]{2,1,0:T(8,128)(2,1)S(1)} %get-tuple-element.66), channel_id=1, source_target_pairs={{0,2},{2,0},{1,3},{3,1},{4,6},{6,4},{5,7},{7,5},{8,10},{10,8},{9,1... | collective-permute-start | bytes 331784 | tf_op jit(solution)/shard_map/ppermute | solution.py:282
  48.4 0.5 collective-permute-start.14
  49.0 3.8 %collective-permute-done.13.got0_ref = bf16[3,48,384]{2,1,0:T(8,128)(2,1)S(1)} collective-permute-done((bf16[3,48,384]{2,1,0:T(8,128)(2,1)S(1)}, bf16[3,48,384]{2,1,0:T(8,128)(2,1)S(1)}, u32[]{:S(2)}, u32[]{:S(2)}) %collective-permute-start.13) | collective-permute-done | bytes 110624 | tf_op jit(solution)/shard_map/ppermute | solution.py:282
  52.7 1.2 %collective-permute-done.14.got1_ref = bf16[3,48,384]{2,1,0:T(8,128)(2,1)S(1)} collective-permute-done((bf16[3,48,384]{2,1,0:T(8,128)(2,1)S(1)}, bf16[3,48,384]{2,1,0:T(8,128)(2,1)S(1)}, u32[]{:S(2)}, u32[]{:S(2)}) %collective-permute-start.14) | collective-permute-done | bytes 110624 | tf_op jit(solution)/shard_map/ppermute | solution.py:282
  53.9 0.8 %add_weight.1 = f32[3,96,384]{2,1,0:T(8,128)} custom-call(f32[3,96,384]{2,1,0:T(8,128)S(1)} %get-tuple-element.65.own_ref, bf16[3,48,384]{2,1,0:T(8,128)(2,1)S(1)} %collective-permute-done.13.got0_ref, bf16[3,48,384]{2,1,0:T(8,128)(2,1)S(1)} %collective-permute-done.14.got1_ref), custom_call_target="tpu_custom_call" | custom-call | tf_op jit(solution)/shard_map/add_weight/pallas_call | solution.py:42
  54.7 0.0 collective-permute-done.15.refs_1_
  54.7 0.0 collective-permute-done.16.refs_2_
  54.7 0.7 %collective-permute-done.17.refs_3_ = bf16[3,64,384]{2,1,0:T(8,128)(2,1)S(1)} collective-permute-done((bf16[3,64,384]{2,1,0:T(8,128)(2,1)S(1)}, bf16[3,64,384]{2,1,0:T(8,128)(2,1)S(1)}, u32[]{:S(2)}, u32[]{:S(2)}) %collective-permute-start.17) | collective-permute-done | bytes 147488 | tf_op jit(solution)/shard_map/ppermute | solution.py:282
  55.4 0.9 %place.1 = (bf16[4,64,384]{2,1,0:T(8,128)(2,1)}, bf16[4,64,384]{2,1,0:T(8,128)(2,1)}, bf16[4,64,384]{2,1,0:T(8,128)(2,1)}) custom-call(bf16[3,64,384]{2,1,0:T(8,128)(2,1)S(1)} %get-tuple-element.69.refs_0_, bf16[3,64,384]{2,1,0:T(8,128)(2,1)S(1)} %collective-permute-done.15.refs_1_, bf16[3,64,384]{2,1,0:T(8,128)(2,1)S(1)} %collective-permute-done.16.refs_2_, ...), custom_call_target="tpu_custom_call" | custom-call | bytes 1179648 | tf_op jit(solution)/shard_map/place/pallas_call | solution.py:42
  (2 shorter events, 0.0 us)
Async XLA Ops:
  1.8 10.3 %collective-permute-start.1 = (bf16[7,64,384]{2,1,0:T(8,128)(2,1)S(1)}, bf16[7,64,384]{2,1,0:T(8,128)(2,1)S(1)}, u32[]{:S(2)}, u32[]{:S(2)}) collective-permute-start(bf16[7,64,384]{2,1,0:T(8,128)(2,1)S(1)} %get-tuple-element.42.to_mirror), channel_id=1, source_target_pairs={{4,8},{8,4},{5,9},{9,5},{6,10},{10,6},{7,11},{11,7},{20,24},{24,20... | collective-permute-start | bytes 1032200 | tf_op jit(solution)/shard_map/ppermute | solution.py:282
  2.5 14.4 %collective-permute-start = (bf16[7,64,384]{2,1,0:T(8,128)(2,1)S(1)}, bf16[7,64,384]{2,1,0:T(8,128)(2,1)S(1)}, u32[]{:S(2)}, u32[]{:S(2)}) collective-permute-start(bf16[7,64,384]{2,1,0:T(8,128)(2,1)S(1)} %get-tuple-element.41.cot_ref), channel_id=1, source_target_pairs={{0,4},{4,0},{8,12},{12,8},{1,5},{5,1},{9,13},{13,9},{2,6},{6,2},{1... | collective-permute-start | bytes 1032200 | tf_op jit(solution)/shard_map/ppermute | solution.py:282
  10.2 1.4 %collective-permute-start.2 = (bf16[2,64,384]{2,1,0:T(8,128)(2,1)S(1)}, bf16[2,64,384]{2,1,0:T(8,128)(2,1)S(1)}, u32[]{:S(2)}, u32[]{:S(2)}) collective-permute-start(bf16[2,64,384]{2,1,0:T(8,128)(2,1)S(1)} %get-tuple-element.48), channel_id=1, source_target_pairs={{0,1},{1,0},{2,3},{3,2},{4,5},{5,4},{6,7},{7,6},{8,9},{9,8},{10,11... | collective-permute-start | bytes 294920 | tf_op jit(solution)/shard_map/ppermute | solution.py:282
  12.0 12.5 %collective-permute-start.8 = (bf16[4,64,384]{2,1,0:T(8,128)(2,1)S(1)}, bf16[4,64,384]{2,1,0:T(8,128)(2,1)S(1)}, u32[]{:S(2)}, u32[]{:S(2)}) collective-permute-start(bf16[4,64,384]{2,1,0:T(8,128)(2,1)S(1)} %get-tuple-element.57), channel_id=1, source_target_pairs={{0,8},{4,12},{8,0},{12,4},{1,9},{5,13},{9,1},{13,5},{2,10},{6,14},... | collective-permute-start | bytes 589832 | tf_op jit(solution)/shard_map/ppermute | solution.py:282
  17.3 1.4 %collective-permute-start.4 = (bf16[2,64,384]{2,1,0:T(8,128)(2,1)S(1)}, bf16[2,64,384]{2,1,0:T(8,128)(2,1)S(1)}, u32[]{:S(2)}, u32[]{:S(2)}) collective-permute-start(bf16[2,64,384]{2,1,0:T(8,128)(2,1)S(1)} %get-tuple-element.53), channel_id=1, source_target_pairs={{0,1},{1,0},{2,3},{3,2},{4,5},{5,4},{6,7},{7,6},{8,9},{9,8},{10,11... | collective-permute-start | bytes 294920 | tf_op jit(solution)/shard_map/ppermute | solution.py:282
  17.4 1.4 %collective-permute-start.3 = (bf16[2,64,384]{2,1,0:T(8,128)(2,1)S(1)}, bf16[2,64,384]{2,1,0:T(8,128)(2,1)S(1)}, u32[]{:S(2)}, u32[]{:S(2)}) collective-permute-start(bf16[2,64,384]{2,1,0:T(8,128)(2,1)S(1)} %get-tuple-element.50), channel_id=1, source_target_pairs={{0,1},{1,0},{2,3},{3,2},{4,5},{5,4},{6,7},{7,6},{8,9},{9,8},{10,11... | collective-permute-start | bytes 294920 | tf_op jit(solution)/shard_map/ppermute | solution.py:282
  19.0 11.8 %collective-permute-start.5 = (bf16[6,64,384]{2,1,0:T(8,128)(2,1)S(1)}, bf16[6,64,384]{2,1,0:T(8,128)(2,1)S(1)}, u32[]{:S(2)}, u32[]{:S(2)}) collective-permute-start(bf16[6,64,384]{2,1,0:T(8,128)(2,1)S(1)} %get-tuple-element.54.to_beside), channel_id=1, source_target_pairs={{0,4},{4,0},{8,12},{12,8},{1,5},{5,1},{9,13},{13,9},{2,6},{6,2},{1... | collective-permute-start | bytes 884744 | tf_op jit(solution)/shard_map/ppermute | solution.py:282
  21.6 9.4 %collective-permute-start.6 = (bf16[6,64,384]{2,1,0:T(8,128)(2,1)S(1)}, bf16[6,64,384]{2,1,0:T(8,128)(2,1)S(1)}, u32[]{:S(2)}, u32[]{:S(2)}) collective-permute-start(bf16[6,64,384]{2,1,0:T(8,128)(2,1)S(1)} %get-tuple-element.55.to_mirror), channel_id=1, source_target_pairs={{4,8},{8,4},{5,9},{9,5},{6,10},{10,6},{7,11},{11,7},{20,24},{24,20... | collective-permute-start | bytes 884744 | tf_op jit(solution)/shard_map/ppermute | solution.py:282
  24.5 15.0 %collective-permute-start.10 = (bf16[5,64,384]{2,1,0:T(8,128)(2,1)S(1)}, bf16[5,64,384]{2,1,0:T(8,128)(2,1)S(1)}, u32[]{:S(2)}, u32[]{:S(2)}) collective-permute-start(bf16[5,64,384]{2,1,0:T(8,128)(2,1)S(1)} %get-tuple-element.62), channel_id=1, source_target_pairs={{0,12},{12,0},{1,13},{13,1},{2,14},{14,2},{3,15},{15,3},{16,28},{2... | collective-permute-start | bytes 737288 | tf_op jit(solution)/shard_map/ppermute | solution.py:282
  28.9 10.7 %collective-permute-start.11 = (bf16[1,64,384]{2,1,0:T(8,128)(2,1)S(1)}, bf16[1,64,384]{2,1,0:T(8,128)(2,1)S(1)}, u32[]{:S(2)}, u32[]{:S(2)}) collective-permute-start(bf16[1,64,384]{2,1,0:T(8,128)(2,1)S(1)} %get-tuple-element.63.to_opposite), channel_id=1, source_target_pairs={{0,8},{4,12},{8,0},{12,4},{1,9},{5,13},{9,1},{13,5},{2,10},{6,14},... | collective-permute-start | bytes 147464 | tf_op jit(solution)/shard_map/ppermute | solution.py:282
  30.8 14.6 %collective-permute-start.9 = (bf16[3,64,384]{2,1,0:T(8,128)(2,1)S(1)}, bf16[3,64,384]{2,1,0:T(8,128)(2,1)S(1)}, u32[]{:S(2)}, u32[]{:S(2)}) collective-permute-start(bf16[3,64,384]{2,1,0:T(8,128)(2,1)S(1)} %gather.1.act_ref), channel_id=1, source_target_pairs={{0,1},{1,0},{2,3},{3,2},{4,5},{5,4},{6,7},{7,6},{8,9},{9,8},{10,11... | collective-permute-start | bytes 442376 | tf_op jit(solution)/shard_map/ppermute | solution.py:282
  30.9 14.5 %collective-permute-start.7 = (bf16[4,64,384]{2,1,0:T(8,128)(2,1)S(1)}, bf16[4,64,384]{2,1,0:T(8,128)(2,1)S(1)}, u32[]{:S(2)}, u32[]{:S(2)}) collective-permute-start(bf16[4,64,384]{2,1,0:T(8,128)(2,1)S(1)} %pick.1), channel_id=1, source_target_pairs={{4,0},{8,12},{5,1},{9,13},{6,2},{10,14},{7,3},{11,15},{20,16},{24,... | collective-permute-start | bytes 589832 | tf_op jit(solution)/shard_map/ppermute | solution.py:344
  40.9 2.8 %collective-permute-start.12 = (bf16[1,64,384]{2,1,0:T(8,128)(2,1)S(1)}, bf16[1,64,384]{2,1,0:T(8,128)(2,1)S(1)}, u32[]{:S(2)}, u32[]{:S(2)}) collective-permute-start(bf16[1,64,384]{2,1,0:T(8,128)(2,1)S(1)} %get-tuple-element.64.act_last), channel_id=1, source_target_pairs={{0,1},{1,0},{2,3},{3,2},{4,5},{5,4},{6,7},{7,6},{8,9},{9,8},{10,11... | collective-permute-start | bytes 147464 | tf_op jit(solution)/shard_map/ppermute | solution.py:282
  40.9 13.8 %collective-permute-start.15 = (bf16[3,64,384]{2,1,0:T(8,128)(2,1)S(1)}, bf16[3,64,384]{2,1,0:T(8,128)(2,1)S(1)}, u32[]{:S(2)}, u32[]{:S(2)}) collective-permute-start(bf16[3,64,384]{2,1,0:T(8,128)(2,1)S(1)} %get-tuple-element.70), channel_id=1, source_target_pairs={{0,8},{4,12},{8,0},{12,4},{1,9},{5,13},{9,1},{13,5},{2,10},{6,14},... | collective-permute-start | bytes 442376 | tf_op jit(solution)/shard_map/ppermute | solution.py:282
  43.0 11.7 %collective-permute-start.16 = (bf16[3,64,384]{2,1,0:T(8,128)(2,1)S(1)}, bf16[3,64,384]{2,1,0:T(8,128)(2,1)S(1)}, u32[]{:S(2)}, u32[]{:S(2)}) collective-permute-start(bf16[3,64,384]{2,1,0:T(8,128)(2,1)S(1)} %get-tuple-element.71), channel_id=1, source_target_pairs={{0,4},{4,0},{8,12},{12,8},{1,5},{5,1},{9,13},{13,9},{2,6},{6,2},{1... | collective-permute-start | bytes 442376 | tf_op jit(solution)/shard_map/ppermute | solution.py:282
  43.7 11.7 %collective-permute-start.17 = (bf16[3,64,384]{2,1,0:T(8,128)(2,1)S(1)}, bf16[3,64,384]{2,1,0:T(8,128)(2,1)S(1)}, u32[]{:S(2)}, u32[]{:S(2)}) collective-permute-start(bf16[3,64,384]{2,1,0:T(8,128)(2,1)S(1)} %get-tuple-element.72), channel_id=1, source_target_pairs={{0,12},{4,8},{8,4},{12,0},{1,13},{5,9},{9,5},{13,1},{2,14},{6,10},... | collective-permute-start | bytes 442376 | tf_op jit(solution)/shard_map/ppermute | solution.py:282
  46.9 5.8 %collective-permute-start.13 = (bf16[3,48,384]{2,1,0:T(8,128)(2,1)S(1)}, bf16[3,48,384]{2,1,0:T(8,128)(2,1)S(1)}, u32[]{:S(2)}, u32[]{:S(2)}) collective-permute-start(bf16[3,48,384]{2,1,0:T(8,128)(2,1)S(1)} %get-tuple-element.66), channel_id=1, source_target_pairs={{0,2},{2,0},{1,3},{3,1},{4,6},{6,4},{5,7},{7,5},{8,10},{10,8},{9,1... | collective-permute-start | bytes 331784 | tf_op jit(solution)/shard_map/ppermute | solution.py:282
  48.4 5.5 %collective-permute-start.14 = (bf16[3,48,384]{2,1,0:T(8,128)(2,1)S(1)}, bf16[3,48,384]{2,1,0:T(8,128)(2,1)S(1)}, u32[]{:S(2)}, u32[]{:S(2)}) collective-permute-start(bf16[3,48,384]{2,1,0:T(8,128)(2,1)S(1)} %get-tuple-element.67), channel_id=1, source_target_pairs={{0,2},{2,0},{1,3},{3,1},{4,6},{6,4},{5,7},{7,5},{8,10},{10,8},{9,1... | collective-permute-start | bytes 331784 | tf_op jit(solution)/shard_map/ppermute | solution.py:282

commit v7 on v6

--- a/solution.py
+++ b/solution.py
@@ -195,24 +195,34 @@
     nn = (((1,), (0,)), ((), ()))
     tn = (((0,), (0,)), ((), ()))
     dot = functools.partial(lax.dot_general, preferred_element_type=F32)
-    heads = []
+    tile = 128
+    lane = lax.broadcasted_iota(jnp.int32, (1, width), 1)
+    windows, heads = [], []
     for h in range(width // HD):
-        cols = slice(h * HD, (h + 1) * HD)
-        heads.append([x[:, cols] for x in (query, key, value, grad)])
-    scores = [dot(k, q, nt) * scale for q, k, _, _ in heads]
-    d_probs = [dot(v, g, nt) for _, _, v, g in heads]
+        low, high = h * HD // tile * tile, -(-(h + 1) * HD // tile) * tile
+        inside = jnp.logical_and(lane >= h * HD, lane < (h + 1) * HD).astype(F32).astype(BF)[:, low:high]
+        windows.append((low, high))
+        q, k, v, g = (x[:, low:high] for x in (query, key, value, grad))
+        heads.append((q, k, k * inside, v * inside, g))
+    scores = [dot(k, q, nt) * scale for q, _, k, _, _ in heads]
+    d_probs = [dot(v, g, nt) for _, _, _, v, g in heads]
     raised = [jnp.exp(x - jnp.max(x, axis=0, keepdims=True)) for x in scores]
     probs = [x * (1.0 / jnp.sum(x, axis=0, keepdims=True)) for x in raised]
-    v_grads = [dot(p.astype(BF), g, nn).astype(BF) for p, (_, _, _, g) in zip(probs, heads)]
+    v_grads = [dot(p.astype(BF), x[4], nn) for p, x in zip(probs, heads)]
     totals = [jnp.sum(p * d, axis=0, keepdims=True) for p, d in zip(probs, d_probs)]
     d_scores = [(p * (d - t)).astype(BF) for p, d, t in zip(probs, d_probs, totals)]
-    k_grads = [(dot(d, q, nn) * scale).astype(BF) for d, (q, _, _, _) in zip(d_scores, heads)]
-    q_grads = [(dot(d, k, tn) * scale).astype(BF) for d, (_, k, _, _) in zip(d_scores, heads)]
-    results = q_grads, k_grads, v_grads
-    for j in range(3):
-        whole = jnp.concatenate(results[j], axis=1)
-        for d in range(count):
-            outs[d][j] = whole[d * rows : (d + 1) * rows]
+    k_grads = [dot(d, x[0], nn) * scale for d, x in zip(d_scores, heads)]
+    q_grads = [dot(d, x[1], tn) * scale for d, x in zip(d_scores, heads)]
+    for j, results in enumerate((q_grads, k_grads, v_grads)):
+        for at in range(0, width, tile):
+            whole = None
+            for h, ((low, high), x) in enumerate(zip(windows, results)):
+                if low <= at < high:
+                    part = x[:, at - low : at - low + tile]
+                    whole = part if whole is None else jnp.where(lane[:, at : at + tile] < h * HD, whole, part)
+            whole = whole.astype(BF)
+            for d in range(count):
+                outs[d][j, :, at : at + tile] = whole[d * rows : (d + 1) * rows]
 
 
 def weight_kernel(

time: 56.5 us -> 56.4 us (level)
    ppermute x17, waiting for transfers between devices: 23.6 us -> 23 us  [swap(): lax.ppermute(x, axis, [(i, i ^ by) for i in range(n) if only is None or i...]
    ppermute x1, waiting for transfers between devices: 0.01 us -> 0.59 us  [per_device(): farthest = lax.ppermute(far, 'seq', [(1, 0), (2, 3)])]
  transfers between devices with their start and end apart: 18 -> 18, of which waited for: 10 -> 11; matrix products, arithmetic and copies ran while one was open for 0% -> 0% of each run, Pallas kernels for 12% -> 12%
where the time goes in v7:
time: 56.4 us; the launch traced here: 56.2 us
  waiting for transfers between devices  23.6 us (42%)
  starting transfers between devices  22.9 us (41%)
  Pallas kernels  8.88 us (16%)
  between operations  0.78 us (1%)
    ppermute x17, waiting for transfers between devices, swap(): lax.ppermute(x, axis, [(i, i ^ by) for i in range(n) if only is None or i...  23 us
    ppermute x17, starting transfers between devices, swap(): lax.ppermute(x, axis, [(i, i ^ by) for i in range(n) if only is None or i...  21.6 us
    pallas_call x12, Pallas kernels, call(): pl.pallas_call(body, out_shape=list(outs), in_specs=[given] * len(args),...  8.88 us
    ppermute x1, starting transfers between devices, per_device(): farthest = lax.ppermute(far, 'seq', [(1, 0), (2, 3)])  1.29 us
  transfers between devices with their start and end apart: 18, of which 11 were waited for; matrix products, arithmetic and copies ran while one was open for 0% of the time, Pallas kernels for 12%

profile of v7, /device:TPU:0, one launch (start us, length us, event | category | flops | bytes accessed | tf_op | source)
XLA Modules:
  0.0 56.2 jit_solution(7800284913074204548)
XLA Ops:
  0.6 1.2 %near.1 = (bf16[7,64,384]{2,1,0:T(8,128)(2,1)S(1)}, bf16[7,64,384]{2,1,0:T(8,128)(2,1)S(1)}) custom-call(bf16[4,64,384]{2,1,0:T(8,128)(2,1)} %cot.1, bf16[4,64,384]{2,1,0:T(8,128)(2,1)} %q.3, bf16[4,64,384]{2,1,0:T(8,128)(2,1)} %k.3, bf16[4,64,384]{2,1,0:T(8,128)(2,1)} %v.3), custom_call_target="tpu_custom_call" | custom-call | bytes 1474560 | tf_op jit(solution)/shard_map/near/pallas_call | solution.py:42
  1.8 0.7 %collective-permute-start.1 = (bf16[7,64,384]{2,1,0:T(8,128)(2,1)S(1)}, bf16[7,64,384]{2,1,0:T(8,128)(2,1)S(1)}, u32[]{:S(2)}, u32[]{:S(2)}) collective-permute-start(bf16[7,64,384]{2,1,0:T(8,128)(2,1)S(1)} %get-tuple-element.42.to_mirror), channel_id=1, source_target_pairs={{4,8},{8,4},{5,9},{9,5},{6,10},{10,6},{7,11},{11,7},{20,24},{24,20... | collective-permute-start | bytes 1032200 | tf_op jit(solution)/shard_map/ppermute | solution.py:292
  2.5 5.9 %collective-permute-start = (bf16[7,64,384]{2,1,0:T(8,128)(2,1)S(1)}, bf16[7,64,384]{2,1,0:T(8,128)(2,1)S(1)}, u32[]{:S(2)}, u32[]{:S(2)}) collective-permute-start(bf16[7,64,384]{2,1,0:T(8,128)(2,1)S(1)} %get-tuple-element.41.cot_ref), channel_id=1, source_target_pairs={{0,4},{4,0},{8,12},{12,8},{1,5},{5,1},{9,13},{13,9},{2,6},{6,2},{1... | collective-permute-start | bytes 1032200 | tf_op jit(solution)/shard_map/ppermute | solution.py:292
  8.4 1.8 %rest.1 = (bf16[3,64,384]{2,1,0:T(8,128)(2,1)S(1)}, bf16[3,64,384]{2,1,0:T(8,128)(2,1)S(1)}, bf16[3,768,384]{2,1,0:T(8,128)(2,1)S(1)}, f32[4,64,384]{2,1,0:T(8,1...) custom-call(bf16[4,64,384]{2,1,0:T(8,128)(2,1)} %hidden, bf16[4,64,384]{2,1,0:T(8,128)(2,1)} %q.3, ...), custom_call_target="tpu_custom_call" | custom-call | bytes 5210112 | tf_op jit(solution)/shard_map/rest/pallas_call | solution.py:42
  10.2 0.1 collective-permute-start.2
  10.3 1.3 %collective-permute-done.2.act_peer = bf16[2,64,384]{2,1,0:T(8,128)(2,1)S(1)} collective-permute-done((bf16[2,64,384]{2,1,0:T(8,128)(2,1)S(1)}, bf16[2,64,384]{2,1,0:T(8,128)(2,1)S(1)}, u32[]{:S(2)}, u32[]{:S(2)}) %collective-permute-start.2) | collective-permute-done | bytes 98336 | tf_op jit(solution)/shard_map/ppermute | solution.py:292
  11.6 0.4 conv_centre.1
  12.0 0.1 collective-permute-start.8
  12.1 0.0 collective-permute-done.1.mirror_ref.mirror_qkv.mirror
  12.1 4.8 %collective-permute-done.beside_ref.beside_qkv.beside = bf16[7,64,384]{2,1,0:T(8,128)(2,1)S(1)} collective-permute-done((bf16[7,64,384]{2,1,0:T(8,128)(2,1)S(1)}, bf16[7,64,384]{2,1,0:T(8,128)(2,1)S(1)}, u32[]{:S(2)}, u32[]{:S(2)}) %collective-permute-start) | collective-permute-done | bytes 344096 | tf_op jit(solution)/shard_map/ppermute | solution.py:292
  16.9 0.4 conv_other.1
  17.3 0.1 collective-permute-start.4
  17.4 0.5 collective-permute-start.3
  17.9 0.4 conv_mine.1.mine_ref
  18.3 0.4 collective-permute-done.4.got1_ref
  18.7 0.2 collective-permute-done.3.got0_ref
  18.8 0.2 hidden_grad.1
  19.0 2.6 %collective-permute-start.5 = (bf16[6,64,384]{2,1,0:T(8,128)(2,1)S(1)}, bf16[6,64,384]{2,1,0:T(8,128)(2,1)S(1)}, u32[]{:S(2)}, u32[]{:S(2)}) collective-permute-start(bf16[6,64,384]{2,1,0:T(8,128)(2,1)S(1)} %get-tuple-element.54.to_beside), channel_id=1, source_target_pairs={{0,4},{4,0},{8,12},{12,8},{1,5},{5,1},{9,13},{13,9},{2,6},{6,2},{1... | collective-permute-start | bytes 884744 | tf_op jit(solution)/shard_map/ppermute | solution.py:292
  21.6 0.7 %collective-permute-start.6 = (bf16[6,64,384]{2,1,0:T(8,128)(2,1)S(1)}, bf16[6,64,384]{2,1,0:T(8,128)(2,1)S(1)}, u32[]{:S(2)}, u32[]{:S(2)}) collective-permute-start(bf16[6,64,384]{2,1,0:T(8,128)(2,1)S(1)} %get-tuple-element.55.to_mirror), channel_id=1, source_target_pairs={{4,8},{8,4},{5,9},{9,5},{6,10},{10,6},{7,11},{11,7},{20,24},{24,20... | collective-permute-start | bytes 884744 | tf_op jit(solution)/shard_map/ppermute | solution.py:292
  22.2 2.3 %collective-permute-done.8.opposite.opposite_qkv = bf16[4,64,384]{2,1,0:T(8,128)(2,1)S(1)} collective-permute-done((bf16[4,64,384]{2,1,0:T(8,128)(2,1)S(1)}, bf16[4,64,384]{2,1,0:T(8,128)(2,1)S(1)}, u32[]{:S(2)}, u32[]{:S(2)}) %collective-permute-start.8) | collective-permute-done | bytes 196640 | tf_op jit(solution)/shard_map/ppermute | solution.py:292
  24.5 4.4 %collective-permute-start.10 = (bf16[5,64,384]{2,1,0:T(8,128)(2,1)S(1)}, bf16[5,64,384]{2,1,0:T(8,128)(2,1)S(1)}, u32[]{:S(2)}, u32[]{:S(2)}) collective-permute-start(bf16[5,64,384]{2,1,0:T(8,128)(2,1)S(1)} %get-tuple-element.62), channel_id=1, source_target_pairs={{0,12},{12,0},{1,13},{13,1},{2,14},{14,2},{3,15},{15,3},{16,28},{2... | collective-permute-start | bytes 737288 | tf_op jit(solution)/shard_map/ppermute | solution.py:292
  28.9 0.1 collective-permute-start.11
  29.0 1.8 %collective-permute-done.5.beside.beside2 = bf16[6,64,384]{2,1,0:T(8,128)(2,1)S(1)} collective-permute-done((bf16[6,64,384]{2,1,0:T(8,128)(2,1)S(1)}, bf16[6,64,384]{2,1,0:T(8,128)(2,1)S(1)}, u32[]{:S(2)}, u32[]{:S(2)}) %collective-permute-start.5) | collective-permute-done | bytes 294944 | tf_op jit(solution)/shard_map/ppermute | solution.py:292
  30.8 0.1 collective-permute-start.9
  30.9 0.0 collective-permute-done.6.held_ref.mirror.mirror2
  30.9 1.3 %collective-permute-start.7 = (bf16[4,64,384]{2,1,0:T(8,128)(2,1)S(1)}, bf16[4,64,384]{2,1,0:T(8,128)(2,1)S(1)}, u32[]{:S(2)}, u32[]{:S(2)}) collective-permute-start(bf16[4,64,384]{2,1,0:T(8,128)(2,1)S(1)} %pick.1), channel_id=1, source_target_pairs={{4,0},{8,12},{5,1},{9,13},{6,2},{10,14},{7,3},{11,15},{20,16},{24,... | collective-permute-start | bytes 589832 | tf_op jit(solution)/shard_map/ppermute | solution.py:354
  32.2 7.3 %collective-permute-done.11.opposite = bf16[1,64,384]{2,1,0:T(8,128)(2,1)S(1)} collective-permute-done((bf16[1,64,384]{2,1,0:T(8,128)(2,1)S(1)}, bf16[1,64,384]{2,1,0:T(8,128)(2,1)S(1)}, u32[]{:S(2)}, u32[]{:S(2)}) %collective-permute-start.11) | collective-permute-done | bytes 49184 | tf_op jit(solution)/shard_map/ppermute | solution.py:292
  39.5 0.0 collective-permute-done.10.end
  39.5 1.2 %attention.1 = (bf16[3,64,384]{2,1,0:T(8,128)(2,1)S(1)}, bf16[3,64,384]{2,1,0:T(8,128)(2,1)S(1)}, bf16[3,64,384]{2,1,0:T(8,128)(2,1)S(1)}, bf16[3,64,384]{2,1,0:T(8,128)(2,1)S(1)}, bf16[1,64,384]{2,1,0:T(8,128)(2,1)S(1)}) custom-call(bf16[3,64,384]{2,1,0:T(8,128)(2,1)S(1)} %get-tuple-element.59.own_qkv, bf16[2,64,384]{2,1,0:T(8,128)(2,1)S(1)} %get-tuple-element.56.own, ...), custom_call_target="tpu_custom_call" | custom-call | flops 2013265920 | bytes 2654208 | tf_op jit(solution)/shard_map/attention/pallas_call | solution.py:42
  40.7 0.1 collective-permute-start.12
  40.8 2.1 %collective-permute-start.15 = (bf16[3,64,384]{2,1,0:T(8,128)(2,1)S(1)}, bf16[3,64,384]{2,1,0:T(8,128)(2,1)S(1)}, u32[]{:S(2)}, u32[]{:S(2)}) collective-permute-start(bf16[3,64,384]{2,1,0:T(8,128)(2,1)S(1)} %get-tuple-element.70), channel_id=1, source_target_pairs={{0,8},{4,12},{8,0},{12,4},{1,9},{5,13},{9,1},{13,5},{2,10},{6,14},... | collective-permute-start | bytes 442376 | tf_op jit(solution)/shard_map/ppermute | solution.py:292
  42.9 0.6 %collective-permute-start.16 = (bf16[3,64,384]{2,1,0:T(8,128)(2,1)S(1)}, bf16[3,64,384]{2,1,0:T(8,128)(2,1)S(1)}, u32[]{:S(2)}, u32[]{:S(2)}) collective-permute-start(bf16[3,64,384]{2,1,0:T(8,128)(2,1)S(1)} %get-tuple-element.71), channel_id=1, source_target_pairs={{0,4},{4,0},{8,12},{12,8},{1,5},{5,1},{9,13},{13,9},{2,6},{6,2},{1... | collective-permute-start | bytes 442376 | tf_op jit(solution)/shard_map/ppermute | solution.py:292
  43.6 0.0 collective-permute-done.12.peer_last
  43.6 1.7 %collective-permute-start.17 = (bf16[3,64,384]{2,1,0:T(8,128)(2,1)S(1)}, bf16[3,64,384]{2,1,0:T(8,128)(2,1)S(1)}, u32[]{:S(2)}, u32[]{:S(2)}) collective-permute-start(bf16[3,64,384]{2,1,0:T(8,128)(2,1)S(1)} %get-tuple-element.72), channel_id=1, source_target_pairs={{0,12},{4,8},{8,4},{12,0},{1,13},{5,9},{9,5},{13,1},{2,14},{6,10},... | collective-permute-start | bytes 442376 | tf_op jit(solution)/shard_map/ppermute | solution.py:292
  45.3 0.0 collective-permute-done.9.act_peer
  45.3 0.6 %collective-permute-done.7.farthest = bf16[4,64,384]{2,1,0:T(8,128)(2,1)S(1)} collective-permute-done((bf16[4,64,384]{2,1,0:T(8,128)(2,1)S(1)}, bf16[4,64,384]{2,1,0:T(8,128)(2,1)S(1)}, u32[]{:S(2)}, u32[]{:S(2)}) %collective-permute-start.7) | collective-permute-done | bytes 196640 | tf_op jit(solution)/shard_map/ppermute | solution.py:354
  45.9 1.5 %weight_grad.1 = (f32[3,96,384]{2,1,0:T(8,128)S(1)}, bf16[3,48,384]{2,1,0:T(8,128)(2,1)S(1)}, bf16[3,48,384]{2,1,0:T(8,128)(2,1)S(1)}, bf16[4,64,384]{2,1,0:T(8,128)(2,1)}) custom-call(bf16[7,64,384]{2,1,0:T(8,128)(2,1)S(1)} %get-tuple-element.41.cot_ref, bf16[7,64,384]{2,1,0:T(8,128)(2,1)S(1)} %collective-permute-done.beside_ref.beside_qkv.beside, ...), custom_call_target="tpu_custom_call" | custom-call | tf_op jit(solution)/shard_map/weight_grad/pallas_call | solution.py:42
  47.4 1.5 %collective-permute-start.13 = (bf16[3,48,384]{2,1,0:T(8,128)(2,1)S(1)}, bf16[3,48,384]{2,1,0:T(8,128)(2,1)S(1)}, u32[]{:S(2)}, u32[]{:S(2)}) collective-permute-start(bf16[3,48,384]{2,1,0:T(8,128)(2,1)S(1)} %get-tuple-element.66), channel_id=1, source_target_pairs={{0,2},{2,0},{1,3},{3,1},{4,6},{6,4},{5,7},{7,5},{8,10},{10,8},{9,1... | collective-permute-start | bytes 331784 | tf_op jit(solution)/shard_map/ppermute | solution.py:292
  48.9 0.5 collective-permute-start.14
  49.4 3.2 %collective-permute-done.13.got0_ref = bf16[3,48,384]{2,1,0:T(8,128)(2,1)S(1)} collective-permute-done((bf16[3,48,384]{2,1,0:T(8,128)(2,1)S(1)}, bf16[3,48,384]{2,1,0:T(8,128)(2,1)S(1)}, u32[]{:S(2)}, u32[]{:S(2)}) %collective-permute-start.13) | collective-permute-done | bytes 110624 | tf_op jit(solution)/shard_map/ppermute | solution.py:292
  52.6 1.2 %collective-permute-done.14.got1_ref = bf16[3,48,384]{2,1,0:T(8,128)(2,1)S(1)} collective-permute-done((bf16[3,48,384]{2,1,0:T(8,128)(2,1)S(1)}, bf16[3,48,384]{2,1,0:T(8,128)(2,1)S(1)}, u32[]{:S(2)}, u32[]{:S(2)}) %collective-permute-start.14) | collective-permute-done | bytes 110624 | tf_op jit(solution)/shard_map/ppermute | solution.py:292
  53.8 0.8 %add_weight.1 = f32[3,96,384]{2,1,0:T(8,128)} custom-call(f32[3,96,384]{2,1,0:T(8,128)S(1)} %get-tuple-element.65.own_ref, bf16[3,48,384]{2,1,0:T(8,128)(2,1)S(1)} %collective-permute-done.13.got0_ref, bf16[3,48,384]{2,1,0:T(8,128)(2,1)S(1)} %collective-permute-done.14.got1_ref), custom_call_target="tpu_custom_call" | custom-call | tf_op jit(solution)/shard_map/add_weight/pallas_call | solution.py:42
  54.6 0.0 collective-permute-done.15.refs_1_
  54.6 0.0 collective-permute-done.16.refs_2_
  54.6 0.7 %collective-permute-done.17.refs_3_ = bf16[3,64,384]{2,1,0:T(8,128)(2,1)S(1)} collective-permute-done((bf16[3,64,384]{2,1,0:T(8,128)(2,1)S(1)}, bf16[3,64,384]{2,1,0:T(8,128)(2,1)S(1)}, u32[]{:S(2)}, u32[]{:S(2)}) %collective-permute-start.17) | collective-permute-done | bytes 147488 | tf_op jit(solution)/shard_map/ppermute | solution.py:292
  55.3 0.9 %place.1 = (bf16[4,64,384]{2,1,0:T(8,128)(2,1)}, bf16[4,64,384]{2,1,0:T(8,128)(2,1)}, bf16[4,64,384]{2,1,0:T(8,128)(2,1)}) custom-call(bf16[3,64,384]{2,1,0:T(8,128)(2,1)S(1)} %get-tuple-element.69.refs_0_, bf16[3,64,384]{2,1,0:T(8,128)(2,1)S(1)} %collective-permute-done.15.refs_1_, bf16[3,64,384]{2,1,0:T(8,128)(2,1)S(1)} %collective-permute-done.16.refs_2_, ...), custom_call_target="tpu_custom_call" | custom-call | bytes 1179648 | tf_op jit(solution)/shard_map/place/pallas_call | solution.py:42
  (2 shorter events, 0.0 us)
Async XLA Ops:
  1.8 10.3 %collective-permute-start.1 = (bf16[7,64,384]{2,1,0:T(8,128)(2,1)S(1)}, bf16[7,64,384]{2,1,0:T(8,128)(2,1)S(1)}, u32[]{:S(2)}, u32[]{:S(2)}) collective-permute-start(bf16[7,64,384]{2,1,0:T(8,128)(2,1)S(1)} %get-tuple-element.42.to_mirror), channel_id=1, source_target_pairs={{4,8},{8,4},{5,9},{9,5},{6,10},{10,6},{7,11},{11,7},{20,24},{24,20... | collective-permute-start | bytes 1032200 | tf_op jit(solution)/shard_map/ppermute | solution.py:292
  2.5 14.4 %collective-permute-start = (bf16[7,64,384]{2,1,0:T(8,128)(2,1)S(1)}, bf16[7,64,384]{2,1,0:T(8,128)(2,1)S(1)}, u32[]{:S(2)}, u32[]{:S(2)}) collective-permute-start(bf16[7,64,384]{2,1,0:T(8,128)(2,1)S(1)} %get-tuple-element.41.cot_ref), channel_id=1, source_target_pairs={{0,4},{4,0},{8,12},{12,8},{1,5},{5,1},{9,13},{13,9},{2,6},{6,2},{1... | collective-permute-start | bytes 1032200 | tf_op jit(solution)/shard_map/ppermute | solution.py:292
  10.2 1.4 %collective-permute-start.2 = (bf16[2,64,384]{2,1,0:T(8,128)(2,1)S(1)}, bf16[2,64,384]{2,1,0:T(8,128)(2,1)S(1)}, u32[]{:S(2)}, u32[]{:S(2)}) collective-permute-start(bf16[2,64,384]{2,1,0:T(8,128)(2,1)S(1)} %get-tuple-element.48), channel_id=1, source_target_pairs={{0,1},{1,0},{2,3},{3,2},{4,5},{5,4},{6,7},{7,6},{8,9},{9,8},{10,11... | collective-permute-start | bytes 294920 | tf_op jit(solution)/shard_map/ppermute | solution.py:292
  12.0 12.5 %collective-permute-start.8 = (bf16[4,64,384]{2,1,0:T(8,128)(2,1)S(1)}, bf16[4,64,384]{2,1,0:T(8,128)(2,1)S(1)}, u32[]{:S(2)}, u32[]{:S(2)}) collective-permute-start(bf16[4,64,384]{2,1,0:T(8,128)(2,1)S(1)} %get-tuple-element.57), channel_id=1, source_target_pairs={{0,8},{4,12},{8,0},{12,4},{1,9},{5,13},{9,1},{13,5},{2,10},{6,14},... | collective-permute-start | bytes 589832 | tf_op jit(solution)/shard_map/ppermute | solution.py:292
  17.3 1.4 %collective-permute-start.4 = (bf16[2,64,384]{2,1,0:T(8,128)(2,1)S(1)}, bf16[2,64,384]{2,1,0:T(8,128)(2,1)S(1)}, u32[]{:S(2)}, u32[]{:S(2)}) collective-permute-start(bf16[2,64,384]{2,1,0:T(8,128)(2,1)S(1)} %get-tuple-element.53), channel_id=1, source_target_pairs={{0,1},{1,0},{2,3},{3,2},{4,5},{5,4},{6,7},{7,6},{8,9},{9,8},{10,11... | collective-permute-start | bytes 294920 | tf_op jit(solution)/shard_map/ppermute | solution.py:292
  17.4 1.4 %collective-permute-start.3 = (bf16[2,64,384]{2,1,0:T(8,128)(2,1)S(1)}, bf16[2,64,384]{2,1,0:T(8,128)(2,1)S(1)}, u32[]{:S(2)}, u32[]{:S(2)}) collective-permute-start(bf16[2,64,384]{2,1,0:T(8,128)(2,1)S(1)} %get-tuple-element.50), channel_id=1, source_target_pairs={{0,1},{1,0},{2,3},{3,2},{4,5},{5,4},{6,7},{7,6},{8,9},{9,8},{10,11... | collective-permute-start | bytes 294920 | tf_op jit(solution)/shard_map/ppermute | solution.py:292
  19.0 11.8 %collective-permute-start.5 = (bf16[6,64,384]{2,1,0:T(8,128)(2,1)S(1)}, bf16[6,64,384]{2,1,0:T(8,128)(2,1)S(1)}, u32[]{:S(2)}, u32[]{:S(2)}) collective-permute-start(bf16[6,64,384]{2,1,0:T(8,128)(2,1)S(1)} %get-tuple-element.54.to_beside), channel_id=1, source_target_pairs={{0,4},{4,0},{8,12},{12,8},{1,5},{5,1},{9,13},{13,9},{2,6},{6,2},{1... | collective-permute-start | bytes 884744 | tf_op jit(solution)/shard_map/ppermute | solution.py:292
  21.6 9.4 %collective-permute-start.6 = (bf16[6,64,384]{2,1,0:T(8,128)(2,1)S(1)}, bf16[6,64,384]{2,1,0:T(8,128)(2,1)S(1)}, u32[]{:S(2)}, u32[]{:S(2)}) collective-permute-start(bf16[6,64,384]{2,1,0:T(8,128)(2,1)S(1)} %get-tuple-element.55.to_mirror), channel_id=1, source_target_pairs={{4,8},{8,4},{5,9},{9,5},{6,10},{10,6},{7,11},{11,7},{20,24},{24,20... | collective-permute-start | bytes 884744 | tf_op jit(solution)/shard_map/ppermute | solution.py:292
  24.5 15.0 %collective-permute-start.10 = (bf16[5,64,384]{2,1,0:T(8,128)(2,1)S(1)}, bf16[5,64,384]{2,1,0:T(8,128)(2,1)S(1)}, u32[]{:S(2)}, u32[]{:S(2)}) collective-permute-start(bf16[5,64,384]{2,1,0:T(8,128)(2,1)S(1)} %get-tuple-element.62), channel_id=1, source_target_pairs={{0,12},{12,0},{1,13},{13,1},{2,14},{14,2},{3,15},{15,3},{16,28},{2... | collective-permute-start | bytes 737288 | tf_op jit(solution)/shard_map/ppermute | solution.py:292
  28.9 10.7 %collective-permute-start.11 = (bf16[1,64,384]{2,1,0:T(8,128)(2,1)S(1)}, bf16[1,64,384]{2,1,0:T(8,128)(2,1)S(1)}, u32[]{:S(2)}, u32[]{:S(2)}) collective-permute-start(bf16[1,64,384]{2,1,0:T(8,128)(2,1)S(1)} %get-tuple-element.63.to_opposite), channel_id=1, source_target_pairs={{0,8},{4,12},{8,0},{12,4},{1,9},{5,13},{9,1},{13,5},{2,10},{6,14},... | collective-permute-start | bytes 147464 | tf_op jit(solution)/shard_map/ppermute | solution.py:292
  30.8 14.5 %collective-permute-start.9 = (bf16[3,64,384]{2,1,0:T(8,128)(2,1)S(1)}, bf16[3,64,384]{2,1,0:T(8,128)(2,1)S(1)}, u32[]{:S(2)}, u32[]{:S(2)}) collective-permute-start(bf16[3,64,384]{2,1,0:T(8,128)(2,1)S(1)} %gather.1.act_ref), channel_id=1, source_target_pairs={{0,1},{1,0},{2,3},{3,2},{4,5},{5,4},{6,7},{7,6},{8,9},{9,8},{10,11... | collective-permute-start | bytes 442376 | tf_op jit(solution)/shard_map/ppermute | solution.py:292
  30.9 14.9 %collective-permute-start.7 = (bf16[4,64,384]{2,1,0:T(8,128)(2,1)S(1)}, bf16[4,64,384]{2,1,0:T(8,128)(2,1)S(1)}, u32[]{:S(2)}, u32[]{:S(2)}) collective-permute-start(bf16[4,64,384]{2,1,0:T(8,128)(2,1)S(1)} %pick.1), channel_id=1, source_target_pairs={{4,0},{8,12},{5,1},{9,13},{6,2},{10,14},{7,3},{11,15},{20,16},{24,... | collective-permute-start | bytes 589832 | tf_op jit(solution)/shard_map/ppermute | solution.py:354
  40.7 2.8 %collective-permute-start.12 = (bf16[1,64,384]{2,1,0:T(8,128)(2,1)S(1)}, bf16[1,64,384]{2,1,0:T(8,128)(2,1)S(1)}, u32[]{:S(2)}, u32[]{:S(2)}) collective-permute-start(bf16[1,64,384]{2,1,0:T(8,128)(2,1)S(1)} %get-tuple-element.64.act_last), channel_id=1, source_target_pairs={{0,1},{1,0},{2,3},{3,2},{4,5},{5,4},{6,7},{7,6},{8,9},{9,8},{10,11... | collective-permute-start | bytes 147464 | tf_op jit(solution)/shard_map/ppermute | solution.py:292
  40.8 13.8 %collective-permute-start.15 = (bf16[3,64,384]{2,1,0:T(8,128)(2,1)S(1)}, bf16[3,64,384]{2,1,0:T(8,128)(2,1)S(1)}, u32[]{:S(2)}, u32[]{:S(2)}) collective-permute-start(bf16[3,64,384]{2,1,0:T(8,128)(2,1)S(1)} %get-tuple-element.70), channel_id=1, source_target_pairs={{0,8},{4,12},{8,0},{12,4},{1,9},{5,13},{9,1},{13,5},{2,10},{6,14},... | collective-permute-start | bytes 442376 | tf_op jit(solution)/shard_map/ppermute | solution.py:292
  42.9 11.7 %collective-permute-start.16 = (bf16[3,64,384]{2,1,0:T(8,128)(2,1)S(1)}, bf16[3,64,384]{2,1,0:T(8,128)(2,1)S(1)}, u32[]{:S(2)}, u32[]{:S(2)}) collective-permute-start(bf16[3,64,384]{2,1,0:T(8,128)(2,1)S(1)} %get-tuple-element.71), channel_id=1, source_target_pairs={{0,4},{4,0},{8,12},{12,8},{1,5},{5,1},{9,13},{13,9},{2,6},{6,2},{1... | collective-permute-start | bytes 442376 | tf_op jit(solution)/shard_map/ppermute | solution.py:292
  43.6 11.7 %collective-permute-start.17 = (bf16[3,64,384]{2,1,0:T(8,128)(2,1)S(1)}, bf16[3,64,384]{2,1,0:T(8,128)(2,1)S(1)}, u32[]{:S(2)}, u32[]{:S(2)}) collective-permute-start(bf16[3,64,384]{2,1,0:T(8,128)(2,1)S(1)} %get-tuple-element.72), channel_id=1, source_target_pairs={{0,12},{4,8},{8,4},{12,0},{1,13},{5,9},{9,5},{13,1},{2,14},{6,10},... | collective-permute-start | bytes 442376 | tf_op jit(solution)/shard_map/ppermute | solution.py:292
  47.4 5.2 %collective-permute-start.13 = (bf16[3,48,384]{2,1,0:T(8,128)(2,1)S(1)}, bf16[3,48,384]{2,1,0:T(8,128)(2,1)S(1)}, u32[]{:S(2)}, u32[]{:S(2)}) collective-permute-start(bf16[3,48,384]{2,1,0:T(8,128)(2,1)S(1)} %get-tuple-element.66), channel_id=1, source_target_pairs={{0,2},{2,0},{1,3},{3,1},{4,6},{6,4},{5,7},{7,5},{8,10},{10,8},{9,1... | collective-permute-start | bytes 331784 | tf_op jit(solution)/shard_map/ppermute | solution.py:292
  48.9 4.9 %collective-permute-start.14 = (bf16[3,48,384]{2,1,0:T(8,128)(2,1)S(1)}, bf16[3,48,384]{2,1,0:T(8,128)(2,1)S(1)}, u32[]{:S(2)}, u32[]{:S(2)}) collective-permute-start(bf16[3,48,384]{2,1,0:T(8,128)(2,1)S(1)} %get-tuple-element.67), channel_id=1, source_target_pairs={{0,2},{2,0},{1,3},{3,1},{4,6},{6,4},{5,7},{7,5},{8,10},{10,8},{9,1... | collective-permute-start | bytes 331784 | tf_op jit(solution)/shard_map/ppermute | solution.py:292

commit v8 on v7

--- a/solution.py
+++ b/solution.py
@@ -30,7 +30,7 @@
 
 def kernel_call(
     body, outs, flops=0, transcendentals=0, name=None, scratch=(), space=pltpu.VMEM,
-    out_space=pltpu.VMEM, bytes_too=True,
+    out_space=pltpu.VMEM, bytes_too=True, aliases=None,
 ):
     given, made = (pl.BlockSpec(memory_space=x) for x in (space, out_space))
 
@@ -45,6 +45,7 @@
             in_specs=[given] * len(args),
             out_specs=[made] * len(outs),
             scratch_shapes=list(scratch),
+            input_output_aliases=aliases or {},
             compiler_params=pltpu.CompilerParams(vmem_limit_bytes=VMEM_LIMIT),
             cost_estimate=pl.CostEstimate(
                 flops=flops, bytes_accessed=moved * bytes_too, transcendentals=transcendentals
@@ -279,10 +280,10 @@
     out_ref[:, half:] = own_ref[:, half:] + got1_ref[...].astype(F32)
 
 
-def place_kernel(*refs):
-    pieces, outs, sems = refs[:-4], refs[-4:-1], refs[-1]
+def place_kernel(taken, *refs):
+    pieces, outs, sems = refs[: len(taken)], refs[-4:-1], refs[-1]
     s = lax.axis_index("seq")
-    pairs = [(piece.at[j], outs[j].at[s ^ d]) for d, piece in zip((0, 2, 1, 3), pieces) for j in range(3)]
+    pairs = [(piece.at[j], outs[j].at[s ^ d]) for piece, d in zip(pieces, taken) for j in range(3)]
     for copy in fetch(pairs, sems):
         copy.wait()
 
@@ -385,15 +386,22 @@
     (weight_grad,) = kernel_call(add_kernel, [shape((3, part // 2, width), F32)], name="add_weight", bytes_too=False)(
         total, *got_sums
     )
-    pieces = [returned[0], *back.values()]
-    (pieces[0],) = after(weight_grad, pieces[0])
-    query_grad, key_grad, value_grad = kernel_call(
-        place_kernel,
-        [units(blocks)] * 3,
-        name="place",
-        scratch=[pltpu.SemaphoreType.DMA((3 * count,))],
-        out_space=pltpu.HBM,
-    )(*pieces)
+    back[0] = returned[0]
+    placed = ()
+    for taken in ((0, 2, 1), (3,)):
+        pieces = [back[d] for d in taken]
+        if placed:
+            (pieces[0],) = after(weight_grad, pieces[0])
+        placed = kernel_call(
+            functools.partial(place_kernel, taken),
+            [units(blocks)] * 3,
+            name="place",
+            scratch=[pltpu.SemaphoreType.DMA((3 * len(taken),))],
+            out_space=pltpu.HBM,
+            space=pl.ANY,
+            aliases={len(pieces) + j: j for j in range(len(placed))},
+        )(*pieces, *placed)
+    query_grad, key_grad, value_grad = placed
     return (query_grad, key_grad, value_grad, hidden_grad, weight_grad.transpose(1, 0, 2))
 
 

time: 56.4 us -> 56.2 us (level)
  waiting for transfers between devices: 23.6 us -> 22.8 us
  Pallas kernels: 8.88 us -> 9.49 us
    ppermute x17, waiting for transfers between devices: 23 us -> 22.2 us  [swap(): lax.ppermute(x, axis, [(i, i ^ by) for i in range(n) if only is None or i...]
    pallas_call x12 -> x13, Pallas kernels: 8.88 us -> 9.49 us  [call(): pl.pallas_call(body, out_shape=list(outs), in_specs=[given] * len(args),...]
  transfers between devices with their start and end apart: 18 -> 18, of which waited for: 11 -> 11; matrix products, arithmetic and copies ran while one was open for 0% -> 0% of each run, Pallas kernels for 12% -> 14%
where the time goes in v8:
time: 56.2 us; the launch traced here: 56 us
  starting transfers between devices  22.9 us (41%)
  waiting for transfers between devices  22.8 us (41%)
  Pallas kernels  9.49 us (17%)
  between operations  0.79 us (1%)
    ppermute x17, waiting for transfers between devices, swap(): lax.ppermute(x, axis, [(i, i ^ by) for i in range(n) if only is None or i...  22.2 us
    ppermute x17, starting transfers between devices, swap(): lax.ppermute(x, axis, [(i, i ^ by) for i in range(n) if only is None or i...  21.6 us
    pallas_call x13, Pallas kernels, call(): pl.pallas_call(body, out_shape=list(outs), in_specs=[given] * len(args),...  9.49 us
    ppermute x1, starting transfers between devices, per_device(): farthest = lax.ppermute(far, 'seq', [(1, 0), (2, 3)])  1.29 us
  transfers between devices with their start and end apart: 18, of which 11 were waited for; matrix products, arithmetic and copies ran while one was open for 0% of the time, Pallas kernels for 14%

profile of v8, /device:TPU:0, one launch (start us, length us, event | category | flops | bytes accessed | tf_op | source)
XLA Modules:
  0.0 56.0 jit_solution(14333398572906952146)
XLA Ops:
  0.6 1.2 %near.1 = (bf16[7,64,384]{2,1,0:T(8,128)(2,1)S(1)}, bf16[7,64,384]{2,1,0:T(8,128)(2,1)S(1)}) custom-call(bf16[4,64,384]{2,1,0:T(8,128)(2,1)} %cot.1, bf16[4,64,384]{2,1,0:T(8,128)(2,1)} %q.3, bf16[4,64,384]{2,1,0:T(8,128)(2,1)} %k.3, bf16[4,64,384]{2,1,0:T(8,128)(2,1)} %v.3), custom_call_target="tpu_custom_call" | custom-call | bytes 1474560 | tf_op jit(solution)/shard_map/near/pallas_call | solution.py:42
  1.8 0.7 %collective-permute-start.1 = (bf16[7,64,384]{2,1,0:T(8,128)(2,1)S(1)}, bf16[7,64,384]{2,1,0:T(8,128)(2,1)S(1)}, u32[]{:S(2)}, u32[]{:S(2)}) collective-permute-start(bf16[7,64,384]{2,1,0:T(8,128)(2,1)S(1)} %get-tuple-element.45.to_mirror), channel_id=1, source_target_pairs={{4,8},{8,4},{5,9},{9,5},{6,10},{10,6},{7,11},{11,7},{20,24},{24,20... | collective-permute-start | bytes 1032200 | tf_op jit(solution)/shard_map/ppermute | solution.py:293
  2.5 5.9 %collective-permute-start = (bf16[7,64,384]{2,1,0:T(8,128)(2,1)S(1)}, bf16[7,64,384]{2,1,0:T(8,128)(2,1)S(1)}, u32[]{:S(2)}, u32[]{:S(2)}) collective-permute-start(bf16[7,64,384]{2,1,0:T(8,128)(2,1)S(1)} %get-tuple-element.44.cot_ref), channel_id=1, source_target_pairs={{0,4},{4,0},{8,12},{12,8},{1,5},{5,1},{9,13},{13,9},{2,6},{6,2},{1... | collective-permute-start | bytes 1032200 | tf_op jit(solution)/shard_map/ppermute | solution.py:293
  8.4 1.8 %rest.1 = (bf16[3,64,384]{2,1,0:T(8,128)(2,1)S(1)}, bf16[3,64,384]{2,1,0:T(8,128)(2,1)S(1)}, bf16[3,768,384]{2,1,0:T(8,128)(2,1)S(1)}, f32[4,64,384]{2,1,0:T(8,1...) custom-call(bf16[4,64,384]{2,1,0:T(8,128)(2,1)} %hidden, bf16[4,64,384]{2,1,0:T(8,128)(2,1)} %q.3, ...), custom_call_target="tpu_custom_call" | custom-call | bytes 5210112 | tf_op jit(solution)/shard_map/rest/pallas_call | solution.py:42
  10.2 0.1 collective-permute-start.2
  10.3 1.3 %collective-permute-done.2.act_peer = bf16[2,64,384]{2,1,0:T(8,128)(2,1)S(1)} collective-permute-done((bf16[2,64,384]{2,1,0:T(8,128)(2,1)S(1)}, bf16[2,64,384]{2,1,0:T(8,128)(2,1)S(1)}, u32[]{:S(2)}, u32[]{:S(2)}) %collective-permute-start.2) | collective-permute-done | bytes 98336 | tf_op jit(solution)/shard_map/ppermute | solution.py:293
  11.6 0.4 conv_centre.1
  12.0 0.1 collective-permute-start.8
  12.1 0.0 collective-permute-done.1.mirror_ref.mirror_qkv.mirror
  12.1 4.8 %collective-permute-done.beside_ref.beside_qkv.beside = bf16[7,64,384]{2,1,0:T(8,128)(2,1)S(1)} collective-permute-done((bf16[7,64,384]{2,1,0:T(8,128)(2,1)S(1)}, bf16[7,64,384]{2,1,0:T(8,128)(2,1)S(1)}, u32[]{:S(2)}, u32[]{:S(2)}) %collective-permute-start) | collective-permute-done | bytes 344096 | tf_op jit(solution)/shard_map/ppermute | solution.py:293
  16.9 0.4 conv_other.1
  17.3 0.1 collective-permute-start.4
  17.4 0.5 collective-permute-start.3
  17.9 0.4 conv_mine.1.mine_ref
  18.3 0.4 collective-permute-done.4.got1_ref
  18.7 0.2 collective-permute-done.3.got0_ref
  18.8 0.2 hidden_grad.1
  19.0 2.6 %collective-permute-start.5 = (bf16[6,64,384]{2,1,0:T(8,128)(2,1)S(1)}, bf16[6,64,384]{2,1,0:T(8,128)(2,1)S(1)}, u32[]{:S(2)}, u32[]{:S(2)}) collective-permute-start(bf16[6,64,384]{2,1,0:T(8,128)(2,1)S(1)} %get-tuple-element.57.to_beside), channel_id=1, source_target_pairs={{0,4},{4,0},{8,12},{12,8},{1,5},{5,1},{9,13},{13,9},{2,6},{6,2},{1... | collective-permute-start | bytes 884744 | tf_op jit(solution)/shard_map/ppermute | solution.py:293
  21.6 0.7 %collective-permute-start.6 = (bf16[6,64,384]{2,1,0:T(8,128)(2,1)S(1)}, bf16[6,64,384]{2,1,0:T(8,128)(2,1)S(1)}, u32[]{:S(2)}, u32[]{:S(2)}) collective-permute-start(bf16[6,64,384]{2,1,0:T(8,128)(2,1)S(1)} %get-tuple-element.58.to_mirror), channel_id=1, source_target_pairs={{4,8},{8,4},{5,9},{9,5},{6,10},{10,6},{7,11},{11,7},{20,24},{24,20... | collective-permute-start | bytes 884744 | tf_op jit(solution)/shard_map/ppermute | solution.py:293
  22.2 2.3 %collective-permute-done.8.opposite.opposite_qkv = bf16[4,64,384]{2,1,0:T(8,128)(2,1)S(1)} collective-permute-done((bf16[4,64,384]{2,1,0:T(8,128)(2,1)S(1)}, bf16[4,64,384]{2,1,0:T(8,128)(2,1)S(1)}, u32[]{:S(2)}, u32[]{:S(2)}) %collective-permute-start.8) | collective-permute-done | bytes 196640 | tf_op jit(solution)/shard_map/ppermute | solution.py:293
  24.5 4.4 %collective-permute-start.10 = (bf16[5,64,384]{2,1,0:T(8,128)(2,1)S(1)}, bf16[5,64,384]{2,1,0:T(8,128)(2,1)S(1)}, u32[]{:S(2)}, u32[]{:S(2)}) collective-permute-start(bf16[5,64,384]{2,1,0:T(8,128)(2,1)S(1)} %get-tuple-element.65), channel_id=1, source_target_pairs={{0,12},{12,0},{1,13},{13,1},{2,14},{14,2},{3,15},{15,3},{16,28},{2... | collective-permute-start | bytes 737288 | tf_op jit(solution)/shard_map/ppermute | solution.py:293
  28.9 0.1 collective-permute-start.11
  29.0 1.8 %collective-permute-done.5.beside.beside2 = bf16[6,64,384]{2,1,0:T(8,128)(2,1)S(1)} collective-permute-done((bf16[6,64,384]{2,1,0:T(8,128)(2,1)S(1)}, bf16[6,64,384]{2,1,0:T(8,128)(2,1)S(1)}, u32[]{:S(2)}, u32[]{:S(2)}) %collective-permute-start.5) | collective-permute-done | bytes 294944 | tf_op jit(solution)/shard_map/ppermute | solution.py:293
  30.8 0.1 collective-permute-start.9
  30.9 0.0 collective-permute-done.6.held_ref.mirror.mirror2
  30.9 1.3 %collective-permute-start.7 = (bf16[4,64,384]{2,1,0:T(8,128)(2,1)S(1)}, bf16[4,64,384]{2,1,0:T(8,128)(2,1)S(1)}, u32[]{:S(2)}, u32[]{:S(2)}) collective-permute-start(bf16[4,64,384]{2,1,0:T(8,128)(2,1)S(1)} %pick.1), channel_id=1, source_target_pairs={{4,0},{8,12},{5,1},{9,13},{6,2},{10,14},{7,3},{11,15},{20,16},{24,... | collective-permute-start | bytes 589832 | tf_op jit(solution)/shard_map/ppermute | solution.py:355
  32.2 7.3 %collective-permute-done.11.opposite = bf16[1,64,384]{2,1,0:T(8,128)(2,1)S(1)} collective-permute-done((bf16[1,64,384]{2,1,0:T(8,128)(2,1)S(1)}, bf16[1,64,384]{2,1,0:T(8,128)(2,1)S(1)}, u32[]{:S(2)}, u32[]{:S(2)}) %collective-permute-start.11) | collective-permute-done | bytes 49184 | tf_op jit(solution)/shard_map/ppermute | solution.py:293
  39.5 0.0 collective-permute-done.10.end
  39.5 1.2 %attention.1 = (bf16[3,64,384]{2,1,0:T(8,128)(2,1)S(1)}, bf16[3,64,384]{2,1,0:T(8,128)(2,1)S(1)}, bf16[3,64,384]{2,1,0:T(8,128)(2,1)S(1)}, bf16[3,64,384]{2,1,0:T(8,128)(2,1)S(1)}, bf16[1,64,384]{2,1,0:T(8,128)(2,1)S(1)}) custom-call(bf16[3,64,384]{2,1,0:T(8,128)(2,1)S(1)} %get-tuple-element.62.own_qkv, bf16[2,64,384]{2,1,0:T(8,128)(2,1)S(1)} %get-tuple-element.59.own, ...), custom_call_target="tpu_custom_call" | custom-call | flops 2013265920 | bytes 2654208 | tf_op jit(solution)/shard_map/attention/pallas_call | solution.py:42
  40.7 0.1 collective-permute-start.12
  40.8 2.1 %collective-permute-start.16 = (bf16[3,64,384]{2,1,0:T(8,128)(2,1)S(1)}, bf16[3,64,384]{2,1,0:T(8,128)(2,1)S(1)}, u32[]{:S(2)}, u32[]{:S(2)}) collective-permute-start(bf16[3,64,384]{2,1,0:T(8,128)(2,1)S(1)} %get-tuple-element.74), channel_id=1, source_target_pairs={{0,8},{4,12},{8,0},{12,4},{1,9},{5,13},{9,1},{13,5},{2,10},{6,14},... | collective-permute-start | bytes 442376 | tf_op jit(solution)/shard_map/ppermute | solution.py:293
  42.9 0.6 %collective-permute-start.17 = (bf16[3,64,384]{2,1,0:T(8,128)(2,1)S(1)}, bf16[3,64,384]{2,1,0:T(8,128)(2,1)S(1)}, u32[]{:S(2)}, u32[]{:S(2)}) collective-permute-start(bf16[3,64,384]{2,1,0:T(8,128)(2,1)S(1)} %get-tuple-element.75), channel_id=1, source_target_pairs={{0,4},{4,0},{8,12},{12,8},{1,5},{5,1},{9,13},{13,9},{2,6},{6,2},{1... | collective-permute-start | bytes 442376 | tf_op jit(solution)/shard_map/ppermute | solution.py:293
  43.6 0.0 collective-permute-done.12.peer_last
  43.6 1.7 %collective-permute-start.15 = (bf16[3,64,384]{2,1,0:T(8,128)(2,1)S(1)}, bf16[3,64,384]{2,1,0:T(8,128)(2,1)S(1)}, u32[]{:S(2)}, u32[]{:S(2)}) collective-permute-start(bf16[3,64,384]{2,1,0:T(8,128)(2,1)S(1)} %get-tuple-element.71), channel_id=1, source_target_pairs={{0,12},{4,8},{8,4},{12,0},{1,13},{5,9},{9,5},{13,1},{2,14},{6,10},... | collective-permute-start | bytes 442376 | tf_op jit(solution)/shard_map/ppermute | solution.py:293
  45.3 0.0 collective-permute-done.9.act_peer
  45.3 0.6 %collective-permute-done.7.farthest = bf16[4,64,384]{2,1,0:T(8,128)(2,1)S(1)} collective-permute-done((bf16[4,64,384]{2,1,0:T(8,128)(2,1)S(1)}, bf16[4,64,384]{2,1,0:T(8,128)(2,1)S(1)}, u32[]{:S(2)}, u32[]{:S(2)}) %collective-permute-start.7) | collective-permute-done | bytes 196640 | tf_op jit(solution)/shard_map/ppermute | solution.py:355
  45.9 1.5 %weight_grad.1 = (f32[3,96,384]{2,1,0:T(8,128)S(1)}, bf16[3,48,384]{2,1,0:T(8,128)(2,1)S(1)}, bf16[3,48,384]{2,1,0:T(8,128)(2,1)S(1)}, bf16[4,64,384]{2,1,0:T(8,128)(2,1)}) custom-call(bf16[7,64,384]{2,1,0:T(8,128)(2,1)S(1)} %get-tuple-element.44.cot_ref, bf16[7,64,384]{2,1,0:T(8,128)(2,1)S(1)} %collective-permute-done.beside_ref.beside_qkv.beside, ...), custom_call_target="tpu_custom_call" | custom-call | tf_op jit(solution)/shard_map/weight_grad/pallas_call | solution.py:42
  47.4 1.5 %collective-permute-start.13 = (bf16[3,48,384]{2,1,0:T(8,128)(2,1)S(1)}, bf16[3,48,384]{2,1,0:T(8,128)(2,1)S(1)}, u32[]{:S(2)}, u32[]{:S(2)}) collective-permute-start(bf16[3,48,384]{2,1,0:T(8,128)(2,1)S(1)} %get-tuple-element.69), channel_id=1, source_target_pairs={{0,2},{2,0},{1,3},{3,1},{4,6},{6,4},{5,7},{7,5},{8,10},{10,8},{9,1... | collective-permute-start | bytes 331784 | tf_op jit(solution)/shard_map/ppermute | solution.py:293
  48.9 0.5 collective-permute-start.14
  49.4 2.3 %collective-permute-done.16.refs_1_ = bf16[3,64,384]{2,1,0:T(8,128)(2,1)S(1)} collective-permute-done((bf16[3,64,384]{2,1,0:T(8,128)(2,1)S(1)}, bf16[3,64,384]{2,1,0:T(8,128)(2,1)S(1)}, u32[]{:S(2)}, u32[]{:S(2)}) %collective-permute-start.16) | collective-permute-done | bytes 147488 | tf_op jit(solution)/shard_map/ppermute | solution.py:293
  51.7 0.0 collective-permute-done.17.refs_2_
  51.7 0.8 %place.2 = (bf16[4,64,384]{2,1,0:T(8,128)(2,1)}, bf16[4,64,384]{2,1,0:T(8,128)(2,1)}, bf16[4,64,384]{2,1,0:T(8,128)(2,1)}) custom-call(bf16[3,64,384]{2,1,0:T(8,128)(2,1)S(1)} %get-tuple-element.73.refs_0_, bf16[3,64,384]{2,1,0:T(8,128)(2,1)S(1)} %collective-permute-done.16.refs_1_, bf16[3,64,384]{2,1,0:T(8,128)(2,1)S(1)} %collective-permute-done.17.refs_2_), custom_call_target="tpu_custom_call" | custom-call | bytes 1032192 | tf_op jit(solution)/shard_map/place/pallas_call | solution.py:42
  52.6 0.0 collective-permute-done.13.got0_ref
  52.6 1.2 %collective-permute-done.14.got1_ref = bf16[3,48,384]{2,1,0:T(8,128)(2,1)S(1)} collective-permute-done((bf16[3,48,384]{2,1,0:T(8,128)(2,1)S(1)}, bf16[3,48,384]{2,1,0:T(8,128)(2,1)S(1)}, u32[]{:S(2)}, u32[]{:S(2)}) %collective-permute-start.14) | collective-permute-done | bytes 110624 | tf_op jit(solution)/shard_map/ppermute | solution.py:293
  53.8 0.8 %add_weight.1 = f32[3,96,384]{2,1,0:T(8,128)} custom-call(f32[3,96,384]{2,1,0:T(8,128)S(1)} %get-tuple-element.68.own_ref, bf16[3,48,384]{2,1,0:T(8,128)(2,1)S(1)} %collective-permute-done.13.got0_ref, bf16[3,48,384]{2,1,0:T(8,128)(2,1)S(1)} %collective-permute-done.14.got1_ref), custom_call_target="tpu_custom_call" | custom-call | tf_op jit(solution)/shard_map/add_weight/pallas_call | solution.py:42
  54.6 0.7 %collective-permute-done.15.refs_0_ = bf16[3,64,384]{2,1,0:T(8,128)(2,1)S(1)} collective-permute-done((bf16[3,64,384]{2,1,0:T(8,128)(2,1)S(1)}, bf16[3,64,384]{2,1,0:T(8,128)(2,1)S(1)}, u32[]{:S(2)}, u32[]{:S(2)}) %collective-permute-start.15) | collective-permute-done | bytes 147488 | tf_op jit(solution)/shard_map/ppermute | solution.py:293
  55.3 0.7 %place.3 = (bf16[4,64,384]{2,1,0:T(8,128)(2,1)}, bf16[4,64,384]{2,1,0:T(8,128)(2,1)}, bf16[4,64,384]{2,1,0:T(8,128)(2,1)}) custom-call(bf16[3,64,384]{2,1,0:T(8,128)(2,1)S(1)} %collective-permute-done.15.refs_0_, bf16[4,64,384]{2,1,0:T(8,128)(2,1)} %get-tuple-element.76.refs_1_, ...), custom_call_target="tpu_custom_call", output_to_operand_aliasing={{0}: (1, {}), {1}: (2, {}), {2}: (3, {})} | custom-call | bytes 1327104 | tf_op jit(solution)/shard_map/place/pallas_call | solution.py:42
  (2 shorter events, 0.0 us)
Async XLA Ops:
  1.8 10.3 %collective-permute-start.1 = (bf16[7,64,384]{2,1,0:T(8,128)(2,1)S(1)}, bf16[7,64,384]{2,1,0:T(8,128)(2,1)S(1)}, u32[]{:S(2)}, u32[]{:S(2)}) collective-permute-start(bf16[7,64,384]{2,1,0:T(8,128)(2,1)S(1)} %get-tuple-element.45.to_mirror), channel_id=1, source_target_pairs={{4,8},{8,4},{5,9},{9,5},{6,10},{10,6},{7,11},{11,7},{20,24},{24,20... | collective-permute-start | bytes 1032200 | tf_op jit(solution)/shard_map/ppermute | solution.py:293
  2.5 14.4 %collective-permute-start = (bf16[7,64,384]{2,1,0:T(8,128)(2,1)S(1)}, bf16[7,64,384]{2,1,0:T(8,128)(2,1)S(1)}, u32[]{:S(2)}, u32[]{:S(2)}) collective-permute-start(bf16[7,64,384]{2,1,0:T(8,128)(2,1)S(1)} %get-tuple-element.44.cot_ref), channel_id=1, source_target_pairs={{0,4},{4,0},{8,12},{12,8},{1,5},{5,1},{9,13},{13,9},{2,6},{6,2},{1... | collective-permute-start | bytes 1032200 | tf_op jit(solution)/shard_map/ppermute | solution.py:293
  10.2 1.4 %collective-permute-start.2 = (bf16[2,64,384]{2,1,0:T(8,128)(2,1)S(1)}, bf16[2,64,384]{2,1,0:T(8,128)(2,1)S(1)}, u32[]{:S(2)}, u32[]{:S(2)}) collective-permute-start(bf16[2,64,384]{2,1,0:T(8,128)(2,1)S(1)} %get-tuple-element.51), channel_id=1, source_target_pairs={{0,1},{1,0},{2,3},{3,2},{4,5},{5,4},{6,7},{7,6},{8,9},{9,8},{10,11... | collective-permute-start | bytes 294920 | tf_op jit(solution)/shard_map/ppermute | solution.py:293
  12.0 12.5 %collective-permute-start.8 = (bf16[4,64,384]{2,1,0:T(8,128)(2,1)S(1)}, bf16[4,64,384]{2,1,0:T(8,128)(2,1)S(1)}, u32[]{:S(2)}, u32[]{:S(2)}) collective-permute-start(bf16[4,64,384]{2,1,0:T(8,128)(2,1)S(1)} %get-tuple-element.60), channel_id=1, source_target_pairs={{0,8},{4,12},{8,0},{12,4},{1,9},{5,13},{9,1},{13,5},{2,10},{6,14},... | collective-permute-start | bytes 589832 | tf_op jit(solution)/shard_map/ppermute | solution.py:293
  17.3 1.4 %collective-permute-start.4 = (bf16[2,64,384]{2,1,0:T(8,128)(2,1)S(1)}, bf16[2,64,384]{2,1,0:T(8,128)(2,1)S(1)}, u32[]{:S(2)}, u32[]{:S(2)}) collective-permute-start(bf16[2,64,384]{2,1,0:T(8,128)(2,1)S(1)} %get-tuple-element.56), channel_id=1, source_target_pairs={{0,1},{1,0},{2,3},{3,2},{4,5},{5,4},{6,7},{7,6},{8,9},{9,8},{10,11... | collective-permute-start | bytes 294920 | tf_op jit(solution)/shard_map/ppermute | solution.py:293
  17.4 1.4 %collective-permute-start.3 = (bf16[2,64,384]{2,1,0:T(8,128)(2,1)S(1)}, bf16[2,64,384]{2,1,0:T(8,128)(2,1)S(1)}, u32[]{:S(2)}, u32[]{:S(2)}) collective-permute-start(bf16[2,64,384]{2,1,0:T(8,128)(2,1)S(1)} %get-tuple-element.53), channel_id=1, source_target_pairs={{0,1},{1,0},{2,3},{3,2},{4,5},{5,4},{6,7},{7,6},{8,9},{9,8},{10,11... | collective-permute-start | bytes 294920 | tf_op jit(solution)/shard_map/ppermute | solution.py:293
  19.0 11.8 %collective-permute-start.5 = (bf16[6,64,384]{2,1,0:T(8,128)(2,1)S(1)}, bf16[6,64,384]{2,1,0:T(8,128)(2,1)S(1)}, u32[]{:S(2)}, u32[]{:S(2)}) collective-permute-start(bf16[6,64,384]{2,1,0:T(8,128)(2,1)S(1)} %get-tuple-element.57.to_beside), channel_id=1, source_target_pairs={{0,4},{4,0},{8,12},{12,8},{1,5},{5,1},{9,13},{13,9},{2,6},{6,2},{1... | collective-permute-start | bytes 884744 | tf_op jit(solution)/shard_map/ppermute | solution.py:293
  21.6 9.4 %collective-permute-start.6 = (bf16[6,64,384]{2,1,0:T(8,128)(2,1)S(1)}, bf16[6,64,384]{2,1,0:T(8,128)(2,1)S(1)}, u32[]{:S(2)}, u32[]{:S(2)}) collective-permute-start(bf16[6,64,384]{2,1,0:T(8,128)(2,1)S(1)} %get-tuple-element.58.to_mirror), channel_id=1, source_target_pairs={{4,8},{8,4},{5,9},{9,5},{6,10},{10,6},{7,11},{11,7},{20,24},{24,20... | collective-permute-start | bytes 884744 | tf_op jit(solution)/shard_map/ppermute | solution.py:293
  24.5 15.0 %collective-permute-start.10 = (bf16[5,64,384]{2,1,0:T(8,128)(2,1)S(1)}, bf16[5,64,384]{2,1,0:T(8,128)(2,1)S(1)}, u32[]{:S(2)}, u32[]{:S(2)}) collective-permute-start(bf16[5,64,384]{2,1,0:T(8,128)(2,1)S(1)} %get-tuple-element.65), channel_id=1, source_target_pairs={{0,12},{12,0},{1,13},{13,1},{2,14},{14,2},{3,15},{15,3},{16,28},{2... | collective-permute-start | bytes 737288 | tf_op jit(solution)/shard_map/ppermute | solution.py:293
  28.9 10.7 %collective-permute-start.11 = (bf16[1,64,384]{2,1,0:T(8,128)(2,1)S(1)}, bf16[1,64,384]{2,1,0:T(8,128)(2,1)S(1)}, u32[]{:S(2)}, u32[]{:S(2)}) collective-permute-start(bf16[1,64,384]{2,1,0:T(8,128)(2,1)S(1)} %get-tuple-element.66.to_opposite), channel_id=1, source_target_pairs={{0,8},{4,12},{8,0},{12,4},{1,9},{5,13},{9,1},{13,5},{2,10},{6,14},... | collective-permute-start | bytes 147464 | tf_op jit(solution)/shard_map/ppermute | solution.py:293
  30.8 14.5 %collective-permute-start.9 = (bf16[3,64,384]{2,1,0:T(8,128)(2,1)S(1)}, bf16[3,64,384]{2,1,0:T(8,128)(2,1)S(1)}, u32[]{:S(2)}, u32[]{:S(2)}) collective-permute-start(bf16[3,64,384]{2,1,0:T(8,128)(2,1)S(1)} %gather.1.act_ref), channel_id=1, source_target_pairs={{0,1},{1,0},{2,3},{3,2},{4,5},{5,4},{6,7},{7,6},{8,9},{9,8},{10,11... | collective-permute-start | bytes 442376 | tf_op jit(solution)/shard_map/ppermute | solution.py:293
  30.9 14.9 %collective-permute-start.7 = (bf16[4,64,384]{2,1,0:T(8,128)(2,1)S(1)}, bf16[4,64,384]{2,1,0:T(8,128)(2,1)S(1)}, u32[]{:S(2)}, u32[]{:S(2)}) collective-permute-start(bf16[4,64,384]{2,1,0:T(8,128)(2,1)S(1)} %pick.1), channel_id=1, source_target_pairs={{4,0},{8,12},{5,1},{9,13},{6,2},{10,14},{7,3},{11,15},{20,16},{24,... | collective-permute-start | bytes 589832 | tf_op jit(solution)/shard_map/ppermute | solution.py:355
  40.7 2.8 %collective-permute-start.12 = (bf16[1,64,384]{2,1,0:T(8,128)(2,1)S(1)}, bf16[1,64,384]{2,1,0:T(8,128)(2,1)S(1)}, u32[]{:S(2)}, u32[]{:S(2)}) collective-permute-start(bf16[1,64,384]{2,1,0:T(8,128)(2,1)S(1)} %get-tuple-element.67.act_last), channel_id=1, source_target_pairs={{0,1},{1,0},{2,3},{3,2},{4,5},{5,4},{6,7},{7,6},{8,9},{9,8},{10,11... | collective-permute-start | bytes 147464 | tf_op jit(solution)/shard_map/ppermute | solution.py:293
  40.8 10.9 %collective-permute-start.16 = (bf16[3,64,384]{2,1,0:T(8,128)(2,1)S(1)}, bf16[3,64,384]{2,1,0:T(8,128)(2,1)S(1)}, u32[]{:S(2)}, u32[]{:S(2)}) collective-permute-start(bf16[3,64,384]{2,1,0:T(8,128)(2,1)S(1)} %get-tuple-element.74), channel_id=1, source_target_pairs={{0,8},{4,12},{8,0},{12,4},{1,9},{5,13},{9,1},{13,5},{2,10},{6,14},... | collective-permute-start | bytes 442376 | tf_op jit(solution)/shard_map/ppermute | solution.py:293
  42.9 8.8 %collective-permute-start.17 = (bf16[3,64,384]{2,1,0:T(8,128)(2,1)S(1)}, bf16[3,64,384]{2,1,0:T(8,128)(2,1)S(1)}, u32[]{:S(2)}, u32[]{:S(2)}) collective-permute-start(bf16[3,64,384]{2,1,0:T(8,128)(2,1)S(1)} %get-tuple-element.75), channel_id=1, source_target_pairs={{0,4},{4,0},{8,12},{12,8},{1,5},{5,1},{9,13},{13,9},{2,6},{6,2},{1... | collective-permute-start | bytes 442376 | tf_op jit(solution)/shard_map/ppermute | solution.py:293
  43.6 11.7 %collective-permute-start.15 = (bf16[3,64,384]{2,1,0:T(8,128)(2,1)S(1)}, bf16[3,64,384]{2,1,0:T(8,128)(2,1)S(1)}, u32[]{:S(2)}, u32[]{:S(2)}) collective-permute-start(bf16[3,64,384]{2,1,0:T(8,128)(2,1)S(1)} %get-tuple-element.71), channel_id=1, source_target_pairs={{0,12},{4,8},{8,4},{12,0},{1,13},{5,9},{9,5},{13,1},{2,14},{6,10},... | collective-permute-start | bytes 442376 | tf_op jit(solution)/shard_map/ppermute | solution.py:293
  47.4 5.2 %collective-permute-start.13 = (bf16[3,48,384]{2,1,0:T(8,128)(2,1)S(1)}, bf16[3,48,384]{2,1,0:T(8,128)(2,1)S(1)}, u32[]{:S(2)}, u32[]{:S(2)}) collective-permute-start(bf16[3,48,384]{2,1,0:T(8,128)(2,1)S(1)} %get-tuple-element.69), channel_id=1, source_target_pairs={{0,2},{2,0},{1,3},{3,1},{4,6},{6,4},{5,7},{7,5},{8,10},{10,8},{9,1... | collective-permute-start | bytes 331784 | tf_op jit(solution)/shard_map/ppermute | solution.py:293
  48.9 4.9 %collective-permute-start.14 = (bf16[3,48,384]{2,1,0:T(8,128)(2,1)S(1)}, bf16[3,48,384]{2,1,0:T(8,128)(2,1)S(1)}, u32[]{:S(2)}, u32[]{:S(2)}) collective-permute-start(bf16[3,48,384]{2,1,0:T(8,128)(2,1)S(1)} %get-tuple-element.70), channel_id=1, source_target_pairs={{0,2},{2,0},{1,3},{3,1},{4,6},{6,4},{5,7},{7,5},{8,10},{10,8},{9,1... | collective-permute-start | bytes 331784 | tf_op jit(solution)/shard_map/ppermute | solution.py:293

commit v9 on v8

--- a/solution.py
+++ b/solution.py
@@ -205,9 +205,10 @@
         windows.append((low, high))
         q, k, v, g = (x[:, low:high] for x in (query, key, value, grad))
         heads.append((q, k, k * inside, v * inside, g))
-    scores = [dot(k, q, nt) * scale for q, _, k, _, _ in heads]
+    scores = [dot(k, q, nt) for q, _, k, _, _ in heads]
     d_probs = [dot(v, g, nt) for _, _, _, v, g in heads]
-    raised = [jnp.exp(x - jnp.max(x, axis=0, keepdims=True)) for x in scores]
+    power = scale * math.log2(math.e)
+    raised = [jnp.exp2((x - jnp.max(x, axis=0, keepdims=True)) * power) for x in scores]
     probs = [x * (1.0 / jnp.sum(x, axis=0, keepdims=True)) for x in raised]
     v_grads = [dot(p.astype(BF), x[4], nn) for p, x in zip(probs, heads)]
     totals = [jnp.sum(p * d, axis=0, keepdims=True) for p, d in zip(probs, d_probs)]
@@ -256,22 +257,16 @@
     for t in range(3):
         low = max(0, 1 - t)
         high = min(count, count + 1 - t)
-        for is_own, side in ((False, 1 - b), (True, b)):
-            start = pl.multiple_of(side * half, half)
-            total = None
-            for j in range(low, high):
-                term = jnp.dot(
-                    act_buf[j + t - 1, pl.ds(start, half), :],
-                    cot_buf[j],
-                    preferred_element_type=F32,
-                )
-                total = term if total is None else total + term
-            total = factor * total
-            if is_own:
-                own_ref[t] = total
-            else:
-                sent0_ref[t] = total[: half // 2].astype(BF)
-                sent1_ref[t] = total[half // 2 :].astype(BF)
+        total = None
+        for j in range(low, high):
+            term = jnp.dot(act_buf[j + t - 1], cot_buf[j], preferred_element_type=F32)
+            total = term if total is None else total + term
+        total = factor * total
+        lower, upper = total[:half], total[half:]
+        own_ref[t] = jnp.where(b == 0, lower, upper)
+        sent = jnp.where(b == 0, upper, lower).astype(BF)
+        sent0_ref[t] = sent[: half // 2]
+        sent1_ref[t] = sent[half // 2 :]
 
 
 def add_kernel(own_ref, got0_ref, got1_ref, out_ref):

time: 56.2 us -> 56.1 us (level)
  transfers between devices with their start and end apart: 18 -> 18, of which waited for: 11 -> 11; matrix products, arithmetic and copies ran while one was open for 0% -> 0% of each run, Pallas kernels for 14% -> 13%
where the time goes in v9:
time: 56.1 us; the launch traced here: 55.9 us
  starting transfers between devices  22.9 us (41%)
  waiting for transfers between devices  22.9 us (41%)
  Pallas kernels  9.34 us (17%)
  between operations  0.8 us (1%)
    ppermute x17, waiting for transfers between devices, swap(): lax.ppermute(x, axis, [(i, i ^ by) for i in range(n) if only is None or i...  22.2 us
    ppermute x17, starting transfers between devices, swap(): lax.ppermute(x, axis, [(i, i ^ by) for i in range(n) if only is None or i...  21.6 us
    pallas_call x13, Pallas kernels, call(): pl.pallas_call(body, out_shape=list(outs), in_specs=[given] * len(args),...  9.34 us
    ppermute x1, starting transfers between devices, per_device(): farthest = lax.ppermute(far, 'seq', [(1, 0), (2, 3)])  1.29 us
  transfers between devices with their start and end apart: 18, of which 11 were waited for; matrix products, arithmetic and copies ran while one was open for 0% of the time, Pallas kernels for 13%

profile of v9, /device:TPU:0, one launch (start us, length us, event | category | flops | bytes accessed | tf_op | source)
XLA Modules:
  0.0 55.9 jit_solution(16985719004307438019)
XLA Ops:
  0.6 1.2 %near.1 = (bf16[7,64,384]{2,1,0:T(8,128)(2,1)S(1)}, bf16[7,64,384]{2,1,0:T(8,128)(2,1)S(1)}) custom-call(bf16[4,64,384]{2,1,0:T(8,128)(2,1)} %cot.1, bf16[4,64,384]{2,1,0:T(8,128)(2,1)} %q.3, bf16[4,64,384]{2,1,0:T(8,128)(2,1)} %k.3, bf16[4,64,384]{2,1,0:T(8,128)(2,1)} %v.3), custom_call_target="tpu_custom_call" | custom-call | bytes 1474560 | tf_op jit(solution)/shard_map/near/pallas_call | solution.py:42
  1.8 0.7 %collective-permute-start.1 = (bf16[7,64,384]{2,1,0:T(8,128)(2,1)S(1)}, bf16[7,64,384]{2,1,0:T(8,128)(2,1)S(1)}, u32[]{:S(2)}, u32[]{:S(2)}) collective-permute-start(bf16[7,64,384]{2,1,0:T(8,128)(2,1)S(1)} %get-tuple-element.45.to_mirror), channel_id=1, source_target_pairs={{4,8},{8,4},{5,9},{9,5},{6,10},{10,6},{7,11},{11,7},{20,24},{24,20... | collective-permute-start | bytes 1032200 | tf_op jit(solution)/shard_map/ppermute | solution.py:288
  2.5 5.9 %collective-permute-start = (bf16[7,64,384]{2,1,0:T(8,128)(2,1)S(1)}, bf16[7,64,384]{2,1,0:T(8,128)(2,1)S(1)}, u32[]{:S(2)}, u32[]{:S(2)}) collective-permute-start(bf16[7,64,384]{2,1,0:T(8,128)(2,1)S(1)} %get-tuple-element.44.cot_ref), channel_id=1, source_target_pairs={{0,4},{4,0},{8,12},{12,8},{1,5},{5,1},{9,13},{13,9},{2,6},{6,2},{1... | collective-permute-start | bytes 1032200 | tf_op jit(solution)/shard_map/ppermute | solution.py:288
  8.4 1.8 %rest.1 = (bf16[3,64,384]{2,1,0:T(8,128)(2,1)S(1)}, bf16[3,64,384]{2,1,0:T(8,128)(2,1)S(1)}, bf16[3,768,384]{2,1,0:T(8,128)(2,1)S(1)}, f32[4,64,384]{2,1,0:T(8,1...) custom-call(bf16[4,64,384]{2,1,0:T(8,128)(2,1)} %hidden, bf16[4,64,384]{2,1,0:T(8,128)(2,1)} %q.3, ...), custom_call_target="tpu_custom_call" | custom-call | bytes 5210112 | tf_op jit(solution)/shard_map/rest/pallas_call | solution.py:42
  10.2 0.1 collective-permute-start.2
  10.3 1.3 %collective-permute-done.2.act_peer = bf16[2,64,384]{2,1,0:T(8,128)(2,1)S(1)} collective-permute-done((bf16[2,64,384]{2,1,0:T(8,128)(2,1)S(1)}, bf16[2,64,384]{2,1,0:T(8,128)(2,1)S(1)}, u32[]{:S(2)}, u32[]{:S(2)}) %collective-permute-start.2) | collective-permute-done | bytes 98336 | tf_op jit(solution)/shard_map/ppermute | solution.py:288
  11.6 0.4 conv_centre.1
  12.0 0.1 collective-permute-start.8
  12.1 0.0 collective-permute-done.1.mirror_ref.mirror_qkv.mirror
  12.1 4.8 %collective-permute-done.beside_ref.beside_qkv.beside = bf16[7,64,384]{2,1,0:T(8,128)(2,1)S(1)} collective-permute-done((bf16[7,64,384]{2,1,0:T(8,128)(2,1)S(1)}, bf16[7,64,384]{2,1,0:T(8,128)(2,1)S(1)}, u32[]{:S(2)}, u32[]{:S(2)}) %collective-permute-start) | collective-permute-done | bytes 344096 | tf_op jit(solution)/shard_map/ppermute | solution.py:288
  16.9 0.4 conv_other.1
  17.3 0.1 collective-permute-start.4
  17.4 0.5 collective-permute-start.3
  17.9 0.4 conv_mine.1.mine_ref
  18.3 0.4 collective-permute-done.4.got1_ref
  18.7 0.2 collective-permute-done.3.got0_ref
  18.8 0.2 hidden_grad.1
  19.0 2.6 %collective-permute-start.5 = (bf16[6,64,384]{2,1,0:T(8,128)(2,1)S(1)}, bf16[6,64,384]{2,1,0:T(8,128)(2,1)S(1)}, u32[]{:S(2)}, u32[]{:S(2)}) collective-permute-start(bf16[6,64,384]{2,1,0:T(8,128)(2,1)S(1)} %get-tuple-element.57.to_beside), channel_id=1, source_target_pairs={{0,4},{4,0},{8,12},{12,8},{1,5},{5,1},{9,13},{13,9},{2,6},{6,2},{1... | collective-permute-start | bytes 884744 | tf_op jit(solution)/shard_map/ppermute | solution.py:288
  21.6 0.7 %collective-permute-start.6 = (bf16[6,64,384]{2,1,0:T(8,128)(2,1)S(1)}, bf16[6,64,384]{2,1,0:T(8,128)(2,1)S(1)}, u32[]{:S(2)}, u32[]{:S(2)}) collective-permute-start(bf16[6,64,384]{2,1,0:T(8,128)(2,1)S(1)} %get-tuple-element.58.to_mirror), channel_id=1, source_target_pairs={{4,8},{8,4},{5,9},{9,5},{6,10},{10,6},{7,11},{11,7},{20,24},{24,20... | collective-permute-start | bytes 884744 | tf_op jit(solution)/shard_map/ppermute | solution.py:288
  22.2 2.3 %collective-permute-done.8.opposite.opposite_qkv = bf16[4,64,384]{2,1,0:T(8,128)(2,1)S(1)} collective-permute-done((bf16[4,64,384]{2,1,0:T(8,128)(2,1)S(1)}, bf16[4,64,384]{2,1,0:T(8,128)(2,1)S(1)}, u32[]{:S(2)}, u32[]{:S(2)}) %collective-permute-start.8) | collective-permute-done | bytes 196640 | tf_op jit(solution)/shard_map/ppermute | solution.py:288
  24.5 4.4 %collective-permute-start.10 = (bf16[5,64,384]{2,1,0:T(8,128)(2,1)S(1)}, bf16[5,64,384]{2,1,0:T(8,128)(2,1)S(1)}, u32[]{:S(2)}, u32[]{:S(2)}) collective-permute-start(bf16[5,64,384]{2,1,0:T(8,128)(2,1)S(1)} %get-tuple-element.65), channel_id=1, source_target_pairs={{0,12},{12,0},{1,13},{13,1},{2,14},{14,2},{3,15},{15,3},{16,28},{2... | collective-permute-start | bytes 737288 | tf_op jit(solution)/shard_map/ppermute | solution.py:288
  28.9 0.1 collective-permute-start.11
  29.0 1.8 %collective-permute-done.5.beside.beside2 = bf16[6,64,384]{2,1,0:T(8,128)(2,1)S(1)} collective-permute-done((bf16[6,64,384]{2,1,0:T(8,128)(2,1)S(1)}, bf16[6,64,384]{2,1,0:T(8,128)(2,1)S(1)}, u32[]{:S(2)}, u32[]{:S(2)}) %collective-permute-start.5) | collective-permute-done | bytes 294944 | tf_op jit(solution)/shard_map/ppermute | solution.py:288
  30.8 0.1 collective-permute-start.9
  30.9 0.0 collective-permute-done.6.held_ref.mirror.mirror2
  30.9 1.3 %collective-permute-start.7 = (bf16[4,64,384]{2,1,0:T(8,128)(2,1)S(1)}, bf16[4,64,384]{2,1,0:T(8,128)(2,1)S(1)}, u32[]{:S(2)}, u32[]{:S(2)}) collective-permute-start(bf16[4,64,384]{2,1,0:T(8,128)(2,1)S(1)} %pick.1), channel_id=1, source_target_pairs={{4,0},{8,12},{5,1},{9,13},{6,2},{10,14},{7,3},{11,15},{20,16},{24,... | collective-permute-start | bytes 589832 | tf_op jit(solution)/shard_map/ppermute | solution.py:350
  32.2 7.3 %collective-permute-done.11.opposite = bf16[1,64,384]{2,1,0:T(8,128)(2,1)S(1)} collective-permute-done((bf16[1,64,384]{2,1,0:T(8,128)(2,1)S(1)}, bf16[1,64,384]{2,1,0:T(8,128)(2,1)S(1)}, u32[]{:S(2)}, u32[]{:S(2)}) %collective-permute-start.11) | collective-permute-done | bytes 49184 | tf_op jit(solution)/shard_map/ppermute | solution.py:288
  39.5 0.0 collective-permute-done.10.end
  39.5 1.2 %attention.1 = (bf16[3,64,384]{2,1,0:T(8,128)(2,1)S(1)}, bf16[3,64,384]{2,1,0:T(8,128)(2,1)S(1)}, bf16[3,64,384]{2,1,0:T(8,128)(2,1)S(1)}, bf16[3,64,384]{2,1,0:T(8,128)(2,1)S(1)}, bf16[1,64,384]{2,1,0:T(8,128)(2,1)S(1)}) custom-call(bf16[3,64,384]{2,1,0:T(8,128)(2,1)S(1)} %get-tuple-element.62.own_qkv, bf16[2,64,384]{2,1,0:T(8,128)(2,1)S(1)} %get-tuple-element.59.own, ...), custom_call_target="tpu_custom_call" | custom-call | flops 2013265920 | bytes 2654208 | tf_op jit(solution)/shard_map/attention/pallas_call | solution.py:42
  40.7 0.1 collective-permute-start.12
  40.8 2.1 %collective-permute-start.16 = (bf16[3,64,384]{2,1,0:T(8,128)(2,1)S(1)}, bf16[3,64,384]{2,1,0:T(8,128)(2,1)S(1)}, u32[]{:S(2)}, u32[]{:S(2)}) collective-permute-start(bf16[3,64,384]{2,1,0:T(8,128)(2,1)S(1)} %get-tuple-element.74), channel_id=1, source_target_pairs={{0,8},{4,12},{8,0},{12,4},{1,9},{5,13},{9,1},{13,5},{2,10},{6,14},... | collective-permute-start | bytes 442376 | tf_op jit(solution)/shard_map/ppermute | solution.py:288
  42.9 0.6 %collective-permute-start.17 = (bf16[3,64,384]{2,1,0:T(8,128)(2,1)S(1)}, bf16[3,64,384]{2,1,0:T(8,128)(2,1)S(1)}, u32[]{:S(2)}, u32[]{:S(2)}) collective-permute-start(bf16[3,64,384]{2,1,0:T(8,128)(2,1)S(1)} %get-tuple-element.75), channel_id=1, source_target_pairs={{0,4},{4,0},{8,12},{12,8},{1,5},{5,1},{9,13},{13,9},{2,6},{6,2},{1... | collective-permute-start | bytes 442376 | tf_op jit(solution)/shard_map/ppermute | solution.py:288
  43.5 0.0 collective-permute-done.12.peer_last
  43.5 1.7 %collective-permute-start.15 = (bf16[3,64,384]{2,1,0:T(8,128)(2,1)S(1)}, bf16[3,64,384]{2,1,0:T(8,128)(2,1)S(1)}, u32[]{:S(2)}, u32[]{:S(2)}) collective-permute-start(bf16[3,64,384]{2,1,0:T(8,128)(2,1)S(1)} %get-tuple-element.71), channel_id=1, source_target_pairs={{0,12},{4,8},{8,4},{12,0},{1,13},{5,9},{9,5},{13,1},{2,14},{6,10},... | collective-permute-start | bytes 442376 | tf_op jit(solution)/shard_map/ppermute | solution.py:288
  45.2 0.0 collective-permute-done.9.act_peer
  45.2 0.6 %collective-permute-done.7.farthest = bf16[4,64,384]{2,1,0:T(8,128)(2,1)S(1)} collective-permute-done((bf16[4,64,384]{2,1,0:T(8,128)(2,1)S(1)}, bf16[4,64,384]{2,1,0:T(8,128)(2,1)S(1)}, u32[]{:S(2)}, u32[]{:S(2)}) %collective-permute-start.7) | collective-permute-done | bytes 196640 | tf_op jit(solution)/shard_map/ppermute | solution.py:350
  45.9 1.4 %weight_grad.1 = (f32[3,96,384]{2,1,0:T(8,128)S(1)}, bf16[3,48,384]{2,1,0:T(8,128)(2,1)S(1)}, bf16[3,48,384]{2,1,0:T(8,128)(2,1)S(1)}, bf16[4,64,384]{2,1,0:T(8,128)(2,1)}) custom-call(bf16[7,64,384]{2,1,0:T(8,128)(2,1)S(1)} %get-tuple-element.44.cot_ref, bf16[7,64,384]{2,1,0:T(8,128)(2,1)S(1)} %collective-permute-done.beside_ref.beside_qkv.beside, ...), custom_call_target="tpu_custom_call" | custom-call | tf_op jit(solution)/shard_map/weight_grad/pallas_call | solution.py:42
  47.3 1.5 %collective-permute-start.13 = (bf16[3,48,384]{2,1,0:T(8,128)(2,1)S(1)}, bf16[3,48,384]{2,1,0:T(8,128)(2,1)S(1)}, u32[]{:S(2)}, u32[]{:S(2)}) collective-permute-start(bf16[3,48,384]{2,1,0:T(8,128)(2,1)S(1)} %get-tuple-element.69), channel_id=1, source_target_pairs={{0,2},{2,0},{1,3},{3,1},{4,6},{6,4},{5,7},{7,5},{8,10},{10,8},{9,1... | collective-permute-start | bytes 331784 | tf_op jit(solution)/shard_map/ppermute | solution.py:288
  48.8 0.5 collective-permute-start.14
  49.3 2.3 %collective-permute-done.16.refs_1_ = bf16[3,64,384]{2,1,0:T(8,128)(2,1)S(1)} collective-permute-done((bf16[3,64,384]{2,1,0:T(8,128)(2,1)S(1)}, bf16[3,64,384]{2,1,0:T(8,128)(2,1)S(1)}, u32[]{:S(2)}, u32[]{:S(2)}) %collective-permute-start.16) | collective-permute-done | bytes 147488 | tf_op jit(solution)/shard_map/ppermute | solution.py:288
  51.7 0.0 collective-permute-done.17.refs_2_
  51.7 0.8 %place.2 = (bf16[4,64,384]{2,1,0:T(8,128)(2,1)}, bf16[4,64,384]{2,1,0:T(8,128)(2,1)}, bf16[4,64,384]{2,1,0:T(8,128)(2,1)}) custom-call(bf16[3,64,384]{2,1,0:T(8,128)(2,1)S(1)} %get-tuple-element.73.refs_0_, bf16[3,64,384]{2,1,0:T(8,128)(2,1)S(1)} %collective-permute-done.16.refs_1_, bf16[3,64,384]{2,1,0:T(8,128)(2,1)S(1)} %collective-permute-done.17.refs_2_), custom_call_target="tpu_custom_call" | custom-call | bytes 1032192 | tf_op jit(solution)/shard_map/place/pallas_call | solution.py:42
  52.5 0.0 collective-permute-done.13.got0_ref
  52.5 1.1 %collective-permute-done.14.got1_ref = bf16[3,48,384]{2,1,0:T(8,128)(2,1)S(1)} collective-permute-done((bf16[3,48,384]{2,1,0:T(8,128)(2,1)S(1)}, bf16[3,48,384]{2,1,0:T(8,128)(2,1)S(1)}, u32[]{:S(2)}, u32[]{:S(2)}) %collective-permute-start.14) | collective-permute-done | bytes 110624 | tf_op jit(solution)/shard_map/ppermute | solution.py:288
  53.6 0.8 %add_weight.1 = f32[3,96,384]{2,1,0:T(8,128)} custom-call(f32[3,96,384]{2,1,0:T(8,128)S(1)} %get-tuple-element.68.own_ref, bf16[3,48,384]{2,1,0:T(8,128)(2,1)S(1)} %collective-permute-done.13.got0_ref, bf16[3,48,384]{2,1,0:T(8,128)(2,1)S(1)} %collective-permute-done.14.got1_ref), custom_call_target="tpu_custom_call" | custom-call | tf_op jit(solution)/shard_map/add_weight/pallas_call | solution.py:42
  54.5 0.8 %collective-permute-done.15.refs_0_ = bf16[3,64,384]{2,1,0:T(8,128)(2,1)S(1)} collective-permute-done((bf16[3,64,384]{2,1,0:T(8,128)(2,1)S(1)}, bf16[3,64,384]{2,1,0:T(8,128)(2,1)S(1)}, u32[]{:S(2)}, u32[]{:S(2)}) %collective-permute-start.15) | collective-permute-done | bytes 147488 | tf_op jit(solution)/shard_map/ppermute | solution.py:288
  55.2 0.7 %place.3 = (bf16[4,64,384]{2,1,0:T(8,128)(2,1)}, bf16[4,64,384]{2,1,0:T(8,128)(2,1)}, bf16[4,64,384]{2,1,0:T(8,128)(2,1)}) custom-call(bf16[3,64,384]{2,1,0:T(8,128)(2,1)S(1)} %collective-permute-done.15.refs_0_, bf16[4,64,384]{2,1,0:T(8,128)(2,1)} %get-tuple-element.76.refs_1_, ...), custom_call_target="tpu_custom_call", output_to_operand_aliasing={{0}: (1, {}), {1}: (2, {}), {2}: (3, {})} | custom-call | bytes 1327104 | tf_op jit(solution)/shard_map/place/pallas_call | solution.py:42
  (2 shorter events, 0.0 us)
Async XLA Ops:
  1.8 10.3 %collective-permute-start.1 = (bf16[7,64,384]{2,1,0:T(8,128)(2,1)S(1)}, bf16[7,64,384]{2,1,0:T(8,128)(2,1)S(1)}, u32[]{:S(2)}, u32[]{:S(2)}) collective-permute-start(bf16[7,64,384]{2,1,0:T(8,128)(2,1)S(1)} %get-tuple-element.45.to_mirror), channel_id=1, source_target_pairs={{4,8},{8,4},{5,9},{9,5},{6,10},{10,6},{7,11},{11,7},{20,24},{24,20... | collective-permute-start | bytes 1032200 | tf_op jit(solution)/shard_map/ppermute | solution.py:288
  2.5 14.4 %collective-permute-start = (bf16[7,64,384]{2,1,0:T(8,128)(2,1)S(1)}, bf16[7,64,384]{2,1,0:T(8,128)(2,1)S(1)}, u32[]{:S(2)}, u32[]{:S(2)}) collective-permute-start(bf16[7,64,384]{2,1,0:T(8,128)(2,1)S(1)} %get-tuple-element.44.cot_ref), channel_id=1, source_target_pairs={{0,4},{4,0},{8,12},{12,8},{1,5},{5,1},{9,13},{13,9},{2,6},{6,2},{1... | collective-permute-start | bytes 1032200 | tf_op jit(solution)/shard_map/ppermute | solution.py:288
  10.2 1.4 %collective-permute-start.2 = (bf16[2,64,384]{2,1,0:T(8,128)(2,1)S(1)}, bf16[2,64,384]{2,1,0:T(8,128)(2,1)S(1)}, u32[]{:S(2)}, u32[]{:S(2)}) collective-permute-start(bf16[2,64,384]{2,1,0:T(8,128)(2,1)S(1)} %get-tuple-element.51), channel_id=1, source_target_pairs={{0,1},{1,0},{2,3},{3,2},{4,5},{5,4},{6,7},{7,6},{8,9},{9,8},{10,11... | collective-permute-start | bytes 294920 | tf_op jit(solution)/shard_map/ppermute | solution.py:288
  12.0 12.5 %collective-permute-start.8 = (bf16[4,64,384]{2,1,0:T(8,128)(2,1)S(1)}, bf16[4,64,384]{2,1,0:T(8,128)(2,1)S(1)}, u32[]{:S(2)}, u32[]{:S(2)}) collective-permute-start(bf16[4,64,384]{2,1,0:T(8,128)(2,1)S(1)} %get-tuple-element.60), channel_id=1, source_target_pairs={{0,8},{4,12},{8,0},{12,4},{1,9},{5,13},{9,1},{13,5},{2,10},{6,14},... | collective-permute-start | bytes 589832 | tf_op jit(solution)/shard_map/ppermute | solution.py:288
  17.3 1.4 %collective-permute-start.4 = (bf16[2,64,384]{2,1,0:T(8,128)(2,1)S(1)}, bf16[2,64,384]{2,1,0:T(8,128)(2,1)S(1)}, u32[]{:S(2)}, u32[]{:S(2)}) collective-permute-start(bf16[2,64,384]{2,1,0:T(8,128)(2,1)S(1)} %get-tuple-element.56), channel_id=1, source_target_pairs={{0,1},{1,0},{2,3},{3,2},{4,5},{5,4},{6,7},{7,6},{8,9},{9,8},{10,11... | collective-permute-start | bytes 294920 | tf_op jit(solution)/shard_map/ppermute | solution.py:288
  17.4 1.4 %collective-permute-start.3 = (bf16[2,64,384]{2,1,0:T(8,128)(2,1)S(1)}, bf16[2,64,384]{2,1,0:T(8,128)(2,1)S(1)}, u32[]{:S(2)}, u32[]{:S(2)}) collective-permute-start(bf16[2,64,384]{2,1,0:T(8,128)(2,1)S(1)} %get-tuple-element.53), channel_id=1, source_target_pairs={{0,1},{1,0},{2,3},{3,2},{4,5},{5,4},{6,7},{7,6},{8,9},{9,8},{10,11... | collective-permute-start | bytes 294920 | tf_op jit(solution)/shard_map/ppermute | solution.py:288
  19.0 11.8 %collective-permute-start.5 = (bf16[6,64,384]{2,1,0:T(8,128)(2,1)S(1)}, bf16[6,64,384]{2,1,0:T(8,128)(2,1)S(1)}, u32[]{:S(2)}, u32[]{:S(2)}) collective-permute-start(bf16[6,64,384]{2,1,0:T(8,128)(2,1)S(1)} %get-tuple-element.57.to_beside), channel_id=1, source_target_pairs={{0,4},{4,0},{8,12},{12,8},{1,5},{5,1},{9,13},{13,9},{2,6},{6,2},{1... | collective-permute-start | bytes 884744 | tf_op jit(solution)/shard_map/ppermute | solution.py:288
  21.6 9.4 %collective-permute-start.6 = (bf16[6,64,384]{2,1,0:T(8,128)(2,1)S(1)}, bf16[6,64,384]{2,1,0:T(8,128)(2,1)S(1)}, u32[]{:S(2)}, u32[]{:S(2)}) collective-permute-start(bf16[6,64,384]{2,1,0:T(8,128)(2,1)S(1)} %get-tuple-element.58.to_mirror), channel_id=1, source_target_pairs={{4,8},{8,4},{5,9},{9,5},{6,10},{10,6},{7,11},{11,7},{20,24},{24,20... | collective-permute-start | bytes 884744 | tf_op jit(solution)/shard_map/ppermute | solution.py:288
  24.5 15.0 %collective-permute-start.10 = (bf16[5,64,384]{2,1,0:T(8,128)(2,1)S(1)}, bf16[5,64,384]{2,1,0:T(8,128)(2,1)S(1)}, u32[]{:S(2)}, u32[]{:S(2)}) collective-permute-start(bf16[5,64,384]{2,1,0:T(8,128)(2,1)S(1)} %get-tuple-element.65), channel_id=1, source_target_pairs={{0,12},{12,0},{1,13},{13,1},{2,14},{14,2},{3,15},{15,3},{16,28},{2... | collective-permute-start | bytes 737288 | tf_op jit(solution)/shard_map/ppermute | solution.py:288
  28.9 10.7 %collective-permute-start.11 = (bf16[1,64,384]{2,1,0:T(8,128)(2,1)S(1)}, bf16[1,64,384]{2,1,0:T(8,128)(2,1)S(1)}, u32[]{:S(2)}, u32[]{:S(2)}) collective-permute-start(bf16[1,64,384]{2,1,0:T(8,128)(2,1)S(1)} %get-tuple-element.66.to_opposite), channel_id=1, source_target_pairs={{0,8},{4,12},{8,0},{12,4},{1,9},{5,13},{9,1},{13,5},{2,10},{6,14},... | collective-permute-start | bytes 147464 | tf_op jit(solution)/shard_map/ppermute | solution.py:288
  30.8 14.4 %collective-permute-start.9 = (bf16[3,64,384]{2,1,0:T(8,128)(2,1)S(1)}, bf16[3,64,384]{2,1,0:T(8,128)(2,1)S(1)}, u32[]{:S(2)}, u32[]{:S(2)}) collective-permute-start(bf16[3,64,384]{2,1,0:T(8,128)(2,1)S(1)} %gather.1.act_ref), channel_id=1, source_target_pairs={{0,1},{1,0},{2,3},{3,2},{4,5},{5,4},{6,7},{7,6},{8,9},{9,8},{10,11... | collective-permute-start | bytes 442376 | tf_op jit(solution)/shard_map/ppermute | solution.py:288
  30.9 14.9 %collective-permute-start.7 = (bf16[4,64,384]{2,1,0:T(8,128)(2,1)S(1)}, bf16[4,64,384]{2,1,0:T(8,128)(2,1)S(1)}, u32[]{:S(2)}, u32[]{:S(2)}) collective-permute-start(bf16[4,64,384]{2,1,0:T(8,128)(2,1)S(1)} %pick.1), channel_id=1, source_target_pairs={{4,0},{8,12},{5,1},{9,13},{6,2},{10,14},{7,3},{11,15},{20,16},{24,... | collective-permute-start | bytes 589832 | tf_op jit(solution)/shard_map/ppermute | solution.py:350
  40.7 2.8 %collective-permute-start.12 = (bf16[1,64,384]{2,1,0:T(8,128)(2,1)S(1)}, bf16[1,64,384]{2,1,0:T(8,128)(2,1)S(1)}, u32[]{:S(2)}, u32[]{:S(2)}) collective-permute-start(bf16[1,64,384]{2,1,0:T(8,128)(2,1)S(1)} %get-tuple-element.67.act_last), channel_id=1, source_target_pairs={{0,1},{1,0},{2,3},{3,2},{4,5},{5,4},{6,7},{7,6},{8,9},{9,8},{10,11... | collective-permute-start | bytes 147464 | tf_op jit(solution)/shard_map/ppermute | solution.py:288
  40.8 10.9 %collective-permute-start.16 = (bf16[3,64,384]{2,1,0:T(8,128)(2,1)S(1)}, bf16[3,64,384]{2,1,0:T(8,128)(2,1)S(1)}, u32[]{:S(2)}, u32[]{:S(2)}) collective-permute-start(bf16[3,64,384]{2,1,0:T(8,128)(2,1)S(1)} %get-tuple-element.74), channel_id=1, source_target_pairs={{0,8},{4,12},{8,0},{12,4},{1,9},{5,13},{9,1},{13,5},{2,10},{6,14},... | collective-permute-start | bytes 442376 | tf_op jit(solution)/shard_map/ppermute | solution.py:288
  42.9 8.8 %collective-permute-start.17 = (bf16[3,64,384]{2,1,0:T(8,128)(2,1)S(1)}, bf16[3,64,384]{2,1,0:T(8,128)(2,1)S(1)}, u32[]{:S(2)}, u32[]{:S(2)}) collective-permute-start(bf16[3,64,384]{2,1,0:T(8,128)(2,1)S(1)} %get-tuple-element.75), channel_id=1, source_target_pairs={{0,4},{4,0},{8,12},{12,8},{1,5},{5,1},{9,13},{13,9},{2,6},{6,2},{1... | collective-permute-start | bytes 442376 | tf_op jit(solution)/shard_map/ppermute | solution.py:288
  43.5 11.7 %collective-permute-start.15 = (bf16[3,64,384]{2,1,0:T(8,128)(2,1)S(1)}, bf16[3,64,384]{2,1,0:T(8,128)(2,1)S(1)}, u32[]{:S(2)}, u32[]{:S(2)}) collective-permute-start(bf16[3,64,384]{2,1,0:T(8,128)(2,1)S(1)} %get-tuple-element.71), channel_id=1, source_target_pairs={{0,12},{4,8},{8,4},{12,0},{1,13},{5,9},{9,5},{13,1},{2,14},{6,10},... | collective-permute-start | bytes 442376 | tf_op jit(solution)/shard_map/ppermute | solution.py:288
  47.3 5.2 %collective-permute-start.13 = (bf16[3,48,384]{2,1,0:T(8,128)(2,1)S(1)}, bf16[3,48,384]{2,1,0:T(8,128)(2,1)S(1)}, u32[]{:S(2)}, u32[]{:S(2)}) collective-permute-start(bf16[3,48,384]{2,1,0:T(8,128)(2,1)S(1)} %get-tuple-element.69), channel_id=1, source_target_pairs={{0,2},{2,0},{1,3},{3,1},{4,6},{6,4},{5,7},{7,5},{8,10},{10,8},{9,1... | collective-permute-start | bytes 331784 | tf_op jit(solution)/shard_map/ppermute | solution.py:288
  48.8 4.9 %collective-permute-start.14 = (bf16[3,48,384]{2,1,0:T(8,128)(2,1)S(1)}, bf16[3,48,384]{2,1,0:T(8,128)(2,1)S(1)}, u32[]{:S(2)}, u32[]{:S(2)}) collective-permute-start(bf16[3,48,384]{2,1,0:T(8,128)(2,1)S(1)} %get-tuple-element.70), channel_id=1, source_target_pairs={{0,2},{2,0},{1,3},{3,1},{4,6},{6,4},{5,7},{7,5},{8,10},{10,8},{9,1... | collective-permute-start | bytes 331784 | tf_op jit(solution)/shard_map/ppermute | solution.py:288
